TPU v7x, 256 devices: a whole 4x4x8 slice. The times are simulated.
256 devices in a mesh: band: 32 (over y, z_hi, core), slab: 8 (over z_lo, x).
Axes of the slice: x: 4, y: 4, z: 8 (z_hi: 4, z_lo: 2; z = z_hi * 2 + z_lo), core: 2. Of those that a mesh axis runs over, the one named last changes fastest.
Arguments:
- orbitals: float32 [32, 160, 160, 160], P('band', 'slab'), may hold values from -6 to 6
Outputs:
- exchange_field: float32 [32, 160, 160, 160], P('band', 'slab')
All inputs are finite; a program needn't handle non-finite values.
Results may differ from a plain program's by a relative error of at most 0.0003.
Values sent between devices are 32-bit elements; how exact they have to be, the bound alone decides.
No kernel may reach another device: no remote copies, remote signals or barrier semaphores. Data moves between devices by JAX's collectives and lax.ppermute only.
A program may use at most 128 MiB of HBM per device.

v0:
```python
import math

import jax
import jax.numpy as jnp
from jax import lax
from jax.sharding import PartitionSpec as P

STEPS = 2


highest = lax.Precision.HIGHEST


def passed_along(value, axis, steps):
    count = lax.axis_size(axis)
    pairs = [(source, (source + steps) % count) for source in range(count)]
    return lax.ppermute(value, axis, pairs)


def cas_table(length):
    indices = jnp.arange(length, dtype=jnp.int32)
    product = indices[:, None] * indices[None, :] % length
    phases = product.astype(jnp.float32) * (2.0 * math.pi / length)
    return jnp.cos(phases) + jnp.sin(phases)


def wave_square(indices, length):
    return 4.0 * jnp.sin(indices.astype(jnp.float32) * (math.pi / length)) ** 2


def potential(density, hartley, kernel, length):
    field = jnp.einsum("xk,zyx->zyk", hartley, density, precision=highest)
    field = jnp.einsum("yk,zyx->zkx", hartley, field, precision=highest)
    field = lax.all_to_all(field, "slab", split_axis=1, concat_axis=0, tiled=True)
    field = jnp.einsum("zk,zyx->kyx", hartley, field, precision=highest)
    field = field * kernel
    field = jnp.einsum("zk,zyx->kyx", hartley, field, precision=highest)
    field = jnp.einsum("xk,zyx->zyk", hartley, field, precision=highest)
    field = lax.all_to_all(field, "slab", split_axis=0, concat_axis=1, tiled=True)
    field = jnp.einsum("yk,zyx->zkx", hartley, field, precision=highest)
    return field / float(length**3)


def shards(orbitals):
    resident = orbitals[0]
    length = resident.shape[2]
    groups = lax.axis_size("slab")
    width_y = length // groups
    hartley = cas_table(length)
    waves = wave_square(jnp.arange(length, dtype=jnp.int32), length)
    first_y = lax.axis_index("slab") * width_y
    waves_y = wave_square(first_y + jnp.arange(width_y, dtype=jnp.int32), length)
    square = waves[:, None, None] + waves_y[None, :, None] + waves[None, None, :]
    kernel = jnp.where(square > 0, 1.0 / jnp.where(square > 0, square, 1.0), 0.0)
    accumulated = jnp.zeros(resident.shape, jnp.float32)
    visiting = passed_along(resident, "band", 1)
    travel_sum = jnp.zeros(resident.shape, jnp.float32)
    for offset in range(STEPS):
        if offset > 0:
            visiting, travel_sum = passed_along((visiting, travel_sum), "band", 1)
        field = potential(resident * visiting, hartley, kernel, length)
        accumulated = accumulated + field * visiting
        travel_sum = travel_sum + field * resident
    returned = passed_along(travel_sum, "band", -STEPS)
    accumulated = accumulated + returned
    return accumulated[None]


def solution(mesh):
    in_specs = (P("band", "slab", None, None),)
    out_specs = P("band", "slab", None, None)
    return jax.shard_map(shards, mesh=mesh, in_specs=in_specs, out_specs=out_specs, check_vma=False)
```

profile of v0, /device:TPU:32, one launch (start us, length us, event | category | flops | bytes accessed | tf_op | source)
XLA Modules:
  0.0 583.1 jit_solution(6739756017049597198)
XLA Ops:
  3.9 78.7 %collective-permute-done = f32[20,160,160]{1,2,0:T(8,128)S(1)} collective-permute-done((f32[20,160,160]{1,2,0:T(8,128)S(1)}, f32[20,160,160]{1,2,0:T(8,128)S(1)}, u32[]{:S(2)}, u32[]{:S(2)}) %collective-permute-start) | collective-permute-done | bytes 2048032 | tf_op jit(solution)/shard_map/ppermute | solution.py:17
  86.7 5.1 convolution_bitcast_fusion.1
  91.8 5.3 copy.19
  97.1 5.8 all-to-all-start
  103.0 42.6 %collective-permute-done.1 = f32[20,160,160]{1,2,0:T(8,128)S(1)} collective-permute-done((f32[20,160,160]{1,2,0:T(8,128)}, f32[20,160,160]{1,2,0:T(8,128)S(1)}, u32[]{:S(2)}, u32[]{:S(2)}) %collective-permute-start.1) | collective-permute-done | bytes 2048032 | tf_op jit(solution)/shard_map/ppermute | solution.py:17
  149.7 5.1 convolution_bitcast_fusion
  154.8 5.3 copy.30
  160.0 22.0 %all-to-all-done = f32[20,160,160]{2,0,1:T(8,128)} async-done(((f32[20,160,160]{2,0,1:T(8,128)}), f32[20,160,160]{2,0,1:T(8,128)}, u32[]{:S(2)}, u32[]{:S(2)}) %all-to-all-start) | async-done | bytes 2048032 | tf_op jit(solution)/shard_map/all_to_all | solution.py:34
  182.0 52.6 %all-to-all-start.2 = ((f32[20,160,160]{2,0,1:T(8,128)}), f32[20,160,160]{2,0,1:T(8,128)}, u32[]{:S(2)}, u32[]{:S(2)}) async-start(f32[20,160,160]{2,0,1:T(8,128)} %copy.30), calls=%async_computation.2 | async-start | bytes 7864320 | tf_op jit(solution)/shard_map/all_to_all | solution.py:34
  234.7 4.5 copy.21
  239.3 5.0 all_to_all.55
  244.2 5.7 fusion.33
  249.9 4.3 fusion.10
  257.7 4.0 copy.24
  261.7 13.8 %all-to-all-done.2 = f32[20,160,160]{2,0,1:T(8,128)} async-done(((f32[20,160,160]{2,0,1:T(8,128)}), f32[20,160,160]{2,0,1:T(8,128)}, u32[]{:S(2)}, u32[]{:S(2)}) %all-to-all-start.2) | async-done | bytes 2048032 | tf_op jit(solution)/shard_map/all_to_all | solution.py:34
  275.6 5.0 all-to-all-start.1
  280.6 4.4 copy.32
  285.1 4.6 all_to_all.63
  289.7 5.7 fusion.18
  295.3 4.3 fusion.6
  303.1 4.0 copy.35
  307.1 18.8 %all-to-all-done.1 = f32[160,20,160]{2,1,0:T(8,128)} async-done(((f32[160,20,160]{2,1,0:T(8,128)}), f32[160,20,160]{2,1,0:T(8,128)}, u32[]{:S(2)}, u32[]{:S(2)}) %all-to-all-start.1) | async-done | bytes 2048032 | tf_op jit(solution)/shard_map/all_to_all | solution.py:39
  326.0 5.0 all-to-all-start.3
  330.9 4.5 copy.26
  335.4 4.6 all_to_all.59
  340.0 12.1 %bitcast_multiply_fusion.2 = (f32[20,160,160]{1,2,0:T(8,128)}, f32[20,160,160]{2,1,0:T(8,128)}) fusion(f32[1,20,160,160]{2,3,1,0:T(8,128)S(1)} %copy.16, f32[20,160,160]{2,1,0:T(8,128)} %all_to_all.59), kind=kOutput, calls=%fused_computation.10 | convolution fusion | flops 984320000 | bytes 8192000 | tf_op jit(solution)/shard_map/yk,zyx->zkx/dot_general | solution.py:40
  352.1 58.0 %all-to-all-done.3 = f32[160,20,160]{2,1,0:T(8,128)} async-done(((f32[160,20,160]{2,1,0:T(8,128)}), f32[160,20,160]{2,1,0:T(8,128)}, u32[]{:S(2)}, u32[]{:S(2)}) %all-to-all-start.3) | async-done | bytes 2048032 | tf_op jit(solution)/shard_map/all_to_all | solution.py:39
  410.1 4.4 copy.37
  414.6 4.8 all_to_all.67
  419.4 11.0 %fusion.5 = (f32[20,160,160]{1,2,0:T(8,128)S(1)}, f32[20,160,160]{2,1,0:T(8,128)S(1)}) fusion(f32[20,160,160]{1,2,0:T(8,128)} %collective-permute-done.2, f32[1,20,160,160]{2,3,1,0:T(8,128)S(1)} %copy.16, f32[20,160,160]{2,1,0:T(8,128)} %all_to_all.67), kind=kOutput, calls=%fused_computation.9 | convolution fusion | flops 984832000 | bytes 10240000 | tf_op jit(solution)/shard_map/yk,zyx->zkx/dot_general | solution.py:40
  430.4 5.0 collective-permute-start.3
  435.4 138.8 %collective-permute-done.3 = f32[20,160,160]{1,2,0:T(8,128)S(1)} collective-permute-done((f32[20,160,160]{1,2,0:T(8,128)S(1)}, f32[20,160,160]{1,2,0:T(8,128)S(1)}, u32[]{:S(2)}, u32[]{:S(2)}) %collective-permute-start.3) | collective-permute-done | bytes 2048032 | tf_op jit(solution)/shard_map/ppermute | solution.py:17
  (26 shorter events, 27.8 us)
Async XLA Ops:
  3.8 78.8 %collective-permute-start = (f32[20,160,160]{1,2,0:T(8,128)S(1)}, f32[20,160,160]{1,2,0:T(8,128)S(1)}, u32[]{:S(2)}, u32[]{:S(2)}) collective-permute-start(f32[20,160,160]{1,2,0:T(8,128)S(1)} %bitcast.94), channel_id=1, source_target_pairs={{0,8},{8,16},{16,24},{24,32},{32,40},{40,48},{48,56},{56,64},{64,7... | collective-permute-start | bytes 6144008 | tf_op jit(solution)/shard_map/ppermute | solution.py:17
  82.7 4.0 copy-start
  97.1 84.9 %all-to-all-start = ((f32[20,160,160]{2,0,1:T(8,128)}), f32[20,160,160]{2,0,1:T(8,128)}, u32[]{:S(2)}, u32[]{:S(2)}) async-start(f32[20,160,160]{2,0,1:T(8,128)} %copy.19), calls=%async_computation | async-start | bytes 7864320 | tf_op jit(solution)/shard_map/all_to_all | solution.py:34
  102.8 42.8 %collective-permute-start.1 = (f32[20,160,160]{1,2,0:T(8,128)}, f32[20,160,160]{1,2,0:T(8,128)S(1)}, u32[]{:S(2)}, u32[]{:S(2)}) collective-permute-start(f32[20,160,160]{1,2,0:T(8,128)} %copy-done), channel_id=1, source_target_pairs={{0,8},{8,16},{16,24},{24,32},{32,40},{40,48},{48,56},{56,64},{64,7... | collective-permute-start | bytes 6144008 | tf_op jit(solution)/shard_map/ppermute | solution.py:17
  145.7 4.0 copy-start.2
  182.0 93.6 %all-to-all-start.2 = ((f32[20,160,160]{2,0,1:T(8,128)}), f32[20,160,160]{2,0,1:T(8,128)}, u32[]{:S(2)}, u32[]{:S(2)}) async-start(f32[20,160,160]{2,0,1:T(8,128)} %copy.30), calls=%async_computation.2 | async-start | bytes 7864320 | tf_op jit(solution)/shard_map/all_to_all | solution.py:34
  275.6 50.4 %all-to-all-start.1 = ((f32[160,20,160]{2,1,0:T(8,128)}), f32[160,20,160]{2,1,0:T(8,128)}, u32[]{:S(2)}, u32[]{:S(2)}) async-start(f32[160,20,160]{2,1,0:T(8,128)} %copy.24), calls=%async_computation.1 | async-start | bytes 7864320 | tf_op jit(solution)/shard_map/all_to_all | solution.py:39
  326.0 84.2 %all-to-all-start.3 = ((f32[160,20,160]{2,1,0:T(8,128)}), f32[160,20,160]{2,1,0:T(8,128)}, u32[]{:S(2)}, u32[]{:S(2)}) async-start(f32[160,20,160]{2,1,0:T(8,128)} %copy.35), calls=%async_computation.3 | async-start | bytes 7864320 | tf_op jit(solution)/shard_map/all_to_all | solution.py:39
  352.1 67.3 %collective-permute-start.2 = (f32[20,160,160]{1,2,0:T(8,128)}, f32[20,160,160]{1,2,0:T(8,128)}, u32[]{:S(2)}, u32[]{:S(2)}) collective-permute-start(f32[20,160,160]{1,2,0:T(8,128)} %get-tuple-element.5), channel_id=1, source_target_pairs={{0,8},{8,16},{16,24},{24,32},{32,40},{40,48},{48,56},{56,64},{64,7... | collective-permute-start | bytes 6144008 | tf_op jit(solution)/shard_map/ppermute | solution.py:17
  419.4 156.5 %copy-start.1 = (f32[20,160,160]{1,2,0:T(8,128)S(1)}, f32[20,160,160]{1,2,0:T(8,128)}, u32[]{:S(2)}) copy-start(f32[20,160,160]{1,2,0:T(8,128)} %copy-done) | copy-start | bytes 6144004
  419.4 156.5 %copy-start.3 = (f32[20,160,160]{1,2,0:T(8,128)S(1)}, f32[20,160,160]{1,2,0:T(8,128)}, u32[]{:S(2)}) copy-start(f32[20,160,160]{1,2,0:T(8,128)} %copy-done.2) | copy-start | bytes 6144004
  419.4 156.5 %copy-start.4 = (f32[20,160,160]{2,1,0:T(8,128)S(1)}, f32[20,160,160]{2,1,0:T(8,128)}, u32[]{:S(2)}) copy-start(f32[20,160,160]{2,1,0:T(8,128)} %get-tuple-element.6) | copy-start | bytes 6144004
  430.4 143.8 %collective-permute-start.3 = (f32[20,160,160]{1,2,0:T(8,128)S(1)}, f32[20,160,160]{1,2,0:T(8,128)S(1)}, u32[]{:S(2)}, u32[]{:S(2)}) collective-permute-start(f32[20,160,160]{1,2,0:T(8,128)S(1)} %get-tuple-element.7), channel_id=1, source_target_pairs={{0,240},{8,248},{16,0},{24,8},{32,16},{40,24},{48,32},{56,40},{64,... | collective-permute-start | bytes 6144008 | tf_op jit(solution)/shard_map/ppermute | solution.py:17
  574.2 1.7 copy-start.5
where the time goes:
time: 594 us; the launch traced here: 583 us
  waiting for transfers between devices  373 us (63%)
  starting transfers between devices  73.6 us (12%)
  matrix products  68.2 us (11%)
  local copies, waits for them, and re-layouts  64.3 us (11%)
    ppermute x4, waiting for transfers between devices, passed_along(): return lax.ppermute(value, axis, pairs)  260 us
    all_to_all x2, waiting for transfers between devices, potential(): lax.all_to_all(field, 'slab', split_axis=0, concat_axis=1, tiled=True)  76.9 us
    all_to_all x2, starting transfers between devices, potential(): lax.all_to_all(field, 'slab', split_axis=1, concat_axis=0, tiled=True)  58.3 us
    all_to_all x2, waiting for transfers between devices, potential(): lax.all_to_all(field, 'slab', split_axis=1, concat_axis=0, tiled=True)  35.8 us
    dot_general x4, matrix products, potential(): field = jnp.einsum('yk,zyx->zkx', hartley, field, precision=highest)  33.3 us
    dot_general x4, matrix products, potential(): field = jnp.einsum('zk,zyx->kyx', hartley, field, precision=highest)  19.9 us
    all_to_all x4, local copies, waits for them, and re-layouts, potential(): lax.all_to_all(field, 'slab', split_axis=1, concat_axis=0, tiled=True)  18.5 us
    all_to_all x4, local copies, waits for them, and re-layouts, potential(): lax.all_to_all(field, 'slab', split_axis=0, concat_axis=1, tiled=True)  18.4 us
  transfers between devices with their start and end apart: 8, of which 7 were waited for; matrix products, arithmetic and copies ran while one was open for 14% of the time, Pallas kernels for 0%

commit v1 on v0

v1 whole, which is shorter than its diff:
```python
import functools

import jax
import jax.numpy as jnp
import ml_dtypes
import numpy as np
from jax import lax
from jax.experimental import pallas as pl
from jax.experimental.pallas import tpu as pltpu
from jax.sharding import PartitionSpec as P

NG = 160
SLABS = 8
DEPTH = NG // SLABS
PLANES = 4
CHUNKS = DEPTH // PLANES
WIDE = 256
MODE_TILES = NG * NG // 1024
SEND_TILES = 13
F32 = jnp.float32
BF16 = jnp.bfloat16


def split_table(table):
    high = table.astype(np.float32).astype(ml_dtypes.bfloat16)
    low = (table - high.astype(np.float64)).astype(np.float32).astype(ml_dtypes.bfloat16)
    return high, low


def plane_tiles(plane):
    main = plane[:, :128].reshape(-1, 8, 128)
    rest = np.concatenate([plane[40 * g : 40 * g + 40, 128:] for g in range(4)], axis=1)
    return np.concatenate([main, rest.reshape(-1, 8, 128)])


def widened(plane):
    return np.pad(plane, [(0, 0)] * (plane.ndim - 1) + [(0, WIDE - NG)])


@functools.cache
def tables():
    index = np.arange(NG)
    angle = 2.0 * np.pi * (index[:, None] * index[None, :] % NG) / NG
    hartley = np.cos(angle) + np.sin(angle)
    forward = np.zeros((PLANES, WIDE, WIDE))
    inverse = np.zeros((PLANES, WIDE, WIDE))
    for j in range(PLANES):
        forward[j, :128, :NG] = hartley[:128]
        forward[j, 128 + 32 * j : 160 + 32 * j, :NG] = hartley[128:]
        inverse[j, :NG, :128] = hartley[:, :128]
        inverse[j, :NG, 128 + 32 * j : 160 + 32 * j] = hartley[:, 128:]
    wave = 4.0 * np.sin(np.pi * index / NG) ** 2
    lam = wave[:, None] + wave[None, :]
    ratio = 1.0 / (1.0 + lam / 2 + np.sqrt(lam + lam * lam / 4))
    ratio[0, 0] = 0.0
    scale = ratio / (1.0 - ratio**2) / NG**2
    powers = np.stack([ratio ** (PLANES * k) for k in range(CHUNKS)])
    edge = np.stack([scale * ratio ** (i + 1) for i in range(DEPTH)])
    jump = np.tile(plane_tiles(ratio**DEPTH), (4, 1, 1))
    wrap = np.tile(plane_tiles(1.0 / (1.0 - ratio**NG)), (4, 1, 1))
    spare = [(0, SLABS * SEND_TILES - 4 * MODE_TILES), (0, 0), (0, 0)]
    zero = np.zeros((SLABS, 24, 128))
    for apart in range(SLABS):
        for i in range(DEPTH):
            d = (DEPTH * apart + i - np.arange(DEPTH)) % NG
            zero[apart, i, :DEPTH] = ((NG**2 - 1) / (12 * NG) - d * (NG - d) / (2 * NG)) / NG**2
    as32 = lambda a: a.astype(np.float32)
    return dict(
        forward=np.stack(split_table(forward), axis=1),
        inverse=np.stack(split_table(inverse), axis=1),
        hartley=np.concatenate(split_table(hartley)),
        ratio=as32(widened(ratio)),
        scale=as32(widened(scale)),
        powers=as32(widened(powers)),
        edge=as32(widened(edge)),
        jump=as32(np.pad(jump, spare)),
        wrap=as32(np.pad(wrap, spare)),
        zero=as32(zero),
    )


def split(value):
    high = value.astype(BF16)
    return high, (value - high.astype(F32)).astype(BF16)


def dot(a, b):
    return jnp.dot(a, b, preferred_element_type=F32)


def times_table(value, high_table, low_table):
    high, low = split(value)
    return dot(high, high_table) + dot(low, high_table) + dot(high, low_table)


def table_times(hartley, value):
    high, low = split(value)
    both = dot(hartley, high)
    return both[:NG] + both[NG:] + dot(hartley[:NG], low)


VMEM = pl.BlockSpec(memory_space=pltpu.VMEM)
SMEM = pl.BlockSpec(memory_space=pltpu.SMEM)


def call(kernel, out_shape, in_specs, out_specs, flops=0, moved=0, **kwargs):
    return pl.pallas_call(
        kernel,
        out_shape=out_shape,
        in_specs=in_specs,
        out_specs=out_specs,
        compiler_params=pltpu.CompilerParams(vmem_limit_bytes=40 * 2**20),
        cost_estimate=pl.CostEstimate(flops=flops, bytes_accessed=moved, transcendentals=0),
        **kwargs,
    )


def f32_shape(*shape):
    return jax.ShapeDtypeStruct(shape, F32)


CHUNK = f32_shape(PLANES + 1, NG, 128)


def packed(orbitals, k):
    def kernel(block, out):
        out[:PLANES] = block[0, :, :, :128]
        out[PLANES] = jnp.concatenate([block[0, j, :, 128:] for j in range(PLANES)], axis=1)

    return call(
        kernel,
        CHUNK,
        [pl.BlockSpec((1, PLANES, NG, NG), lambda i: (0, k, 0, 0))],
        pl.BlockSpec((PLANES + 1, NG, 128), lambda i: (0, 0, 0)),
        moved=2 * 10**6,
        grid=(1,),
    )(orbitals)


def to_tiles(plane):
    rest = plane[:, 128:]
    moved = rest[:40]
    for g in range(1, 4):
        moved = moved + pltpu.roll(rest[40 * g : 40 * g + 40], 32 * g, 1)
    return plane[:, :128].reshape(-1, 8, 128), moved.reshape(-1, 8, 128)


def from_tiles(tiles):
    main = jnp.concatenate(tiles[:20], axis=0)
    rest = jnp.concatenate(tiles[20:], axis=0)
    lane = lax.broadcasted_iota(jnp.int32, rest.shape, 1)
    parts = [rest] + [pltpu.roll(rest, 128 - 32 * g, 1) for g in range(1, 4)]
    rest = jnp.concatenate([jnp.where(lane < 32, part, 0.0) for part in parts], axis=0)
    return jnp.concatenate([main, rest], axis=1)


def transformed(k, core, own, swap, vis, state, t):
    first, last = k == 0, k == CHUNKS - 1

    def kernel(*refs):
        core, own, swap, vis, table, hartley, ratio, power = refs[:8]
        refs = refs[8:]
        if not first:
            right0, left0, zero0 = refs[:3]
            refs = refs[3:]
        fields = refs[0]
        visiting, resident, partner = vis[...], own[...], swap[...]
        other = jnp.where(core[0] == 1, visiting, resident)
        densities = (resident * visiting, other * partner)
        h = hartley[...]
        r = ratio[...]
        row = lax.broadcasted_iota(jnp.int32, (8, 128), 0)
        lane = lax.broadcasted_iota(jnp.int32, (8, 128), 1)
        zero = jnp.zeros((8, 128), F32) if first else zero0[...]
        for j in range(PLANES):
            both = jnp.concatenate(
                [jnp.concatenate([d[j], d[PLANES]], axis=1) for d in densities], axis=0
            )
            along_x = times_table(both, table[j, 0], table[j, 1])
            for pair in range(2):
                field = table_times(h, along_x[NG * pair : NG * (pair + 1)])
                fields[pair, j] = field
                here = (row == pair) & (lane == PLANES * k + j)
                zero = jnp.where(here, jnp.broadcast_to(field[:1, :1], (8, 128)), zero)
        rights, lefts = [], []
        for pair in range(2):
            right = fields[pair, 0]
            if not first:
                right = right + r * right0[pair]
            left = fields[pair, PLANES - 1]
            for j in range(1, PLANES):
                right = r * right + fields[pair, j]
                left = r * left + fields[pair, PLANES - 1 - j]
            if not first:
                left = left0[pair] + power[0] * left
            rights.append(right)
            lefts.append(left)
        if not last:
            for pair in range(2):
                refs[1][pair] = rights[pair]
                refs[2][pair] = lefts[pair]
            refs[3][...] = zero
            return
        out = refs[1]
        for number, plane in enumerate(rights + lefts):
            main, rest = to_tiles(plane)
            for i in range(MODE_TILES):
                tile = main[i] if i < 20 else rest[i - 20]
                to, slot = divmod(MODE_TILES * number + i, SEND_TILES)
                out[to, slot] = tile
        for i in range(4 * MODE_TILES, SLABS * SEND_TILES):
            out[i // SEND_TILES, i % SEND_TILES] = jnp.zeros((8, 128), F32)
        for to in range(SLABS):
            out[to, SEND_TILES] = zero

    planes = f32_shape(2, NG, WIDE)
    outs = [f32_shape(2, PLANES, NG, WIDE)]
    outs += [f32_shape(SLABS, SEND_TILES + 1, 8, 128)] if last else [planes, planes, f32_shape(8, 128)]
    whole = lambda a: pl.BlockSpec(a.shape, lambda i: (0,) * len(a.shape))
    operands = [core, own, swap, vis, t["forward"], t["hartley"], t["ratio"], t["powers"]]
    specs = [SMEM] + [whole(a) for a in operands[1:7]]
    specs.append(pl.BlockSpec((1, NG, WIDE), lambda i: (k, 0, 0)))
    if not first:
        operands += state
        specs += [whole(a) for a in state]
    return call(
        kernel,
        outs,
        specs,
        [whole(a) for a in outs],
        flops=2 * 10**9,
        moved=5 * 10**6,
        grid=(1,),
    )(*operands)


def local_part(fields, t):
    def kernel(*refs):
        ratio, scale = refs[:2]
        fields, outs = refs[2 : 2 + CHUNKS], refs[2 + CHUNKS :]
        r, c = ratio[...], scale[...]
        for pair in range(2):
            run = jnp.zeros((NG, WIDE), F32)
            for z in range(DEPTH):
                k, j = divmod(z, PLANES)
                run = r * run + fields[k][pair, j]
                outs[k][pair, j] = run
            run = jnp.zeros((NG, WIDE), F32)
            for z in reversed(range(DEPTH)):
                k, j = divmod(z, PLANES)
                outs[k][pair, j] = c * (outs[k][pair, j] + run)
                run = r * (run + fields[k][pair, j])

    shape = f32_shape(2, PLANES, NG, WIDE)
    return call(
        kernel,
        [shape] * CHUNKS,
        [VMEM] * (2 + CHUNKS),
        [VMEM] * CHUNKS,
        flops=10**7,
        moved=13 * 10**6,
    )(t["ratio"], t["scale"], *fields)


def solved(slab, moments, jump, wrap, t):
    def kernel(slab, moments, jump, wrap, table, out, mean):
        me = slab[0]
        for slot in range(SEND_TILES):
            leftward = me * SEND_TILES + slot >= 2 * MODE_TILES
            place = lambda p: jnp.where(leftward, SLABS - 1 - p, p)
            values = [moments[place(p), slot] for p in range(SLABS)]
            r = jump[slot]
            run = values[0]
            for p in range(1, SLABS):
                run = run * r + values[p]
            run = run * wrap[slot]
            for p in range(SLABS):
                out[place(p), slot] = run
                run = values[p] + r * run
        for pair in range(2):
            total = jnp.zeros((24, 128), F32)
            for p in range(SLABS):
                apart = lax.rem(me - p + SLABS, SLABS)
                total = total + table[apart] * moments[p, SEND_TILES, pair : pair + 1, :]
            mean[pair] = jnp.broadcast_to(jnp.sum(total, axis=1, keepdims=True), (24, 128))

    return call(
        kernel,
        [f32_shape(SLABS, SEND_TILES, 8, 128), f32_shape(2, 24, 128)],
        [SMEM] + [VMEM] * 4,
        [VMEM] * 2,
        flops=10**6,
        moved=10**6,
    )(slab, moments, jump, wrap, t["zero"])


def products(k, core, own, swap, vis, local, coming, mean, t):
    def kernel(core, own, swap, vis, local, coming, mean, left, right, table, hartley, sent, crossed, kept):
        h = hartley[...]
        row = lax.broadcasted_iota(jnp.int32, (NG, WIDE), 0)
        lane = lax.broadcasted_iota(jnp.int32, (NG, WIDE), 1)
        corner = (row == 0) & (lane == 0)
        edges = []
        for number in range(4):
            tiles = []
            for i in range(MODE_TILES):
                tiles.append(coming[divmod(MODE_TILES * number + i, SEND_TILES)])
            edges.append(from_tiles(tiles))
        mains = [[], []]
        rests = [None, None]
        for j in range(PLANES):
            along_y = []
            for pair in range(2):
                field = local[pair, j] + left[j] * edges[pair] + right[PLANES - 1 - j] * edges[2 + pair]
                middle = mean[pair, PLANES * k + j : PLANES * k + j + 1, :1]
                field = jnp.where(corner, jnp.broadcast_to(middle, (NG, WIDE)), field)
                along_y.append(table_times(h, field))
            both = times_table(jnp.concatenate(along_y, axis=0), table[j, 0], table[j, 1])
            for pair in range(2):
                field = both[NG * pair : NG * (pair + 1)]
                mains[pair].append(field[:, :128])
                rest = field[:, 128:]
                rests[pair] = rest if j == 0 else rests[pair] + rest
        second = core[0] == 1
        for j in range(PLANES + 1):
            x, y = (mains[pair][j] if j < PLANES else rests[pair] for pair in range(2))
            resident, partner, visiting = own[j], swap[j], vis[j]
            extra = y * partner
            nothing = jnp.zeros_like(extra)
            sent[j] = x * resident + jnp.where(second, extra, nothing)
            kept[j] = x * visiting + jnp.where(second, nothing, extra)
            crossed[j] = y * jnp.where(second, visiting, resident)

    whole = lambda a: pl.BlockSpec(a.shape, lambda i: (0,) * len(a.shape))
    operands = [core, own, swap, vis, local, coming, mean, t["edge"], t["edge"], t["inverse"], t["hartley"]]
    specs = [SMEM] + [whole(a) for a in operands[1:7]]
    specs.append(pl.BlockSpec((PLANES, NG, WIDE), lambda i: (k, 0, 0)))
    specs.append(pl.BlockSpec((PLANES, NG, WIDE), lambda i: (CHUNKS - 1 - k, 0, 0)))
    specs += [whole(a) for a in operands[9:]]
    return call(
        kernel,
        [CHUNK] * 3,
        specs,
        [whole(CHUNK)] * 3,
        flops=2 * 10**9,
        moved=6 * 10**6,
        grid=(1,),
    )(*operands)


def finished(k, kept, crossed, returned, result):
    def kernel(kept, crossed, returned, *refs):
        out = refs[-1]
        total = kept[...] + crossed[...] + returned[...]
        out[0, :, :, :128] = total[:PLANES]
        rest = total[PLANES]
        for j in range(PLANES):
            moved = rest if j == 0 else pltpu.roll(rest, 128 - 32 * j, 1)
            out[0, j, :, 128:] = moved[:, :32]

    operands = [kept, crossed, returned]
    specs = [pl.BlockSpec(CHUNK.shape, lambda i: (0, 0, 0))] * 3
    aliases = {}
    if result is not None:
        operands.append(result)
        specs.append(pl.BlockSpec(memory_space=pl.ANY))
        aliases = {3: 0}
    return call(
        kernel,
        f32_shape(1, DEPTH, NG, NG),
        specs,
        pl.BlockSpec((1, PLANES, NG, NG), lambda i: (0, k, 0, 0)),
        moved=2 * 10**6,
        grid=(1,),
        input_output_aliases=aliases,
    )(*operands)


def shards(orbitals):
    t = {name: jnp.asarray(table) for name, table in tables().items()}
    bands = lax.axis_size("band")
    core = lax.rem(lax.axis_index("band"), 2).astype(jnp.int32).reshape(1)
    slab = lax.axis_index("slab").astype(jnp.int32)
    outward = [(g, (g - 2) % bands if g % 2 == 0 else (g + 2) % bands) for g in range(bands)]
    homeward = [(b, a) for a, b in outward]
    across = [(g, g ^ 1) for g in range(bands)]
    jump = lax.dynamic_slice_in_dim(t["jump"], slab * SEND_TILES, SEND_TILES)
    wrap = lax.dynamic_slice_in_dim(t["wrap"], slab * SEND_TILES, SEND_TILES)

    own = [packed(orbitals, k) for k in range(CHUNKS)]
    vis = [lax.ppermute(chunk, "band", outward) for chunk in own]
    swap = [lax.ppermute(chunk, "band", across) for chunk in own]

    fields, state = [], None
    for k in range(CHUNKS):
        field, *state = transformed(k, core, own[k], swap[k], vis[k], state, t)
        fields.append(field)
    shape = state[0].shape
    moments = state[0].reshape(-1, 128)
    moments = lax.all_to_all(moments, "slab", 0, 0, tiled=True).reshape(shape)
    local = local_part(fields, t)
    coming, mean = solved(slab.reshape(1), moments, jump, wrap, t)
    shape = coming.shape
    coming = lax.all_to_all(coming.reshape(-1, 128), "slab", 0, 0, tiled=True).reshape(shape)

    kept, crossed, returned = [], [], []
    for k in range(CHUNKS):
        sent, partner, here = products(k, core, own[k], swap[k], vis[k], local[k], coming, mean, t)
        returned.append(lax.ppermute(sent, "band", homeward))
        crossed.append(lax.ppermute(partner, "band", across))
        kept.append(here)
    result = None
    for k in range(CHUNKS):
        result = finished(k, kept[k], crossed[k], returned[k], result)
    return result


def solution(mesh):
    spec = P("band", "slab", None, None)
    return jax.shard_map(shards, mesh=mesh, in_specs=(spec,), out_specs=spec, check_vma=False)
```

time: 594 us -> 158 us (0.27); the launches traced: 583 us -> 157 us
  waiting for transfers between devices: 373 us -> 38.2 us
  matrix products: 68.2 us -> 0 us
  Pallas kernels: 0 us -> 36.6 us
  local copies, waits for them, and re-layouts: 64.3 us -> 31.6 us
  starting transfers between devices: 73.6 us -> 50.1 us
    ppermute x4 -> x20, waiting for transfers between devices: 260 us -> 29.8 us  [the longest x5 22.6 us: shards(): returned.append(lax.ppermute(sent, 'band', homeward))]
    all_to_all x4 -> x2, waiting for transfers between devices: 113 us -> 8.41 us  [the longest x1 8.41 us: shards(): moments = lax.all_to_all(moments, 'slab', 0, 0, tiled=True).reshape(shape)]
    dot_general x12 -> x0, matrix products: 68.2 us -> none  [the longest x4 33.3 us: potential(): field = jnp.einsum('yk,zyx->zkx', hartley, field, precision=highest)]
    all_to_all x4 -> x2, starting transfers between devices: 68.3 us -> 11.2 us  [the longest x1 6.54 us: shards(): moments = lax.all_to_all(moments, 'slab', 0, 0, tiled=True).reshape(shape)]
    all_to_all x8 -> x0, local copies, waits for them, and re-layouts: 36.9 us -> none  [the longest x4 18.5 us: potential(): lax.all_to_all(field, 'slab', split_axis=1, concat_axis=0, tiled=True)]
    pallas_call x0 -> x22, Pallas kernels: none -> 36.6 us  [the longest x5 14.9 us: products(): call(kernel, [CHUNK] * 3, specs, [whole(CHUNK)] * 3, flops=2 * 10 ** 9, m...]
    ppermute x4 -> x20, starting transfers between devices: 5.27 us -> 38.9 us  [the longest x5 20.9 us: shards(): vis = [lax.ppermute(chunk, 'band', outward) for chunk in own]]
    unnamed x13 -> x120, local copies, waits for them, and re-layouts: 5.55 us -> 30.8 us
  transfers between devices with their start and end apart: 8 -> 22, of which waited for: 7 -> 8; matrix products, arithmetic and copies ran while one was open for 14% -> 1% of each run, Pallas kernels for 0% -> 18%
where the time goes in v1:
time: 158 us; the launch traced here: 157 us
  starting transfers between devices  50.1 us (32%)
  waiting for transfers between devices  38.2 us (24%)
  Pallas kernels  36.6 us (23%)
  local copies, waits for them, and re-layouts  31.6 us (20%)
    unnamed x120, local copies, waits for them, and re-layouts  30.8 us
    ppermute x5, waiting for transfers between devices, shards(): returned.append(lax.ppermute(sent, 'band', homeward))  22.6 us
    ppermute x5, starting transfers between devices, shards(): vis = [lax.ppermute(chunk, 'band', outward) for chunk in own]  20.9 us
    pallas_call x5, Pallas kernels, products(): call(kernel, [CHUNK] * 3, specs, [whole(CHUNK)] * 3, flops=2 * 10 ** 9, m...  14.9 us
    pallas_call x5, Pallas kernels, transformed(): call(kernel, outs, specs, [whole(a) for a in outs], flops=2 * 10 ** 9, mo...  12.6 us
    ppermute x5, starting transfers between devices, shards(): crossed.append(lax.ppermute(partner, 'band', across))  11.8 us
    all_to_all x1, waiting for transfers between devices, shards(): moments = lax.all_to_all(moments, 'slab', 0, 0, tiled=True).reshape(shape)  8.41 us
    ppermute x5, waiting for transfers between devices, shards(): vis = [lax.ppermute(chunk, 'band', outward) for chunk in own]  7.18 us
  transfers between devices with their start and end apart: 22, of which 8 were waited for; matrix products, arithmetic and copies ran while one was open for 1% of the time, Pallas kernels for 18%

profile of v1, /device:TPU:32, one launch (start us, length us, event | category | flops | bytes accessed | tf_op | source)
XLA Modules:
  0.0 157.1 jit_solution(316891506270941819)
XLA Ops:
  0.0 1.9 %copy-done.1 = f32[1,20,160,160]{3,2,1,0:T(8,128)S(1)} copy-done((f32[1,20,160,160]{3,2,1,0:T(8,128)S(1)}, f32[1,20,160,160]{3,2,1,0:T(8,128)}, u32[]{:S(2)}) %copy-start.1) | copy-done | bytes 2048024
  2.2 7.9 %collective-permute-start.3 = (f32[5,160,128]{2,1,0:T(8,128)S(1)}, f32[5,160,128]{2,1,0:T(8,128)}, u32[]{:S(2)}, u32[]{:S(2)}) collective-permute-start(f32[5,160,128]{2,1,0:T(8,128)S(1)} %shard_map.110.refs_1_.own), channel_id=1, source_target_pairs={{0,240},{8,24},{16,0},{24,40},{32,16},{40,56},{48,32},{56,72},{64,... | collective-permute-start | bytes 1228808 | tf_op jit(solution)/shard_map/ppermute | solution.py:391
  10.3 1.5 collective-permute-start.5
  12.9 4.9 %collective-permute-start.7 = (f32[5,160,128]{2,1,0:T(8,128)S(1)}, f32[5,160,128]{2,1,0:T(8,128)S(1)}, u32[]{:S(2)}, u32[]{:S(2)}) collective-permute-start(f32[5,160,128]{2,1,0:T(8,128)S(1)} %shard_map.114.refs_1_.own), channel_id=1, source_target_pairs={{0,240},{8,24},{16,0},{24,40},{32,16},{40,56},{48,32},{56,72},{64,... | collective-permute-start | bytes 1228808 | tf_op jit(solution)/shard_map/ppermute | solution.py:391
  18.1 2.4 %collective-permute-done.3.refs_3_.vis = f32[5,160,128]{2,1,0:T(8,128)} collective-permute-done((f32[5,160,128]{2,1,0:T(8,128)S(1)}, f32[5,160,128]{2,1,0:T(8,128)}, u32[]{:S(2)}, u32[]{:S(2)}) %collective-permute-start.3) | collective-permute-done | bytes 409632 | tf_op jit(solution)/shard_map/ppermute | solution.py:391
  20.5 3.3 %collective-permute-start.8 = (f32[5,160,128]{2,1,0:T(8,128)S(1)}, f32[5,160,128]{2,1,0:T(8,128)S(1)}, u32[]{:S(2)}, u32[]{:S(2)}) collective-permute-start(f32[5,160,128]{2,1,0:T(8,128)S(1)} %shard_map.116.refs_1_.own), channel_id=1, source_target_pairs={{0,8},{8,0},{16,24},{24,16},{32,40},{40,32},{48,56},{56,48},{64,72... | collective-permute-start | bytes 1228808 | tf_op jit(solution)/shard_map/ppermute | solution.py:392
  23.8 3.6 %collective-permute-start.9 = (f32[5,160,128]{2,1,0:T(8,128)S(1)}, f32[5,160,128]{2,1,0:T(8,128)S(1)}, u32[]{:S(2)}, u32[]{:S(2)}) collective-permute-start(f32[5,160,128]{2,1,0:T(8,128)S(1)} %shard_map.116.refs_1_.own), channel_id=1, source_target_pairs={{0,240},{8,24},{16,0},{24,40},{32,16},{40,56},{48,32},{56,72},{64,... | collective-permute-start | bytes 1228808 | tf_op jit(solution)/shard_map/ppermute | solution.py:391
  31.7 3.0 %shard_map.111 = (f32[2,4,160,256]{3,2,1,0:T(8,128)S(1)}, f32[2,160,256]{2,1,0:T(8,128)S(1)}, f32[2,160,256]{2,1,0:T(8,128)S(1)}, f32[8,128]{1,0:T(8,128)S(1)}) custom-call(s32[1]{0:T(128)} %bitcast.refs_0_.core, f32[5,160,128]{2,1,0:T(8,128)S(1)} %shard_map.110.refs_1_.own, f32[5,160,128]{2,1,0:T(8,128)S(1)} %copy-done.41, ...), custom_call_target="tpu_custom_call" | custom-call | flops 2000000000 | bytes 5000000 | tf_op jit(solution)/shard_map/pallas_call | solution.py:226
  36.1 2.9 %collective-permute-start.1 = (f32[5,160,128]{2,1,0:T(8,128)S(1)}, f32[5,160,128]{2,1,0:T(8,128)S(1)}, u32[]{:S(2)}, u32[]{:S(2)}) collective-permute-start(f32[5,160,128]{2,1,0:T(8,128)S(1)} %shard_map.109.refs_1_.own), channel_id=1, source_target_pairs={{0,240},{8,24},{16,0},{24,40},{32,16},{40,56},{48,32},{56,72},{64,... | collective-permute-start | bytes 1228808 | tf_op jit(solution)/shard_map/ppermute | solution.py:391
  39.0 2.9 %shard_map.113 = (f32[2,4,160,256]{3,2,1,0:T(8,128)S(1)}, f32[2,160,256]{2,1,0:T(8,128)S(1)}, f32[2,160,256]{2,1,0:T(8,128)S(1)}, f32[8,128]{1,0:T(8,128)S(1)}) custom-call(s32[1]{0:T(128)} %bitcast.refs_0_.core, f32[5,160,128]{2,1,0:T(8,128)S(1)} %shard_map.112.refs_1_.own, f32[5,160,128]{2,1,0:T(8,128)S(1)} %collective-permute-done.4.refs_2_.swap, ...), custom_call_target="tpu_custom_call" | custom-call | flops 2000000000 | bytes 5000000 | tf_op jit(solution)/shard_map/pallas_call | solution.py:226
  43.0 1.9 %shard_map.115 = (f32[2,4,160,256]{3,2,1,0:T(8,128)S(1)}, f32[2,160,256]{2,1,0:T(8,128)S(1)}, f32[2,160,256]{2,1,0:T(8,128)S(1)}, f32[8,128]{1,0:T(8,128)S(1)}) custom-call(s32[1]{0:T(128)} %bitcast.refs_0_.core, f32[5,160,128]{2,1,0:T(8,128)S(1)} %shard_map.114.refs_1_.own, f32[5,160,128]{2,1,0:T(8,128)S(1)} %collective-permute-done.6.refs_2_.swap, ...), custom_call_target="tpu_custom_call" | custom-call | flops 2000000000 | bytes 5000000 | tf_op jit(solution)/shard_map/pallas_call | solution.py:226
  46.0 3.4 %collective-permute-done.9.refs_3_.vis = f32[5,160,128]{2,1,0:T(8,128)S(1)} collective-permute-done((f32[5,160,128]{2,1,0:T(8,128)S(1)}, f32[5,160,128]{2,1,0:T(8,128)S(1)}, u32[]{:S(2)}, u32[]{:S(2)}) %collective-permute-start.9) | collective-permute-done | bytes 409632 | tf_op jit(solution)/shard_map/ppermute | solution.py:391
  49.5 1.9 %shard_map.117 = (f32[2,4,160,256]{3,2,1,0:T(8,128)S(1)}, f32[2,160,256]{2,1,0:T(8,128)S(1)}, f32[2,160,256]{2,1,0:T(8,128)S(1)}, f32[8,128]{1,0:T(8,128)S(1)}) custom-call(s32[1]{0:T(128)} %bitcast.refs_0_.core, f32[5,160,128]{2,1,0:T(8,128)S(1)} %shard_map.116.refs_1_.own, f32[5,160,128]{2,1,0:T(8,128)S(1)} %collective-permute-done.8.refs_2_.swap, ...), custom_call_target="tpu_custom_call" | custom-call | flops 2000000000 | bytes 5000000 | tf_op jit(solution)/shard_map/pallas_call | solution.py:226
  52.5 1.4 collective-permute-done.1.refs_3_.vis
  53.8 2.8 %shard_map.118 = (f32[2,4,160,256]{3,2,1,0:T(8,128)S(1)}, f32[8,14,8,128]{3,2,1,0:T(8,128)}) custom-call(s32[1]{0:T(128)} %bitcast.refs_0_.core, f32[5,160,128]{2,1,0:T(8,128)S(1)} %shard_map.109.refs_1_.own, f32[5,160,128]{2,1,0:T(8,128)S(1)} %collective-permute-done.refs_2_.swap, f32[5,160,128]{2,1,0:T(8,128)S(1)} %collective-permute-done.1.refs_3_.vis, ...), custom_call_target="tpu_custom_call" | custom-call | flops 2000000000 | bytes 5000000 | tf_op jit(solution)/shard_map/pallas_call | solution.py:226
  57.7 6.5 %all-to-all-start = ((f32[8,112,128]{2,1,0:T(8,128)}), f32[8,112,128]{2,1,0:T(8,128)S(1)}, u32[]{:S(2)}, u32[]{:S(2)}) async-start(f32[8,112,128]{2,1,0:T(8,128)} %bitcast.2), calls=%async_computation | async-start | bytes 917504 | tf_op jit(solution)/shard_map/all_to_all | solution.py:400
  65.1 8.4 %all-to-all-done = f32[8,112,128]{2,1,0:T(8,128)S(1)} async-done(((f32[8,112,128]{2,1,0:T(8,128)}), f32[8,112,128]{2,1,0:T(8,128)S(1)}, u32[]{:S(2)}, u32[]{:S(2)}) %all-to-all-start) | async-done | bytes 458784 | tf_op jit(solution)/shard_map/all_to_all | solution.py:400
  74.5 4.7 %all-to-all-start.1 = ((f32[8,104,128]{2,1,0:T(8,128)}), f32[8,104,128]{2,1,0:T(8,128)}, u32[]{:S(2)}, u32[]{:S(2)}) async-start(f32[8,104,128]{2,1,0:T(8,128)} %bitcast.4), calls=%async_computation.1 | async-start | bytes 851968 | tf_op jit(solution)/shard_map/all_to_all | solution.py:404
  81.8 1.3 copy-done.29
  87.6 2.5 %shard_map.119 = (f32[2,4,160,256]{3,2,1,0:T(8,128)S(1)}, f32[2,4,160,256]{3,2,1,0:T(8,128)S(1)}, f32[2,4,160,256]{3,2,1,0:T(8,128)S(1)}, f32[2,4,160,256]{3,2,1,0:T(8,128)S(1)}, f32[2,4,160,256]{3,2,1,0:T(8,128)S(1)}) custom-call(f32[160,256]{1,0:T(8,128)S(1)} %copy-done.53, f32[160,256]{1,0:T(8,128)S(1)} %copy-done.54, f32[2,4,160,256]{3,2,1,0:T(8,128)S(1)} %copy-done.25, ...), custom_call_target="tpu_custom_call" | custom-call | flops 10000000 | bytes 13000000 | tf_op jit(solution)/shard_map/pallas_call | solution.py:255
  100.1 3.1 %shard_map.125 = (f32[5,160,128]{2,1,0:T(8,128)S(1)}, f32[5,160,128]{2,1,0:T(8,128)S(1)}, f32[5,160,128]{2,1,0:T(8,128)S(1)}) custom-call(s32[1]{0:T(128)} %bitcast.refs_0_.core, f32[5,160,128]{2,1,0:T(8,128)S(1)} %copy-done.13, f32[5,160,128]{2,1,0:T(8,128)S(1)} %copy-done.42, f32[5,160,128]{2,1,0:T(8,128)} %collective-permute-done.3.refs_3_.vis, ...), custom_call_target="tpu_custom_call" | custom-call | flops 2000000000 | bytes 6000000 | tf_op jit(solution)/shard_map/pallas_call | solution.py:340
  103.7 3.1 %shard_map.124 = (f32[5,160,128]{2,1,0:T(8,128)S(1)}, f32[5,160,128]{2,1,0:T(8,128)S(1)}, f32[5,160,128]{2,1,0:T(8,128)S(1)}) custom-call(s32[1]{0:T(128)} %bitcast.refs_0_.core, f32[5,160,128]{2,1,0:T(8,128)S(1)} %copy-done.11, f32[5,160,128]{2,1,0:T(8,128)S(1)} %copy-done.39, f32[5,160,128]{2,1,0:T(8,128)} %collective-permute-done.5.refs_3_.vis, ...), custom_call_target="tpu_custom_call" | custom-call | flops 2000000000 | bytes 6000000 | tf_op jit(solution)/shard_map/pallas_call | solution.py:340
  106.8 4.8 %collective-permute-start.16 = (f32[5,160,128]{2,1,0:T(8,128)S(1)}, f32[5,160,128]{2,1,0:T(8,128)S(1)}, u32[]{:S(2)}, u32[]{:S(2)}) collective-permute-start(f32[5,160,128]{2,1,0:T(8,128)S(1)} %get-tuple-element.79), channel_id=1, source_target_pairs={{0,8},{8,0},{16,24},{24,16},{32,40},{40,32},{48,56},{56,48},{64,72... | collective-permute-start | bytes 1228808 | tf_op jit(solution)/shard_map/ppermute | solution.py:410
  111.6 3.0 %shard_map.123 = (f32[5,160,128]{2,1,0:T(8,128)S(1)}, f32[5,160,128]{2,1,0:T(8,128)S(1)}, f32[5,160,128]{2,1,0:T(8,128)S(1)}) custom-call(s32[1]{0:T(128)} %bitcast.refs_0_.core, f32[5,160,128]{2,1,0:T(8,128)S(1)} %copy-done.7, f32[5,160,128]{2,1,0:T(8,128)S(1)} %copy-done.35, f32[5,160,128]{2,1,0:T(8,128)S(1)} %copy-done.37, ...), custom_call_target="tpu_custom_call" | custom-call | flops 2000000000 | bytes 6000000 | tf_op jit(solution)/shard_map/pallas_call | solution.py:340
  114.6 1.8 %collective-permute-start.14 = (f32[5,160,128]{2,1,0:T(8,128)S(1)}, f32[5,160,128]{2,1,0:T(8,128)S(1)}, u32[]{:S(2)}, u32[]{:S(2)}) collective-permute-start(f32[5,160,128]{2,1,0:T(8,128)S(1)} %get-tuple-element.75), channel_id=1, source_target_pairs={{0,8},{8,0},{16,24},{24,16},{32,40},{40,32},{48,56},{56,48},{64,72... | collective-permute-start | bytes 1228808 | tf_op jit(solution)/shard_map/ppermute | solution.py:410
  116.5 3.0 %shard_map.122 = (f32[5,160,128]{2,1,0:T(8,128)S(1)}, f32[5,160,128]{2,1,0:T(8,128)S(1)}, f32[5,160,128]{2,1,0:T(8,128)S(1)}) custom-call(s32[1]{0:T(128)} %bitcast.refs_0_.core, f32[5,160,128]{2,1,0:T(8,128)S(1)} %copy-done.9, f32[5,160,128]{2,1,0:T(8,128)S(1)} %copy-done.44, f32[5,160,128]{2,1,0:T(8,128)S(1)} %copy-done.46, ...), custom_call_target="tpu_custom_call" | custom-call | flops 2000000000 | bytes 6000000 | tf_op jit(solution)/shard_map/pallas_call | solution.py:340
  119.5 2.8 %shard_map.121 = (f32[5,160,128]{2,1,0:T(8,128)S(1)}, f32[5,160,128]{2,1,0:T(8,128)S(1)}, f32[5,160,128]{2,1,0:T(8,128)S(1)}) custom-call(s32[1]{0:T(128)} %bitcast.refs_0_.core, f32[5,160,128]{2,1,0:T(8,128)S(1)} %copy-done.5, f32[5,160,128]{2,1,0:T(8,128)S(1)} %copy-done.48, f32[5,160,128]{2,1,0:T(8,128)S(1)} %copy-done.50, ...), custom_call_target="tpu_custom_call" | custom-call | flops 2000000000 | bytes 6000000 | tf_op jit(solution)/shard_map/pallas_call | solution.py:340
  123.4 3.7 %collective-permute-start.12 = (f32[5,160,128]{2,1,0:T(8,128)S(1)}, f32[5,160,128]{2,1,0:T(8,128)S(1)}, u32[]{:S(2)}, u32[]{:S(2)}) collective-permute-start(f32[5,160,128]{2,1,0:T(8,128)S(1)} %get-tuple-element.71), channel_id=1, source_target_pairs={{0,8},{8,0},{16,24},{24,16},{32,40},{40,32},{48,56},{56,48},{64,72... | collective-permute-start | bytes 1228808 | tf_op jit(solution)/shard_map/ppermute | solution.py:410
  127.5 1.4 collective-permute-start.10
  131.8 10.5 %collective-permute-done.15.returned = f32[5,160,128]{2,1,0:T(8,128)S(1)} collective-permute-done((f32[5,160,128]{2,1,0:T(8,128)S(1)}, f32[5,160,128]{2,1,0:T(8,128)S(1)}, u32[]{:S(2)}, u32[]{:S(2)}) %collective-permute-start.15) | collective-permute-done | bytes 409632 | tf_op jit(solution)/shard_map/ppermute | solution.py:409
  143.3 8.4 %collective-permute-done.13.returned = f32[5,160,128]{2,1,0:T(8,128)S(1)} collective-permute-done((f32[5,160,128]{2,1,0:T(8,128)S(1)}, f32[5,160,128]{2,1,0:T(8,128)S(1)}, u32[]{:S(2)}, u32[]{:S(2)}) %collective-permute-start.13) | collective-permute-done | bytes 409632 | tf_op jit(solution)/shard_map/ppermute | solution.py:409
  152.7 3.4 %collective-permute-done.11.returned = f32[5,160,128]{2,1,0:T(8,128)S(1)} collective-permute-done((f32[5,160,128]{2,1,0:T(8,128)S(1)}, f32[5,160,128]{2,1,0:T(8,128)S(1)}, u32[]{:S(2)}, u32[]{:S(2)}) %collective-permute-start.11) | collective-permute-done | bytes 409632 | tf_op jit(solution)/shard_map/ppermute | solution.py:409
  (155 shorter events, 38.4 us)
Async XLA Ops:
  2.1 25.3 %copy-start.12 = (f32[5,160,128]{2,1,0:T(8,128)}, f32[5,160,128]{2,1,0:T(8,128)S(1)}, u32[]{:S(2)}) copy-start(f32[5,160,128]{2,1,0:T(8,128)S(1)} %shard_map.110.refs_1_.own) | copy-start | bytes 1228804
  2.1 10.1 %collective-permute-start.2 = (f32[5,160,128]{2,1,0:T(8,128)S(1)}, f32[5,160,128]{2,1,0:T(8,128)S(1)}, u32[]{:S(2)}, u32[]{:S(2)}) collective-permute-start(f32[5,160,128]{2,1,0:T(8,128)S(1)} %shard_map.110.refs_1_.own), channel_id=1, source_target_pairs={{0,8},{8,0},{16,24},{24,16},{32,40},{40,32},{48,56},{56,48},{64,72... | collective-permute-start | bytes 1228808 | tf_op jit(solution)/shard_map/ppermute | solution.py:392
  2.2 18.3 %collective-permute-start.3 = (f32[5,160,128]{2,1,0:T(8,128)S(1)}, f32[5,160,128]{2,1,0:T(8,128)}, u32[]{:S(2)}, u32[]{:S(2)}) collective-permute-start(f32[5,160,128]{2,1,0:T(8,128)S(1)} %shard_map.110.refs_1_.own), channel_id=1, source_target_pairs={{0,240},{8,24},{16,0},{24,40},{32,16},{40,56},{48,32},{56,72},{64,... | collective-permute-start | bytes 1228808 | tf_op jit(solution)/shard_map/ppermute | solution.py:391
  10.2 28.7 %copy-start.10 = (f32[5,160,128]{2,1,0:T(8,128)}, f32[5,160,128]{2,1,0:T(8,128)S(1)}, u32[]{:S(2)}) copy-start(f32[5,160,128]{2,1,0:T(8,128)S(1)} %shard_map.112.refs_1_.own) | copy-start | bytes 1228804
  10.2 13.5 %collective-permute-start.4 = (f32[5,160,128]{2,1,0:T(8,128)S(1)}, f32[5,160,128]{2,1,0:T(8,128)S(1)}, u32[]{:S(2)}, u32[]{:S(2)}) collective-permute-start(f32[5,160,128]{2,1,0:T(8,128)S(1)} %shard_map.112.refs_1_.own), channel_id=1, source_target_pairs={{0,8},{8,0},{16,24},{24,16},{32,40},{40,32},{48,56},{56,48},{64,72... | collective-permute-start | bytes 1228808 | tf_op jit(solution)/shard_map/ppermute | solution.py:392
  10.3 25.4 %collective-permute-start.5 = (f32[5,160,128]{2,1,0:T(8,128)S(1)}, f32[5,160,128]{2,1,0:T(8,128)}, u32[]{:S(2)}, u32[]{:S(2)}) collective-permute-start(f32[5,160,128]{2,1,0:T(8,128)S(1)} %shard_map.112.refs_1_.own), channel_id=1, source_target_pairs={{0,240},{8,24},{16,0},{24,40},{32,16},{40,56},{48,32},{56,72},{64,... | collective-permute-start | bytes 1228808 | tf_op jit(solution)/shard_map/ppermute | solution.py:391
  12.0 31.0 %copy-start.6 = (f32[5,160,128]{2,1,0:T(8,128)}, f32[5,160,128]{2,1,0:T(8,128)S(1)}, u32[]{:S(2)}) copy-start(f32[5,160,128]{2,1,0:T(8,128)S(1)} %shard_map.114.refs_1_.own) | copy-start | bytes 1228804
  12.0 24.1 %collective-permute-start.6 = (f32[5,160,128]{2,1,0:T(8,128)S(1)}, f32[5,160,128]{2,1,0:T(8,128)S(1)}, u32[]{:S(2)}, u32[]{:S(2)}) collective-permute-start(f32[5,160,128]{2,1,0:T(8,128)S(1)} %shard_map.114.refs_1_.own), channel_id=1, source_target_pairs={{0,8},{8,0},{16,24},{24,16},{32,40},{40,32},{48,56},{56,48},{64,72... | collective-permute-start | bytes 1228808 | tf_op jit(solution)/shard_map/ppermute | solution.py:392
  12.9 30.1 %collective-permute-start.7 = (f32[5,160,128]{2,1,0:T(8,128)S(1)}, f32[5,160,128]{2,1,0:T(8,128)S(1)}, u32[]{:S(2)}, u32[]{:S(2)}) collective-permute-start(f32[5,160,128]{2,1,0:T(8,128)S(1)} %shard_map.114.refs_1_.own), channel_id=1, source_target_pairs={{0,240},{8,24},{16,0},{24,40},{32,16},{40,56},{48,32},{56,72},{64,... | collective-permute-start | bytes 1228808 | tf_op jit(solution)/shard_map/ppermute | solution.py:391
  18.0 31.5 %copy-start.8 = (f32[5,160,128]{2,1,0:T(8,128)}, f32[5,160,128]{2,1,0:T(8,128)S(1)}, u32[]{:S(2)}) copy-start(f32[5,160,128]{2,1,0:T(8,128)S(1)} %shard_map.116.refs_1_.own) | copy-start | bytes 1228804
  18.0 9.4 %copy-start.3 = (bf16[320,160]{1,0:T(8,128)(2,1)S(1)}, bf16[320,160]{1,0:T(8,128)(2,1)}, u32[]{:S(2)}) copy-start(bf16[320,160]{1,0:T(8,128)(2,1)} %constant.41.clone.refs_5_.hartley) | copy-start | bytes 307204
  18.1 35.7 %copy-start.4 = (f32[5,160,128]{2,1,0:T(8,128)}, f32[5,160,128]{2,1,0:T(8,128)S(1)}, u32[]{:S(2)}) copy-start(f32[5,160,128]{2,1,0:T(8,128)S(1)} %shard_map.109.refs_1_.own) | copy-start | bytes 1228804
  20.5 25.5 %collective-permute-start.8 = (f32[5,160,128]{2,1,0:T(8,128)S(1)}, f32[5,160,128]{2,1,0:T(8,128)S(1)}, u32[]{:S(2)}, u32[]{:S(2)}) collective-permute-start(f32[5,160,128]{2,1,0:T(8,128)S(1)} %shard_map.116.refs_1_.own), channel_id=1, source_target_pairs={{0,8},{8,0},{16,24},{24,16},{32,40},{40,32},{48,56},{56,48},{64,72... | collective-permute-start | bytes 1228808 | tf_op jit(solution)/shard_map/ppermute | solution.py:392
  23.8 15.2 %copy-start.38 = (f32[5,160,128]{2,1,0:T(8,128)}, f32[5,160,128]{2,1,0:T(8,128)S(1)}, u32[]{:S(2)}) copy-start(f32[5,160,128]{2,1,0:T(8,128)S(1)} %collective-permute-done.4.refs_2_.swap) | copy-start | bytes 1228804
  23.8 25.7 %collective-permute-start.9 = (f32[5,160,128]{2,1,0:T(8,128)S(1)}, f32[5,160,128]{2,1,0:T(8,128)S(1)}, u32[]{:S(2)}, u32[]{:S(2)}) collective-permute-start(f32[5,160,128]{2,1,0:T(8,128)S(1)} %shard_map.116.refs_1_.own), channel_id=1, source_target_pairs={{0,240},{8,24},{16,0},{24,40},{32,16},{40,56},{48,32},{56,72},{64,... | collective-permute-start | bytes 1228808 | tf_op jit(solution)/shard_map/ppermute | solution.py:391
  35.8 16.7 %collective-permute-start = (f32[5,160,128]{2,1,0:T(8,128)S(1)}, f32[5,160,128]{2,1,0:T(8,128)S(1)}, u32[]{:S(2)}, u32[]{:S(2)}) collective-permute-start(f32[5,160,128]{2,1,0:T(8,128)S(1)} %shard_map.109.refs_1_.own), channel_id=1, source_target_pairs={{0,8},{8,0},{16,24},{24,16},{32,40},{40,32},{48,56},{56,48},{64,72... | collective-permute-start | bytes 1228808 | tf_op jit(solution)/shard_map/ppermute | solution.py:392
  36.1 17.8 %collective-permute-start.1 = (f32[5,160,128]{2,1,0:T(8,128)S(1)}, f32[5,160,128]{2,1,0:T(8,128)S(1)}, u32[]{:S(2)}, u32[]{:S(2)}) collective-permute-start(f32[5,160,128]{2,1,0:T(8,128)S(1)} %shard_map.109.refs_1_.own), channel_id=1, source_target_pairs={{0,240},{8,24},{16,0},{24,40},{32,16},{40,56},{48,32},{56,72},{64,... | collective-permute-start | bytes 1228808 | tf_op jit(solution)/shard_map/ppermute | solution.py:391
  53.8 19.7 %copy-start.55 = (f32[8,24,128]{2,1,0:T(8,128)S(1)}, f32[8,24,128]{2,1,0:T(8,128)}, u32[]{:S(2)}) copy-start(f32[8,24,128]{2,1,0:T(8,128)} %constant.48.clone.table) | copy-start | bytes 294916
  57.7 15.8 %all-to-all-start = ((f32[8,112,128]{2,1,0:T(8,128)}), f32[8,112,128]{2,1,0:T(8,128)S(1)}, u32[]{:S(2)}, u32[]{:S(2)}) async-start(f32[8,112,128]{2,1,0:T(8,128)} %bitcast.2), calls=%async_computation | async-start | bytes 917504 | tf_op jit(solution)/shard_map/all_to_all | solution.py:400
  74.5 21.0 %all-to-all-start.1 = ((f32[8,104,128]{2,1,0:T(8,128)}), f32[8,104,128]{2,1,0:T(8,128)}, u32[]{:S(2)}, u32[]{:S(2)}) async-start(f32[8,104,128]{2,1,0:T(8,128)} %bitcast.4), calls=%async_computation.1 | async-start | bytes 851968 | tf_op jit(solution)/shard_map/all_to_all | solution.py:404
  87.6 7.9 %copy-start = (f32[20,160,256]{2,1,0:T(8,128)S(1)}, f32[20,160,256]{2,1,0:T(8,128)}, u32[]{:S(2)}) copy-start(f32[20,160,256]{2,1,0:T(8,128)} %constant.45.clone.left.right) | copy-start | bytes 9830404
  103.2 19.1 %collective-permute-start.18 = (f32[5,160,128]{2,1,0:T(8,128)S(1)}, f32[5,160,128]{2,1,0:T(8,128)S(1)}, u32[]{:S(2)}, u32[]{:S(2)}) collective-permute-start(f32[5,160,128]{2,1,0:T(8,128)S(1)} %get-tuple-element.83), channel_id=1, source_target_pairs={{0,8},{8,0},{16,24},{24,16},{32,40},{40,32},{48,56},{56,48},{64,72... | collective-permute-start | bytes 1228808 | tf_op jit(solution)/shard_map/ppermute | solution.py:410
  103.3 20.1 %collective-permute-start.19 = (f32[5,160,128]{2,1,0:T(8,128)S(1)}, f32[5,160,128]{2,1,0:T(8,128)S(1)}, u32[]{:S(2)}, u32[]{:S(2)}) collective-permute-start(f32[5,160,128]{2,1,0:T(8,128)S(1)} %get-tuple-element.84), channel_id=1, source_target_pairs={{240,0},{24,8},{0,16},{40,24},{16,32},{56,40},{32,48},{72,56},{48,... | collective-permute-start | bytes 1228808 | tf_op jit(solution)/shard_map/ppermute | solution.py:409
  103.6 7.9 %copy-start.7 = (f32[5,160,128]{2,1,0:T(8,128)S(1)}, f32[5,160,128]{2,1,0:T(8,128)}, u32[]{:S(2)}) copy-start(f32[5,160,128]{2,1,0:T(8,128)} %copy-done.6) | copy-start | bytes 1228804
  106.8 20.3 %collective-permute-start.16 = (f32[5,160,128]{2,1,0:T(8,128)S(1)}, f32[5,160,128]{2,1,0:T(8,128)S(1)}, u32[]{:S(2)}, u32[]{:S(2)}) collective-permute-start(f32[5,160,128]{2,1,0:T(8,128)S(1)} %get-tuple-element.79), channel_id=1, source_target_pairs={{0,8},{8,0},{16,24},{24,16},{32,40},{40,32},{48,56},{56,48},{64,72... | collective-permute-start | bytes 1228808 | tf_op jit(solution)/shard_map/ppermute | solution.py:410
  111.5 15.9 %collective-permute-start.17 = (f32[5,160,128]{2,1,0:T(8,128)S(1)}, f32[5,160,128]{2,1,0:T(8,128)S(1)}, u32[]{:S(2)}, u32[]{:S(2)}) collective-permute-start(f32[5,160,128]{2,1,0:T(8,128)S(1)} %get-tuple-element.80), channel_id=1, source_target_pairs={{240,0},{24,8},{0,16},{40,24},{16,32},{56,40},{32,48},{72,56},{48,... | collective-permute-start | bytes 1228808 | tf_op jit(solution)/shard_map/ppermute | solution.py:409
  114.6 14.3 %collective-permute-start.14 = (f32[5,160,128]{2,1,0:T(8,128)S(1)}, f32[5,160,128]{2,1,0:T(8,128)S(1)}, u32[]{:S(2)}, u32[]{:S(2)}) collective-permute-start(f32[5,160,128]{2,1,0:T(8,128)S(1)} %get-tuple-element.75), channel_id=1, source_target_pairs={{0,8},{8,0},{16,24},{24,16},{32,40},{40,32},{48,56},{56,48},{64,72... | collective-permute-start | bytes 1228808 | tf_op jit(solution)/shard_map/ppermute | solution.py:410
  122.3 20.0 %collective-permute-start.15 = (f32[5,160,128]{2,1,0:T(8,128)S(1)}, f32[5,160,128]{2,1,0:T(8,128)S(1)}, u32[]{:S(2)}, u32[]{:S(2)}) collective-permute-start(f32[5,160,128]{2,1,0:T(8,128)S(1)} %get-tuple-element.76), channel_id=1, source_target_pairs={{240,0},{24,8},{0,16},{40,24},{16,32},{56,40},{32,48},{72,56},{48,... | collective-permute-start | bytes 1228808 | tf_op jit(solution)/shard_map/ppermute | solution.py:409
  123.4 19.9 %collective-permute-start.12 = (f32[5,160,128]{2,1,0:T(8,128)S(1)}, f32[5,160,128]{2,1,0:T(8,128)S(1)}, u32[]{:S(2)}, u32[]{:S(2)}) collective-permute-start(f32[5,160,128]{2,1,0:T(8,128)S(1)} %get-tuple-element.71), channel_id=1, source_target_pairs={{0,8},{8,0},{16,24},{24,16},{32,40},{40,32},{48,56},{56,48},{64,72... | collective-permute-start | bytes 1228808 | tf_op jit(solution)/shard_map/ppermute | solution.py:410
  127.1 24.6 %collective-permute-start.13 = (f32[5,160,128]{2,1,0:T(8,128)S(1)}, f32[5,160,128]{2,1,0:T(8,128)S(1)}, u32[]{:S(2)}, u32[]{:S(2)}) collective-permute-start(f32[5,160,128]{2,1,0:T(8,128)S(1)} %get-tuple-element.72), channel_id=1, source_target_pairs={{240,0},{24,8},{0,16},{40,24},{16,32},{56,40},{32,48},{72,56},{48,... | collective-permute-start | bytes 1228808 | tf_op jit(solution)/shard_map/ppermute | solution.py:409
  127.5 25.2 %collective-permute-start.10 = (f32[5,160,128]{2,1,0:T(8,128)S(1)}, f32[5,160,128]{2,1,0:T(8,128)S(1)}, u32[]{:S(2)}, u32[]{:S(2)}) collective-permute-start(f32[5,160,128]{2,1,0:T(8,128)S(1)} %get-tuple-element.67), channel_id=1, source_target_pairs={{0,8},{8,0},{16,24},{24,16},{32,40},{40,32},{48,56},{56,48},{64,72... | collective-permute-start | bytes 1228808 | tf_op jit(solution)/shard_map/ppermute | solution.py:410
  128.9 27.2 %collective-permute-start.11 = (f32[5,160,128]{2,1,0:T(8,128)S(1)}, f32[5,160,128]{2,1,0:T(8,128)S(1)}, u32[]{:S(2)}, u32[]{:S(2)}) collective-permute-start(f32[5,160,128]{2,1,0:T(8,128)S(1)} %get-tuple-element.68), channel_id=1, source_target_pairs={{240,0},{24,8},{0,16},{40,24},{16,32},{56,40},{32,48},{72,56},{48,... | collective-permute-start | bytes 1228808 | tf_op jit(solution)/shard_map/ppermute | solution.py:409
  (50 other events, 141.3 us)

commit v2 on v1

v2 whole, which is shorter than its diff:
```python
import functools

import jax
import jax.numpy as jnp
import ml_dtypes
import numpy as np
from jax import lax
from jax.experimental import pallas as pl
from jax.experimental.pallas import tpu as pltpu
from jax.sharding import PartitionSpec as P

NG = 160
SLABS = 8
DEPTH = NG // SLABS
PLANES = 4
CHUNKS = DEPTH // PLANES
WIDE = 256
MODE_TILES = NG * NG // 1024
SEND_TILES = 13
F32 = jnp.float32
BF16 = jnp.bfloat16


def split_table(table):
    high = table.astype(np.float32).astype(ml_dtypes.bfloat16)
    low = (table - high.astype(np.float64)).astype(np.float32).astype(ml_dtypes.bfloat16)
    return high, low


def stacked(table, axis):
    high, low = split_table(table)
    return np.concatenate([high, high, low] if axis == 0 else [high, low, high], axis=axis)


def plane_tiles(plane):
    main = plane[:, :128].reshape(-1, 8, 128)
    rest = np.concatenate([plane[40 * g : 40 * g + 40, 128:] for g in range(4)], axis=1)
    return np.concatenate([main, rest.reshape(-1, 8, 128)])


def widened(plane):
    return np.pad(plane, [(0, 0)] * (plane.ndim - 1) + [(0, WIDE - NG)])


@functools.cache
def tables():
    index = np.arange(NG)
    angle = 2.0 * np.pi * (index[:, None] * index[None, :] % NG) / NG
    hartley = np.cos(angle) + np.sin(angle)
    forward = np.zeros((WIDE, WIDE))
    forward[:128, :NG] = hartley[:128]
    forward[128:, :NG] = np.tile(hartley[128:], (PLANES, 1))
    inverse = np.zeros((WIDE, WIDE))
    inverse[:NG, :128] = hartley[:, :128]
    inverse[:NG, 128:] = np.tile(hartley[:, 128:], (1, PLANES))
    wave = 4.0 * np.sin(np.pi * index / NG) ** 2
    lam = wave[:, None] + wave[None, :]
    ratio = 1.0 / (1.0 + lam / 2 + np.sqrt(lam + lam * lam / 4))
    ratio[0, 0] = 0.0
    scale = ratio / (1.0 - ratio**2) / NG**2
    powers = np.stack([ratio ** (PLANES * k) for k in range(CHUNKS)])
    edge = np.stack([scale * ratio ** (i + 1) for i in range(DEPTH)])
    jump = np.tile(plane_tiles(ratio**DEPTH), (4, 1, 1))
    wrap = np.tile(plane_tiles(1.0 / (1.0 - ratio**NG)), (4, 1, 1))
    spare = [(0, SLABS * SEND_TILES - 4 * MODE_TILES), (0, 0), (0, 0)]
    zero = np.zeros((SLABS, 24, 128))
    for apart in range(SLABS):
        for i in range(DEPTH):
            d = (DEPTH * apart + i - np.arange(DEPTH)) % NG
            zero[apart, i, :DEPTH] = ((NG**2 - 1) / (12 * NG) - d * (NG - d) / (2 * NG)) / NG**2
    as32 = lambda a: a.astype(np.float32)
    return dict(
        forward=stacked(forward, 0),
        inverse=stacked(inverse, 0),
        hartley=stacked(hartley, 1),
        ratio=as32(widened(ratio)),
        scale=as32(widened(scale)),
        powers=as32(widened(powers)),
        edge=as32(widened(edge)),
        jump=as32(np.pad(jump, spare)),
        wrap=as32(np.pad(wrap, spare)),
        zero=as32(zero),
    )


def split(value):
    high = value.astype(BF16)
    return high, (value - high.astype(F32)).astype(BF16)


def dot(a, b):
    return jnp.dot(a, b, preferred_element_type=F32)


def times_table(value, table):
    high, low = split(value)
    return dot(jnp.concatenate([high, low, high], axis=1), table)


def table_times(table, value):
    high, low = split(value)
    return dot(table, jnp.concatenate([high, high, low], axis=0))


VMEM = pl.BlockSpec(memory_space=pltpu.VMEM)
SMEM = pl.BlockSpec(memory_space=pltpu.SMEM)
HBM = pl.BlockSpec(memory_space=pltpu.HBM)
GROUPS = (2, 2, 1)
FIRST = tuple(sum(GROUPS[:g]) for g in range(len(GROUPS)))


def call(kernel, name, operands, outs, in_specs=None, out_specs=VMEM, limit=14, **kwargs):
    if in_specs is None:
        in_specs = [VMEM] * len(operands)
    return pl.pallas_call(
        kernel,
        name=name,
        out_shape=outs,
        in_specs=in_specs,
        out_specs=jax.tree.map(lambda a: out_specs, outs),
        compiler_params=pltpu.CompilerParams(vmem_limit_bytes=limit * 2**20),
        cost_estimate=pl.CostEstimate(flops=1, bytes_accessed=1, transcendentals=0),
        **kwargs,
    )(*operands)


def at(g, arrays):
    place = pltpu.VMEM if g == len(GROUPS) - 1 else pltpu.HBM
    return [pltpu.with_memory_space_constraint(a, place) for a in arrays]


def kept_close(arrays):
    return [pltpu.with_memory_space_constraint(a, pltpu.VMEM) for a in arrays]


def space(g):
    return pltpu.VMEM


def f32_shape(*shape):
    return jax.ShapeDtypeStruct(shape, F32)


def group_shape(g):
    return space(g)((GROUPS[g] * (PLANES + 1), NG, 128), F32)


def packed(orbitals, g):
    count = GROUPS[g] * PLANES

    def kernel(orbitals, out, block, arrived):
        copy = pltpu.make_async_copy(
            orbitals.at[0, pl.ds(FIRST[g] * PLANES, count)], block, arrived
        )
        copy.start()
        copy.wait()
        for c in range(GROUPS[g]):
            base = c * (PLANES + 1)
            planes = range(c * PLANES, (c + 1) * PLANES)
            for j, z in enumerate(planes):
                out[base + j] = block[z, :, :128]
            out[base + PLANES] = jnp.concatenate([block[z, :, 128:] for z in planes], axis=1)

    return call(
        kernel,
        f"pack_{g}",
        [pltpu.with_memory_space_constraint(orbitals, pltpu.HBM)],
        group_shape(g),
        [HBM],
        scratch_shapes=[pltpu.VMEM((count, NG, NG), F32), pltpu.SemaphoreType.DMA],
    )


def strip():
    return lax.broadcasted_iota(jnp.int32, (NG, 128), 1) // (128 // PLANES)


def to_tiles(plane):
    rest = plane[:, 128:]
    moved = rest[:40]
    for g in range(1, 4):
        moved = moved + pltpu.roll(rest[40 * g : 40 * g + 40], 32 * g, 1)
    return plane[:, :128].reshape(-1, 8, 128), moved.reshape(-1, 8, 128)


def from_tiles(tiles):
    main = jnp.concatenate(tiles[:20], axis=0)
    rest = jnp.concatenate(tiles[20:], axis=0)
    lane = lax.broadcasted_iota(jnp.int32, rest.shape, 1)
    parts = [rest] + [pltpu.roll(rest, 128 - 32 * g, 1) for g in range(1, 4)]
    rest = jnp.concatenate([jnp.where(lane < 32, part, 0.0) for part in parts], axis=0)
    return jnp.concatenate([main, rest], axis=1)


def transformed(g, core, own, swap, vis, state, t):
    first, last = g == 0, g == len(GROUPS) - 1

    def kernel(*refs):
        core, own, swap, vis, table, hartley, ratio, powers = refs[:8]
        refs = refs[8:]
        if not first:
            right0, left0, zero0 = refs[:3]
            refs = refs[3:]
        fields, *results = refs
        second = core[0] == 1
        h, r, x_table, owner = hartley[...], ratio[...], table[...], strip()
        row = lax.broadcasted_iota(jnp.int32, (8, 128), 0)
        lane = lax.broadcasted_iota(jnp.int32, (8, 128), 1)
        means = jnp.zeros((8, 128), F32) if first else zero0[...]
        rights = [None if first else right0[pair] for pair in range(2)]
        lefts = [None if first else left0[pair] for pair in range(2)]
        for c in range(GROUPS[g]):
            start = c * (PLANES + 1)
            densities = []
            for p in range(start, start + PLANES + 1):
                other = jnp.where(second, vis[p], own[p])
                densities.append((own[p] * vis[p], other * swap[p]))
            for j in range(PLANES):
                wide = [
                    jnp.concatenate([densities[j][pair], jnp.where(owner == j, densities[PLANES][pair], 0.0)], axis=1)
                    for pair in range(2)
                ]
                along_x = times_table(jnp.concatenate(wide, axis=0), x_table)
                z = PLANES * c + j
                for pair in range(2):
                    field = table_times(h, along_x[NG * pair : NG * (pair + 1)])
                    fields[pair, z] = field
                    rights[pair] = field if rights[pair] is None else r * rights[pair] + field
                    here = (row == pair) & (lane == PLANES * FIRST[g] + z)
                    means = jnp.where(here, jnp.broadcast_to(field[:1, :1], (8, 128)), means)
            for pair in range(2):
                back = fields[pair, PLANES * c + PLANES - 1]
                for j in reversed(range(PLANES - 1)):
                    back = r * back + fields[pair, PLANES * c + j]
                lefts[pair] = back if lefts[pair] is None else lefts[pair] + powers[FIRST[g] + c] * back
        if not last:
            right, left, zero = results
            for pair in range(2):
                right[pair] = rights[pair]
                left[pair] = lefts[pair]
            zero[...] = means
            return
        (out,) = results
        for number, plane in enumerate(rights + lefts):
            main, rest = to_tiles(plane)
            for i in range(MODE_TILES):
                tile = main[i] if i < 20 else rest[i - 20]
                to, slot = divmod(MODE_TILES * number + i, SEND_TILES)
                out[to, slot] = tile
        for i in range(4 * MODE_TILES, SLABS * SEND_TILES):
            out[i // SEND_TILES, i % SEND_TILES] = jnp.zeros((8, 128), F32)
        for to in range(SLABS):
            out[to, SEND_TILES] = means

    outs = [space(g)((2, GROUPS[g] * PLANES, NG, WIDE), F32)]
    if last:
        outs += [f32_shape(SLABS, SEND_TILES + 1, 8, 128)]
    else:
        outs += [space(g + 1)((2, NG, WIDE), F32)] * 2 + [f32_shape(8, 128)]
    operands = [core, *kept_close([own]), *at(g, [swap, vis])]
    operands += kept_close([t["forward"], t["hartley"], t["ratio"], t["powers"]])
    if not first:
        operands += [*kept_close(state[:2]), state[2]]
    field, *state = call(
        kernel, f"forward_{g}", operands, outs, [SMEM] + [VMEM] * (len(operands) - 1)
    )
    return field, (state[0] if last else state)


def solved(slab, moments, t):
    def kernel(slab, moments, jumps, wraps, table, out, mean, jump, wrap, arrived):
        me = slab[0]
        mine = pl.ds(me * SEND_TILES, SEND_TILES)
        copies = [
            pltpu.make_async_copy(jumps.at[mine], jump, arrived.at[0]),
            pltpu.make_async_copy(wraps.at[mine], wrap, arrived.at[1]),
        ]
        for copy in copies:
            copy.start()
        for pair in range(2):
            total = jnp.zeros((24, 128), F32)
            for p in range(SLABS):
                apart = lax.rem(me - p + SLABS, SLABS)
                total = total + table[apart] * moments[p, SEND_TILES, pair : pair + 1, :]
            mean[pair] = jnp.broadcast_to(jnp.sum(total, axis=1, keepdims=True), (24, 128))
        for copy in copies:
            copy.wait()
        for slot in range(SEND_TILES):
            leftward = me * SEND_TILES + slot >= 2 * MODE_TILES
            place = lambda p: jnp.where(leftward, SLABS - 1 - p, p)
            values = [moments[place(p), slot] for p in range(SLABS)]
            r = jump[slot]
            run = values[0]
            for p in range(1, SLABS):
                run = run * r + values[p]
            run = run * wrap[slot]
            for p in range(SLABS):
                out[place(p), slot] = run
                run = values[p] + r * run

    tables = [pltpu.with_memory_space_constraint(t[name], pltpu.HBM) for name in ("jump", "wrap")]
    return call(
        kernel,
        "solve",
        [slab, moments, *tables, t["zero"]],
        [f32_shape(SLABS, SEND_TILES, 8, 128), f32_shape(2, 24, 128)],
        [SMEM, VMEM, HBM, HBM, VMEM],
        scratch_shapes=[pltpu.VMEM((SEND_TILES, 8, 128), F32)] * 2 + [pltpu.SemaphoreType.DMA((2,))],
    )


def products(g, core, own, swap, vis, field, before, coming, mean, state, t):
    first, whole = state is None, before is not None

    def kernel(core, own, swap, vis, fields, mean, edge, ratio, scale, table, hartley, *refs):
        if whole:
            before = refs[0]
            refs = refs[1:]
        if first:
            tiles = [[refs[0][divmod(MODE_TILES * n + i, SEND_TILES)] for i in range(MODE_TILES)] for n in range(4)]
            edges = [from_tiles(list_) for list_ in tiles]
            refs = refs[1:]
        else:
            edges = [refs[n // 2][n % 2] for n in range(4)]
            refs = refs[2:]
        sent, crossed, kept, right, left = refs
        rights, lefts = edges[:2], edges[2:]
        second = core[0] == 1
        h, r, c, x_table, owner = hartley[...], ratio[...], scale[...], table[...], strip()
        row = lax.broadcasted_iota(jnp.int32, (NG, WIDE), 0)
        lane = lax.broadcasted_iota(jnp.int32, (NG, WIDE), 1)
        corner = (row == 0) & (lane == 0)
        count = GROUPS[g] * PLANES
        sums = [[], []]
        for pair in range(2):
            run = before[pair] if whole else None
            for z in range(count):
                run = fields[pair, z] if run is None else r * run + fields[pair, z]
                sums[pair].append(run)
        for k in reversed(range(GROUPS[g])):
            start = k * (PLANES + 1)
            rests = [None, None]

            def share(p, x, y):
                resident, partner, visiting = own[p], swap[p], vis[p]
                extra = y * partner
                sent[p] = x * resident + jnp.where(second, extra, 0.0)
                kept[p] = x * visiting + jnp.where(second, 0.0, extra)
                crossed[p] = y * jnp.where(second, visiting, resident)

            for j in reversed(range(PLANES)):
                z = PLANES * k + j
                along_y = []
                for pair in range(2):
                    run = r * lefts[pair]
                    value = c * (sums[pair][z] + run) + edge[z] * rights[pair]
                    lefts[pair] = run + fields[pair, z]
                    middle = mean[pair, PLANES * FIRST[g] + z : PLANES * FIRST[g] + z + 1, :1]
                    value = jnp.where(corner, jnp.broadcast_to(middle, (NG, WIDE)), value)
                    along_y.append(table_times(h, value))
                both = times_table(jnp.concatenate(along_y, axis=0), x_table)
                parts = [both[:NG], both[NG:]]
                for pair in range(2):
                    rest = parts[pair][:, 128:]
                    rests[pair] = rest if rests[pair] is None else jnp.where(owner == j, rest, rests[pair])
                share(start + j, parts[0][:, :128], parts[1][:, :128])
            share(start + PLANES, *rests)
        for pair in range(2):
            right[pair] = rights[pair]
            left[pair] = lefts[pair]

    count = GROUPS[g] * PLANES
    edge = t["edge"][PLANES * FIRST[g] : PLANES * FIRST[g] + count]
    operands = [core, *kept_close([own]), *at(g, [swap, vis]), *kept_close([field]), mean]
    operands += kept_close([edge, t["ratio"], t["scale"], t["inverse"], t["hartley"]])
    if whole:
        operands += kept_close([before])
    operands += [coming] if first else kept_close(state)
    planes = space(g)((2, NG, WIDE), F32)
    sent, crossed, kept, *state = call(
        kernel,
        f"products_{g}",
        operands,
        [group_shape(g)] * 3 + [planes] * 2,
        [SMEM] + [VMEM] * (len(operands) - 1),
    )
    return sent, crossed, kept, state


def finished(g, kept, crossed, returned, result):
    def kernel(kept, crossed, returned, *refs):
        out = refs[-1]
        total = kept[...] + crossed[...] + returned[...]
        out[0, :, :, :128] = total[:PLANES]
        rest = total[PLANES]
        for j in range(PLANES):
            moved = rest if j == 0 else pltpu.roll(rest, 128 - 32 * j, 1)
            out[0, j, :, 128:] = moved[:, :32]

    block = pl.BlockSpec((PLANES + 1, NG, 128), lambda i: (i, 0, 0))
    operands = [kept, crossed, returned]
    specs = [block] * 3
    aliases = {}
    if result is not None:
        operands.append(result)
        specs.append(HBM)
        aliases = {3: 0}
    return call(
        kernel,
        f"finish_{g}",
        operands,
        pltpu.HBM((1, DEPTH, NG, NG), F32),
        specs,
        pl.BlockSpec((1, PLANES, NG, NG), lambda i: (0, FIRST[g] + i, 0, 0)),
        grid=(GROUPS[g],),
        input_output_aliases=aliases,
    )


def exchanged(array):
    flat = array.reshape(-1, 128)
    return lax.all_to_all(flat, "slab", 0, 0, tiled=True).reshape(array.shape)


def moved(name, array, pairs):
    with jax.named_scope(name):
        return lax.ppermute(array, "band", pairs)


def shards(orbitals):
    t = {name: jnp.asarray(table) for name, table in tables().items()}
    bands = lax.axis_size("band")
    core = lax.rem(lax.axis_index("band"), 2).astype(jnp.int32).reshape(1)
    slab = lax.axis_index("slab").astype(jnp.int32).reshape(1)
    outward = [(g, (g - 2) % bands if g % 2 == 0 else (g + 2) % bands) for g in range(bands)]
    homeward = [(b, a) for a, b in outward]
    across = [(g, g ^ 1) for g in range(bands)]

    groups = range(len(GROUPS))
    own = [packed(orbitals, g) for g in groups]
    vis = [moved(f"visit_{g}", own[g], outward) for g in groups]
    swap = [moved(f"swap_{g}", own[g], across) for g in groups]

    fields, befores, state = [], [], None
    for g in groups:
        befores.append(state and state[0])
        field, state = transformed(g, core, own[g], swap[g], vis[g], state, t)
        fields.append(field)
    state, slab, core = lax.optimization_barrier((state, slab, core))
    coming, mean = solved(slab, exchanged(state), t)
    coming = exchanged(coming)

    state, parts = None, []
    for g in reversed(groups):
        if len(parts) == 2:
            number, kept, crossed, returned = parts[0]
            crossed, returned, *state = lax.optimization_barrier((crossed, returned, *state))
            parts[0] = (number, kept, crossed, returned)
        sent, partner, kept, state = products(
            g, core, own[g], swap[g], vis[g], fields[g], befores[g], coming, mean, state, t
        )
        returned = moved(f"return_{g}", sent, homeward)
        crossed = moved(f"cross_{g}", partner, across)
        parts.append((g, kept, crossed, returned))
    result = None
    for part in parts:
        result = finished(*part, result)
    return result


def solution(mesh):
    spec = P("band", "slab", None, None)
    return jax.shard_map(shards, mesh=mesh, in_specs=(spec,), out_specs=spec, check_vma=False)
```

time: 158 us -> 142 us (0.90)
  local copies, waits for them, and re-layouts: 31.6 us -> 1.93 us
  blocking collectives: 0 us -> 27.5 us
  starting transfers between devices: 50.1 us -> 36 us
    unnamed x120 -> x24, local copies, waits for them, and re-layouts: 30.8 us -> 1.93 us
    all_to_all x0 -> x2, blocking collectives: none -> 27.5 us  [exchanged(): return lax.all_to_all(flat, 'slab', 0, 0, tiled=True).reshape(array.shape)]
    all_to_all x2 -> x0, starting transfers between devices: 11.2 us -> none  [the longest x1 6.54 us: shards(): moments = lax.all_to_all(moments, 'slab', 0, 0, tiled=True).reshape(shape)]
    ppermute x20 -> x12, waiting for transfers between devices: 29.8 us -> 39.2 us  [moved(): return lax.ppermute(array, 'band', pairs)]
    all_to_all x2 -> x0, waiting for transfers between devices: 8.41 us -> none  [the longest x1 8.41 us: shards(): moments = lax.all_to_all(moments, 'slab', 0, 0, tiled=True).reshape(shape)]
    ppermute x20 -> x12, starting transfers between devices: 38.9 us -> 36 us  [moved(): return lax.ppermute(array, 'band', pairs)]
    pallas_call x22 -> x13, Pallas kernels: 36.6 us -> 37 us  [call(): pl.pallas_call(kernel, name=name, out_shape=outs, in_specs=in_specs, out_...]
  transfers between devices with their start and end apart: 22 -> 12, of which waited for: 8 -> 5; matrix products, arithmetic and copies ran while one was open for 1% -> 0% of each run, Pallas kernels for 18% -> 19%
where the time goes in v2:
time: 142 us
  waiting for transfers between devices  39.2 us (28%)
  Pallas kernels  37 us (26%)
  starting transfers between devices  36 us (25%)
  blocking collectives  27.5 us (19%)
  local copies, waits for them, and re-layouts  1.93 us (1%)
    ppermute x12, waiting for transfers between devices, moved(): return lax.ppermute(array, 'band', pairs)  39.2 us
    pallas_call x13, Pallas kernels, call(): pl.pallas_call(kernel, name=name, out_shape=outs, in_specs=in_specs, out_...  37 us
    ppermute x12, starting transfers between devices, moved(): return lax.ppermute(array, 'band', pairs)  36 us
    all_to_all x2, blocking collectives, exchanged(): return lax.all_to_all(flat, 'slab', 0, 0, tiled=True).reshape(array.shape)  27.5 us
  transfers between devices with their start and end apart: 12, of which 5 were waited for; matrix products, arithmetic and copies ran while one was open for 0% of the time, Pallas kernels for 19%

profile of v2, /device:TPU:32, one launch (start us, length us, event | category | flops | bytes accessed | tf_op | source)
XLA Modules:
  0.0 141.8 jit_solution(3085263575668292066)
XLA Ops:
  0.0 1.6 %pack_0.1.refs_1_.own = f32[10,160,128]{2,1,0:T(8,128)S(1)} custom-call(f32[1,20,160,160]{3,2,1,0:T(8,128)} %orbitals.5), custom_call_target="tpu_custom_call" | custom-call | flops 1 | bytes 1 | tf_op jit(solution)/shard_map/pack_0/pallas_call | solution.py:115
  1.6 7.9 %collective-permute-start.5 = (f32[10,160,128]{2,1,0:T(8,128)S(1)}, f32[10,160,128]{2,1,0:T(8,128)S(1)}, u32[]{:S(2)}, u32[]{:S(2)}) collective-permute-start(f32[10,160,128]{2,1,0:T(8,128)S(1)} %pack_0.1.refs_1_.own), channel_id=1, source_target_pairs={{0,240},{8,24},{16,0},{24,40},{32,16},{40,56},{48,32},{56,72},{64,... | collective-permute-start | bytes 2457608 | tf_op jit(solution)/shard_map/visit_0/ppermute | solution.py:427
  9.5 1.6 %pack_1.1.refs_1_.own = f32[10,160,128]{2,1,0:T(8,128)S(1)} custom-call(f32[1,20,160,160]{3,2,1,0:T(8,128)} %orbitals.5), custom_call_target="tpu_custom_call" | custom-call | flops 1 | bytes 1 | tf_op jit(solution)/shard_map/pack_1/pallas_call | solution.py:115
  11.1 0.0 copy-start
  11.1 0.0 copy-start.1
  11.1 1.5 %collective-permute-start.3 = (f32[10,160,128]{2,1,0:T(8,128)S(1)}, f32[10,160,128]{2,1,0:T(8,128)}, u32[]{:S(2)}, u32[]{:S(2)}) collective-permute-start(f32[10,160,128]{2,1,0:T(8,128)S(1)} %pack_1.1.refs_1_.own), channel_id=1, source_target_pairs={{0,240},{8,24},{16,0},{24,40},{32,16},{40,56},{48,32},{56,72},{64,... | collective-permute-start | bytes 2457608 | tf_op jit(solution)/shard_map/visit_1/ppermute | solution.py:427
  12.6 1.2 pack_2.1.refs_1_.own
  13.9 5.1 %collective-permute-start.1 = (f32[5,160,128]{2,1,0:T(8,128)S(1)}, f32[5,160,128]{2,1,0:T(8,128)}, u32[]{:S(2)}, u32[]{:S(2)}) collective-permute-start(f32[5,160,128]{2,1,0:T(8,128)S(1)} %pack_2.1.refs_1_.own), channel_id=1, source_target_pairs={{0,240},{8,24},{16,0},{24,40},{32,16},{40,56},{48,32},{56,72},{64,... | collective-permute-start | bytes 1228808 | tf_op jit(solution)/shard_map/visit_2/ppermute | solution.py:427
  19.0 2.7 %collective-permute-done.5.refs_3_.vis = f32[10,160,128]{2,1,0:T(8,128)S(1)} collective-permute-done((f32[10,160,128]{2,1,0:T(8,128)S(1)}, f32[10,160,128]{2,1,0:T(8,128)S(1)}, u32[]{:S(2)}, u32[]{:S(2)}) %collective-permute-start.5) | collective-permute-done | bytes 819232 | tf_op jit(solution)/shard_map/visit_0/ppermute | solution.py:427
  21.7 0.9 copy-done.11
  22.6 17.5 %collective-permute-start = (f32[5,160,128]{2,1,0:T(8,128)S(1)}, f32[5,160,128]{2,1,0:T(8,128)}, u32[]{:S(2)}, u32[]{:S(2)}) collective-permute-start(f32[5,160,128]{2,1,0:T(8,128)S(1)} %pack_2.1.refs_1_.own), channel_id=1, source_target_pairs={{0,8},{8,0},{16,24},{24,16},{32,40},{40,32},{48,56},{56,48},{64,72... | collective-permute-start | bytes 1228808 | tf_op jit(solution)/shard_map/swap_2/ppermute | solution.py:427
  40.1 1.0 copy-done.4
  41.1 5.9 %forward_0.1 = (f32[2,8,160,256]{3,2,1,0:T(8,128)S(1)}, f32[2,160,256]{2,1,0:T(8,128)S(1)}, f32[2,160,256]{2,1,0:T(8,128)S(1)}, f32[8,128]{1,0:T(8,128)S(1)}) custom-call(s32[1]{0:T(128)} %bitcast.refs_0_.core, f32[10,160,128]{2,1,0:T(8,128)S(1)} %pack_0.1.refs_1_.own, f32[10,160,128]{2,1,0:T(8,128)} %collective-permute-done.4.refs_2_.swap, ...), custom_call_target="tpu_custom_call" | custom-call | flops 1 | bytes 1 | tf_op jit(solution)/shard_map/forward_0/pallas_call | solution.py:115
  47.0 5.9 %forward_1.1 = (f32[2,8,160,256]{3,2,1,0:T(8,128)S(1)}, f32[2,160,256]{2,1,0:T(8,128)S(1)}, f32[2,160,256]{2,1,0:T(8,128)S(1)}, f32[8,128]{1,0:T(8,128)S(1)}) custom-call(s32[1]{0:T(128)} %bitcast.refs_0_.core, f32[10,160,128]{2,1,0:T(8,128)S(1)} %pack_1.1.refs_1_.own, f32[10,160,128]{2,1,0:T(8,128)} %collective-permute-done.2.refs_2_.swap, ...), custom_call_target="tpu_custom_call" | custom-call | flops 1 | bytes 1 | tf_op jit(solution)/shard_map/forward_1/pallas_call | solution.py:115
  52.9 0.3 collective-permute-done.1.refs_3_.vis
  53.3 3.6 %forward_2.1 = (f32[2,4,160,256]{3,2,1,0:T(8,128)S(1)}, f32[8,14,8,128]{3,2,1,0:T(8,128)S(1)}) custom-call(s32[1]{0:T(128)} %bitcast.refs_0_.core, f32[5,160,128]{2,1,0:T(8,128)S(1)} %pack_2.1.refs_1_.own, f32[5,160,128]{2,1,0:T(8,128)} %collective-permute-done.refs_2_.swap, f32[5,160,128]{2,1,0:T(8,128)} %collective-permute-done.1.refs_3_.vis, ...), custom_call_target="tpu_custom_call" | custom-call | flops 1 | bytes 1 | tf_op jit(solution)/shard_map/forward_2/pallas_call | solution.py:115
  56.9 14.9 %all_to_all.18 = f32[8,112,128]{2,1,0:T(8,128)S(1)} all-to-all(f32[8,112,128]{2,1,0:T(8,128)S(1)} %bitcast.8), channel_id=1, replica_groups=mesh['band'=32,'slab'=8] {'slab'}, dimensions={0} | all-to-all | bytes 917504 | tf_op jit(solution)/shard_map/all_to_all | solution.py:422
  71.8 1.1 solve.1
  72.9 12.6 %all_to_all.19 = f32[8,104,128]{2,1,0:T(8,128)S(1)} all-to-all(f32[8,104,128]{2,1,0:T(8,128)S(1)} %bitcast.9), channel_id=1, replica_groups=mesh['band'=32,'slab'=8] {'slab'}, dimensions={0} | all-to-all | bytes 851968 | tf_op jit(solution)/shard_map/all_to_all | solution.py:422
  85.5 2.9 %products_2.1 = (f32[5,160,128]{2,1,0:T(8,128)S(1)}, f32[5,160,128]{2,1,0:T(8,128)S(1)}, f32[5,160,128]{2,1,0:T(8,128)S(1)}, f32[2,160,256]{2,1,0:T(8,128)S(1)}, f32[2,160,256]{2,1,0:T(8,128)S(1)}) custom-call(s32[1]{0:T(128)} %bitcast.refs_0_.core, f32[5,160,128]{2,1,0:T(8,128)S(1)} %pack_2.1.refs_1_.own, f32[5,160,128]{2,1,0:T(8,128)} %collective-permute-done.refs_2_.swap, ...), custom_call_target="tpu_custom_call" | custom-call | flops 1 | bytes 1 | tf_op jit(solution)/shard_map/products_2/pallas_call | solution.py:115
  88.4 0.1 collective-permute-start.6
  88.5 0.3 collective-permute-start.7
  88.9 4.8 %products_1.1 = (f32[10,160,128]{2,1,0:T(8,128)S(1)}, f32[10,160,128]{2,1,0:T(8,128)S(1)}, f32[10,160,128]{2,1,0:T(8,128)S(1)}, f32[2,160,256]{2,1,0:T(8,128)S(1)}, f32[2,160,256]{2,1,0:T(8,128)S(1)}) custom-call(s32[1]{0:T(128)} %bitcast.refs_0_.core, f32[10,160,128]{2,1,0:T(8,128)S(1)} %pack_1.1.refs_1_.own, ...), custom_call_target="tpu_custom_call" | custom-call | flops 1 | bytes 1 | tf_op jit(solution)/shard_map/products_1/pallas_call | solution.py:115
  93.6 3.2 %collective-permute-start.10 = (f32[10,160,128]{2,1,0:T(8,128)S(1)}, f32[10,160,128]{2,1,0:T(8,128)S(1)}, u32[]{:S(2)}, u32[]{:S(2)}) collective-permute-start(f32[10,160,128]{2,1,0:T(8,128)S(1)} %get-tuple-element.64), channel_id=1, source_target_pairs={{0,8},{8,0},{16,24},{24,16},{32,40},{40,32},{48,56},{56,48},{64,72... | collective-permute-start | bytes 2457608 | tf_op jit(solution)/shard_map/cross_1/ppermute | solution.py:427
  96.8 8.2 %collective-permute-done.7.returned = f32[5,160,128]{2,1,0:T(8,128)S(1)} collective-permute-done((f32[5,160,128]{2,1,0:T(8,128)S(1)}, f32[5,160,128]{2,1,0:T(8,128)S(1)}, u32[]{:S(2)}, u32[]{:S(2)}) %collective-permute-start.7) | collective-permute-done | bytes 409632 | tf_op jit(solution)/shard_map/return_2/ppermute | solution.py:427
  105.0 5.0 %products_0.1 = (f32[10,160,128]{2,1,0:T(8,128)S(1)}, f32[10,160,128]{2,1,0:T(8,128)S(1)}, f32[10,160,128]{2,1,0:T(8,128)S(1)}, f32[2,160,256]{2,1,0:T(8,128)}, f32[2,160,256]{2,1,0:T(8,128)}) custom-call(s32[1]{0:T(128)} %bitcast.refs_0_.core, f32[10,160,128]{2,1,0:T(8,128)S(1)} %pack_0.1.refs_1_.own, f32[10,160,128]{2,1,0:T(8,128)} %collective-permute-done.4.refs_2_.swap, ...), custom_call_target="tpu_custom_call" | custom-call | flops 1 | bytes 1 | tf_op jit(solution)/shard_map/products_0/pallas_call | solution.py:115
  110.0 0.3 collective-permute-start.8
  110.3 1.0 finish_2.1.refs_0_
  111.3 4.9 %collective-permute-done.11.returned = f32[10,160,128]{2,1,0:T(8,128)S(1)} collective-permute-done((f32[10,160,128]{2,1,0:T(8,128)S(1)}, f32[10,160,128]{2,1,0:T(8,128)S(1)}, u32[]{:S(2)}, u32[]{:S(2)}) %collective-permute-start.11) | collective-permute-done | bytes 819232 | tf_op jit(solution)/shard_map/return_1/ppermute | solution.py:427
  116.2 1.2 finish_1.1.refs_0_
  117.4 23.1 %collective-permute-done.9.returned = f32[10,160,128]{2,1,0:T(8,128)S(1)} collective-permute-done((f32[10,160,128]{2,1,0:T(8,128)S(1)}, f32[10,160,128]{2,1,0:T(8,128)S(1)}, u32[]{:S(2)}, u32[]{:S(2)}) %collective-permute-start.9) | collective-permute-done | bytes 819232 | tf_op jit(solution)/shard_map/return_0/ppermute | solution.py:427
  140.6 1.2 finish_0.1
  (31 shorter events, 0.1 us)
Async XLA Ops:
  1.6 20.1 %collective-permute-start.5 = (f32[10,160,128]{2,1,0:T(8,128)S(1)}, f32[10,160,128]{2,1,0:T(8,128)S(1)}, u32[]{:S(2)}, u32[]{:S(2)}) collective-permute-start(f32[10,160,128]{2,1,0:T(8,128)S(1)} %pack_0.1.refs_1_.own), channel_id=1, source_target_pairs={{0,240},{8,24},{16,0},{24,40},{32,16},{40,56},{48,32},{56,72},{64,... | collective-permute-start | bytes 2457608 | tf_op jit(solution)/shard_map/visit_0/ppermute | solution.py:427
  9.5 30.6 %collective-permute-start.4 = (f32[10,160,128]{2,1,0:T(8,128)S(1)}, f32[10,160,128]{2,1,0:T(8,128)}, u32[]{:S(2)}, u32[]{:S(2)}) collective-permute-start(f32[10,160,128]{2,1,0:T(8,128)S(1)} %pack_0.1.refs_1_.own), channel_id=1, source_target_pairs={{0,8},{8,0},{16,24},{24,16},{32,40},{40,32},{48,56},{56,48},{64,72... | collective-permute-start | bytes 2457608 | tf_op jit(solution)/shard_map/swap_0/ppermute | solution.py:427
  11.1 29.0 %copy-start = (f32[5,160,256]{2,1,0:T(8,128)S(1)}, f32[5,160,256]{2,1,0:T(8,128)}, u32[]{:S(2)}) copy-start(f32[5,160,256]{2,1,0:T(8,128)} %constant.39.clone.refs_7_) | copy-start | bytes 2457604
  11.1 29.0 %copy-start.1 = (f32[160,256]{1,0:T(8,128)S(1)}, f32[160,256]{1,0:T(8,128)}, u32[]{:S(2)}) copy-start(f32[160,256]{1,0:T(8,128)} %constant.37.clone.refs_6_.ratio) | copy-start | bytes 491524
  11.1 29.0 %copy-start.2 = (bf16[160,480]{1,0:T(8,128)(2,1)S(1)}, bf16[160,480]{1,0:T(8,128)(2,1)}, u32[]{:S(2)}) copy-start(bf16[160,480]{1,0:T(8,128)(2,1)} %constant.36.clone.refs_5_.hartley) | copy-start | bytes 460804
  11.1 35.9 %collective-permute-start.3 = (f32[10,160,128]{2,1,0:T(8,128)S(1)}, f32[10,160,128]{2,1,0:T(8,128)}, u32[]{:S(2)}, u32[]{:S(2)}) collective-permute-start(f32[10,160,128]{2,1,0:T(8,128)S(1)} %pack_1.1.refs_1_.own), channel_id=1, source_target_pairs={{0,240},{8,24},{16,0},{24,40},{32,16},{40,56},{48,32},{56,72},{64,... | collective-permute-start | bytes 2457608 | tf_op jit(solution)/shard_map/visit_1/ppermute | solution.py:427
  12.6 34.4 %collective-permute-start.2 = (f32[10,160,128]{2,1,0:T(8,128)S(1)}, f32[10,160,128]{2,1,0:T(8,128)}, u32[]{:S(2)}, u32[]{:S(2)}) collective-permute-start(f32[10,160,128]{2,1,0:T(8,128)S(1)} %pack_1.1.refs_1_.own), channel_id=1, source_target_pairs={{0,8},{8,0},{16,24},{24,16},{32,40},{40,32},{48,56},{56,48},{64,72... | collective-permute-start | bytes 2457608 | tf_op jit(solution)/shard_map/swap_1/ppermute | solution.py:427
  13.9 39.4 %collective-permute-start.1 = (f32[5,160,128]{2,1,0:T(8,128)S(1)}, f32[5,160,128]{2,1,0:T(8,128)}, u32[]{:S(2)}, u32[]{:S(2)}) collective-permute-start(f32[5,160,128]{2,1,0:T(8,128)S(1)} %pack_2.1.refs_1_.own), channel_id=1, source_target_pairs={{0,240},{8,24},{16,0},{24,40},{32,16},{40,56},{48,32},{56,72},{64,... | collective-permute-start | bytes 1228808 | tf_op jit(solution)/shard_map/visit_2/ppermute | solution.py:427
  21.7 0.9 copy-start.11
  22.6 30.7 %collective-permute-start = (f32[5,160,128]{2,1,0:T(8,128)S(1)}, f32[5,160,128]{2,1,0:T(8,128)}, u32[]{:S(2)}, u32[]{:S(2)}) collective-permute-start(f32[5,160,128]{2,1,0:T(8,128)S(1)} %pack_2.1.refs_1_.own), channel_id=1, source_target_pairs={{0,8},{8,0},{16,24},{24,16},{32,40},{40,32},{48,56},{56,48},{64,72... | collective-permute-start | bytes 1228808 | tf_op jit(solution)/shard_map/swap_2/ppermute | solution.py:427
  40.1 1.0 copy-start.4
  41.1 5.9 %copy-start.5 = (bf16[768,256]{1,0:T(8,128)(2,1)S(1)}, bf16[768,256]{1,0:T(8,128)(2,1)}, u32[]{:S(2)}) copy-start(bf16[768,256]{1,0:T(8,128)(2,1)} %constant.34.clone.refs_4_) | copy-start | bytes 1179652
  52.9 18.9 %copy-start.10 = (f32[8,24,128]{2,1,0:T(8,128)S(1)}, f32[8,24,128]{2,1,0:T(8,128)}, u32[]{:S(2)}) copy-start(f32[8,24,128]{2,1,0:T(8,128)} %constant.43.clone.table) | copy-start | bytes 294916
  53.3 32.2 %copy-start.3 = (bf16[768,256]{1,0:T(8,128)(2,1)S(1)}, bf16[768,256]{1,0:T(8,128)(2,1)}, u32[]{:S(2)}) copy-start(bf16[768,256]{1,0:T(8,128)(2,1)} %constant.35.clone.table) | copy-start | bytes 1179652
  53.3 32.2 %copy-start.6 = (f32[160,256]{1,0:T(8,128)S(1)}, f32[160,256]{1,0:T(8,128)}, u32[]{:S(2)}) copy-start(f32[160,256]{1,0:T(8,128)} %constant.38.clone.scale) | copy-start | bytes 491524
  53.3 32.2 %copy-start.9 = (f32[4,160,256]{2,1,0:T(8,128)S(1)}, f32[4,160,256]{2,1,0:T(8,128)}, u32[]{:S(2)}) copy-start(f32[4,160,256]{2,1,0:T(8,128)} %constant.46.edge) | copy-start | bytes 1966084
  85.5 3.3 %copy-start.8 = (f32[8,160,256]{2,1,0:T(8,128)S(1)}, f32[8,160,256]{2,1,0:T(8,128)}, u32[]{:S(2)}) copy-start(f32[8,160,256]{2,1,0:T(8,128)} %constant.47.edge) | copy-start | bytes 3932164
  88.4 8.4 %collective-permute-start.6 = (f32[5,160,128]{2,1,0:T(8,128)S(1)}, f32[5,160,128]{2,1,0:T(8,128)S(1)}, u32[]{:S(2)}, u32[]{:S(2)}) collective-permute-start(f32[5,160,128]{2,1,0:T(8,128)S(1)} %get-tuple-element.51), channel_id=1, source_target_pairs={{0,8},{8,0},{16,24},{24,16},{32,40},{40,32},{48,56},{56,48},{64,72... | collective-permute-start | bytes 1228808 | tf_op jit(solution)/shard_map/cross_2/ppermute | solution.py:427
  88.5 16.5 %collective-permute-start.7 = (f32[5,160,128]{2,1,0:T(8,128)S(1)}, f32[5,160,128]{2,1,0:T(8,128)S(1)}, u32[]{:S(2)}, u32[]{:S(2)}) collective-permute-start(f32[5,160,128]{2,1,0:T(8,128)S(1)} %get-tuple-element.52), channel_id=1, source_target_pairs={{240,0},{24,8},{0,16},{40,24},{16,32},{56,40},{32,48},{72,56},{48,... | collective-permute-start | bytes 1228808 | tf_op jit(solution)/shard_map/return_2/ppermute | solution.py:427
  88.8 16.2 %copy-start.7 = (f32[8,160,256]{2,1,0:T(8,128)S(1)}, f32[8,160,256]{2,1,0:T(8,128)}, u32[]{:S(2)}) copy-start(f32[8,160,256]{2,1,0:T(8,128)} %constant.45.edge) | copy-start | bytes 3932164
  93.6 17.7 %collective-permute-start.10 = (f32[10,160,128]{2,1,0:T(8,128)S(1)}, f32[10,160,128]{2,1,0:T(8,128)S(1)}, u32[]{:S(2)}, u32[]{:S(2)}) collective-permute-start(f32[10,160,128]{2,1,0:T(8,128)S(1)} %get-tuple-element.64), channel_id=1, source_target_pairs={{0,8},{8,0},{16,24},{24,16},{32,40},{40,32},{48,56},{56,48},{64,72... | collective-permute-start | bytes 2457608 | tf_op jit(solution)/shard_map/cross_1/ppermute | solution.py:427
  96.8 19.4 %collective-permute-start.11 = (f32[10,160,128]{2,1,0:T(8,128)S(1)}, f32[10,160,128]{2,1,0:T(8,128)S(1)}, u32[]{:S(2)}, u32[]{:S(2)}) collective-permute-start(f32[10,160,128]{2,1,0:T(8,128)S(1)} %get-tuple-element.65), channel_id=1, source_target_pairs={{240,0},{24,8},{0,16},{40,24},{16,32},{56,40},{32,48},{72,56},{48,... | collective-permute-start | bytes 2457608 | tf_op jit(solution)/shard_map/return_1/ppermute | solution.py:427
  110.0 7.4 %collective-permute-start.8 = (f32[10,160,128]{2,1,0:T(8,128)S(1)}, f32[10,160,128]{2,1,0:T(8,128)S(1)}, u32[]{:S(2)}, u32[]{:S(2)}) collective-permute-start(f32[10,160,128]{2,1,0:T(8,128)S(1)} %get-tuple-element.61), channel_id=1, source_target_pairs={{0,8},{8,0},{16,24},{24,16},{32,40},{40,32},{48,56},{56,48},{64,72... | collective-permute-start | bytes 2457608 | tf_op jit(solution)/shard_map/cross_0/ppermute | solution.py:427
  110.3 30.3 %collective-permute-start.9 = (f32[10,160,128]{2,1,0:T(8,128)S(1)}, f32[10,160,128]{2,1,0:T(8,128)S(1)}, u32[]{:S(2)}, u32[]{:S(2)}) collective-permute-start(f32[10,160,128]{2,1,0:T(8,128)S(1)} %get-tuple-element.62), channel_id=1, source_target_pairs={{240,0},{24,8},{0,16},{40,24},{16,32},{56,40},{32,48},{72,56},{48,... | collective-permute-start | bytes 2457608 | tf_op jit(solution)/shard_map/return_0/ppermute | solution.py:427

commit v3 on v2

--- a/solution.py
+++ b/solution.py
@@ -145,29 +145,47 @@
     return space(g)((GROUPS[g] * (PLANES + 1), NG, 128), F32)
 
 
+def own_shape(g):
+    return group_shape(g) if g == 2 else pltpu.HBM((GROUPS[g] * (PLANES + 1), NG, 128), F32)
+
+
 def packed(orbitals, g):
-    count = GROUPS[g] * PLANES
-
-    def kernel(orbitals, out, block, arrived):
-        copy = pltpu.make_async_copy(
-            orbitals.at[0, pl.ds(FIRST[g] * PLANES, count)], block, arrived
-        )
-        copy.start()
-        copy.wait()
-        for c in range(GROUPS[g]):
+    count = GROUPS[g]
+    close = g == len(GROUPS) - 1
+
+    def kernel(orbitals, out, block, *refs):
+        ready, (arrived, gone) = (out, refs) if close else (refs[0], refs[1:])
+        comes, goes = [], []
+        for c in range(count):
+            there = pl.ds((FIRST[g] + c) * PLANES, PLANES)
+            here = pl.ds(c * PLANES, PLANES)
+            comes.append(pltpu.make_async_copy(orbitals.at[0, there], block.at[here], arrived.at[c]))
+            comes[c].start()
+        for c in range(count):
+            comes[c].wait()
             base = c * (PLANES + 1)
             planes = range(c * PLANES, (c + 1) * PLANES)
             for j, z in enumerate(planes):
-                out[base + j] = block[z, :, :128]
-            out[base + PLANES] = jnp.concatenate([block[z, :, 128:] for z in planes], axis=1)
-
+                ready[base + j] = block[z, :, :128]
+            ready[base + PLANES] = jnp.concatenate([block[z, :, 128:] for z in planes], axis=1)
+            if not close:
+                part = pl.ds(base, PLANES + 1)
+                goes.append(pltpu.make_async_copy(ready.at[part], out.at[part], gone.at[c]))
+                goes[c].start()
+        for copy in goes:
+            copy.wait()
+
+    scratch = [pltpu.VMEM((count * PLANES, NG, NG), F32)]
+    if not close:
+        scratch.append(pltpu.VMEM(group_shape(g).shape, F32))
     return call(
         kernel,
         f"pack_{g}",
         [pltpu.with_memory_space_constraint(orbitals, pltpu.HBM)],
-        group_shape(g),
+        own_shape(g),
         [HBM],
-        scratch_shapes=[pltpu.VMEM((count, NG, NG), F32), pltpu.SemaphoreType.DMA],
+        VMEM if close else HBM,
+        scratch_shapes=scratch + [pltpu.SemaphoreType.DMA((count,))] * 2,
     )
 
 
@@ -257,7 +275,7 @@
         outs += [f32_shape(SLABS, SEND_TILES + 1, 8, 128)]
     else:
         outs += [space(g + 1)((2, NG, WIDE), F32)] * 2 + [f32_shape(8, 128)]
-    operands = [core, *kept_close([own]), *at(g, [swap, vis])]
+    operands = [core, *at(g, [own]), *at(g, [swap, vis])]
     operands += kept_close([t["forward"], t["hartley"], t["ratio"], t["powers"]])
     if not first:
         operands += [*kept_close(state[:2]), state[2]]
@@ -267,45 +285,57 @@
     return field, (state[0] if last else state)
 
 
-def solved(slab, moments, t):
-    def kernel(slab, moments, jumps, wraps, table, out, mean, jump, wrap, arrived):
-        me = slab[0]
-        mine = pl.ds(me * SEND_TILES, SEND_TILES)
+def picked(slab, t):
+    def kernel(slab, jumps, wraps, out, arrived):
+        mine = pl.ds(slab[0] * SEND_TILES, SEND_TILES)
         copies = [
-            pltpu.make_async_copy(jumps.at[mine], jump, arrived.at[0]),
-            pltpu.make_async_copy(wraps.at[mine], wrap, arrived.at[1]),
+            pltpu.make_async_copy(table.at[mine], out.at[i], arrived.at[i])
+            for i, table in enumerate((jumps, wraps))
         ]
         for copy in copies:
             copy.start()
+        for copy in copies:
+            copy.wait()
+
+    tables = [pltpu.with_memory_space_constraint(t[name], pltpu.HBM) for name in ("jump", "wrap")]
+    return call(
+        kernel,
+        "pick",
+        [slab, *tables],
+        pltpu.VMEM((2, SEND_TILES, 8, 128), F32),
+        [SMEM, HBM, HBM],
+        scratch_shapes=[pltpu.SemaphoreType.DMA((2,))],
+    )
+
+
+def solved(slab, moments, tables, t):
+    def kernel(slab, moments, tables, zero, out, mean):
+        me = slab[0]
+        for slot in range(SEND_TILES):
+            leftward = me * SEND_TILES + slot >= 2 * MODE_TILES
+            place = lambda p: jnp.where(leftward, SLABS - 1 - p, p)
+            values = [moments[place(p), slot] for p in range(SLABS)]
+            r = tables[0, slot]
+            run = values[0]
+            for p in range(1, SLABS):
+                run = run * r + values[p]
+            run = run * tables[1, slot]
+            for p in range(SLABS):
+                out[place(p), slot] = run
+                run = values[p] + r * run
         for pair in range(2):
             total = jnp.zeros((24, 128), F32)
             for p in range(SLABS):
                 apart = lax.rem(me - p + SLABS, SLABS)
-                total = total + table[apart] * moments[p, SEND_TILES, pair : pair + 1, :]
+                total = total + zero[apart] * moments[p, SEND_TILES, pair : pair + 1, :]
             mean[pair] = jnp.broadcast_to(jnp.sum(total, axis=1, keepdims=True), (24, 128))
-        for copy in copies:
-            copy.wait()
-        for slot in range(SEND_TILES):
-            leftward = me * SEND_TILES + slot >= 2 * MODE_TILES
-            place = lambda p: jnp.where(leftward, SLABS - 1 - p, p)
-            values = [moments[place(p), slot] for p in range(SLABS)]
-            r = jump[slot]
-            run = values[0]
-            for p in range(1, SLABS):
-                run = run * r + values[p]
-            run = run * wrap[slot]
-            for p in range(SLABS):
-                out[place(p), slot] = run
-                run = values[p] + r * run
-
-    tables = [pltpu.with_memory_space_constraint(t[name], pltpu.HBM) for name in ("jump", "wrap")]
+
     return call(
         kernel,
         "solve",
-        [slab, moments, *tables, t["zero"]],
+        [slab, moments, *kept_close([tables, t["zero"]])],
         [f32_shape(SLABS, SEND_TILES, 8, 128), f32_shape(2, 24, 128)],
-        [SMEM, VMEM, HBM, HBM, VMEM],
-        scratch_shapes=[pltpu.VMEM((SEND_TILES, 8, 128), F32)] * 2 + [pltpu.SemaphoreType.DMA((2,))],
+        [SMEM, VMEM, VMEM, VMEM],
     )
 
 
@@ -371,7 +401,7 @@
 
     count = GROUPS[g] * PLANES
     edge = t["edge"][PLANES * FIRST[g] : PLANES * FIRST[g] + count]
-    operands = [core, *kept_close([own]), *at(g, [swap, vis]), *kept_close([field]), mean]
+    operands = [core, *at(g, [own]), *at(g, [swap, vis]), *kept_close([field]), mean]
     operands += kept_close([edge, t["ratio"], t["scale"], t["inverse"], t["hartley"]])
     if whole:
         operands += kept_close([before])
@@ -446,26 +476,31 @@
         befores.append(state and state[0])
         field, state = transformed(g, core, own[g], swap[g], vis[g], state, t)
         fields.append(field)
-    state, slab, core = lax.optimization_barrier((state, slab, core))
-    coming, mean = solved(slab, exchanged(state), t)
+    state, slab, core, mine = lax.optimization_barrier((state, slab, core, picked(slab, t)))
+    coming, mean = solved(slab, exchanged(state), mine, t)
     coming = exchanged(coming)
 
-    state, parts = None, []
-    for g in reversed(groups):
-        if len(parts) == 2:
-            number, kept, crossed, returned = parts[0]
-            crossed, returned, *state = lax.optimization_barrier((crossed, returned, *state))
-            parts[0] = (number, kept, crossed, returned)
-        sent, partner, kept, state = products(
-            g, core, own[g], swap[g], vis[g], fields[g], befores[g], coming, mean, state, t
-        )
-        returned = moved(f"return_{g}", sent, homeward)
-        crossed = moved(f"cross_{g}", partner, across)
-        parts.append((g, kept, crossed, returned))
-    result = None
-    for part in parts:
-        result = finished(*part, result)
-    return result
+    def at_group(g, state):
+        return products(g, core, own[g], swap[g], vis[g], fields[g], befores[g], coming, mean, state, t)
+
+    def home(g, part):
+        return moved(f"return_{g}", part, homeward)
+
+    def cross(g, part):
+        return moved(f"cross_{g}", part, across)
+
+    sent, partner_2, kept_2, state = at_group(2, None)
+    returned_2 = home(2, sent)
+    sent, partner, kept_1, state = at_group(1, state)
+    partner_2, partner = lax.optimization_barrier((partner_2, partner))
+    returned_1 = home(1, sent)
+    crossed_2, crossed_1 = cross(2, partner_2), cross(1, partner)
+    returned_2, *state = lax.optimization_barrier((returned_2, *state))
+    sent, partner, kept_0, state = at_group(0, state)
+    returned_0, crossed_0 = home(0, sent), cross(0, partner)
+    result = finished(2, kept_2, crossed_2, returned_2, None)
+    result = finished(1, kept_1, crossed_1, returned_1, result)
+    return finished(0, kept_0, crossed_0, returned_0, result)
 
 
 def solution(mesh):

time: 142 us -> 139 us (0.979)
  waiting for transfers between devices: 39.2 us -> 41.5 us
  local copies, waits for them, and re-layouts: 1.93 us -> 0.06 us
  starting transfers between devices: 36 us -> 34.3 us
  Pallas kernels: 37 us -> 35.5 us
    ppermute x12, waiting for transfers between devices: 39.2 us -> 41.5 us  [moved(): return lax.ppermute(array, 'band', pairs)]
    unnamed x24 -> x20, local copies, waits for them, and re-layouts: 1.93 us -> 0.06 us
    ppermute x12, starting transfers between devices: 36 us -> 34.3 us  [moved(): return lax.ppermute(array, 'band', pairs)]
    pallas_call x13 -> x14, Pallas kernels: 37 us -> 35.5 us  [call(): pl.pallas_call(kernel, name=name, out_shape=outs, in_specs=in_specs, out_...]
  transfers between devices with their start and end apart: 12 -> 12, of which waited for: 5 -> 6; matrix products, arithmetic and copies ran while one was open for 0% -> 0% of each run, Pallas kernels for 19% -> 20%
where the time goes in v3:
time: 139 us
  waiting for transfers between devices  41.5 us (30%)
  Pallas kernels  35.5 us (26%)
  starting transfers between devices  34.3 us (25%)
  blocking collectives  27.5 us (20%)
    ppermute x12, waiting for transfers between devices, moved(): return lax.ppermute(array, 'band', pairs)  41.5 us
    pallas_call x14, Pallas kernels, call(): pl.pallas_call(kernel, name=name, out_shape=outs, in_specs=in_specs, out_...  35.5 us
    ppermute x12, starting transfers between devices, moved(): return lax.ppermute(array, 'band', pairs)  34.3 us
    all_to_all x2, blocking collectives, exchanged(): return lax.all_to_all(flat, 'slab', 0, 0, tiled=True).reshape(array.shape)  27.5 us
  transfers between devices with their start and end apart: 12, of which 6 were waited for; matrix products, arithmetic and copies ran while one was open for 0% of the time, Pallas kernels for 20%

profile of v3, /device:TPU:32, one launch (start us, length us, event | category | flops | bytes accessed | tf_op | source)
XLA Modules:
  0.0 139.1 jit_solution(3632463215638937701)
XLA Ops:
  0.0 2.2 %pack_0.1.refs_1_.own = f32[10,160,128]{2,1,0:T(8,128)} custom-call(f32[1,20,160,160]{3,2,1,0:T(8,128)} %orbitals.5), custom_call_target="tpu_custom_call" | custom-call | flops 1 | bytes 1 | tf_op jit(solution)/shard_map/pack_0/pallas_call | solution.py:115
  2.2 7.9 %collective-permute-start.5 = (f32[10,160,128]{2,1,0:T(8,128)}, f32[10,160,128]{2,1,0:T(8,128)}, u32[]{:S(2)}, u32[]{:S(2)}) collective-permute-start(f32[10,160,128]{2,1,0:T(8,128)} %pack_0.1.refs_1_.own), channel_id=1, source_target_pairs={{0,240},{8,24},{16,0},{24,40},{32,16},{40,56},{48,32},{56,72},{64,... | collective-permute-start | bytes 2457608 | tf_op jit(solution)/shard_map/visit_0/ppermute | solution.py:457
  10.1 2.2 %pack_1.1.refs_1_.own = f32[10,160,128]{2,1,0:T(8,128)} custom-call(f32[1,20,160,160]{3,2,1,0:T(8,128)} %orbitals.5), custom_call_target="tpu_custom_call" | custom-call | flops 1 | bytes 1 | tf_op jit(solution)/shard_map/pack_1/pallas_call | solution.py:115
  12.3 0.0 copy-start
  12.4 0.0 copy-start.1
  12.4 1.5 %collective-permute-start.3 = (f32[10,160,128]{2,1,0:T(8,128)}, f32[10,160,128]{2,1,0:T(8,128)}, u32[]{:S(2)}, u32[]{:S(2)}) collective-permute-start(f32[10,160,128]{2,1,0:T(8,128)} %pack_1.1.refs_1_.own), channel_id=1, source_target_pairs={{0,240},{8,24},{16,0},{24,40},{32,16},{40,56},{48,32},{56,72},{64,... | collective-permute-start | bytes 2457608 | tf_op jit(solution)/shard_map/visit_1/ppermute | solution.py:457
  13.9 1.3 pack_2.1.refs_1_.own
  15.2 5.1 %collective-permute-start.1 = (f32[5,160,128]{2,1,0:T(8,128)S(1)}, f32[5,160,128]{2,1,0:T(8,128)S(1)}, u32[]{:S(2)}, u32[]{:S(2)}) collective-permute-start(f32[5,160,128]{2,1,0:T(8,128)S(1)} %pack_2.1.refs_1_.own), channel_id=1, source_target_pairs={{0,240},{8,24},{16,0},{24,40},{32,16},{40,56},{48,32},{56,72},{64,... | collective-permute-start | bytes 1228808 | tf_op jit(solution)/shard_map/visit_2/ppermute | solution.py:457
  20.3 2.3 %collective-permute-done.5.refs_3_.vis = f32[10,160,128]{2,1,0:T(8,128)} collective-permute-done((f32[10,160,128]{2,1,0:T(8,128)}, f32[10,160,128]{2,1,0:T(8,128)}, u32[]{:S(2)}, u32[]{:S(2)}) %collective-permute-start.5) | collective-permute-done | bytes 819232 | tf_op jit(solution)/shard_map/visit_0/ppermute | solution.py:457
  22.6 17.5 %collective-permute-start = (f32[5,160,128]{2,1,0:T(8,128)S(1)}, f32[5,160,128]{2,1,0:T(8,128)S(1)}, u32[]{:S(2)}, u32[]{:S(2)}) collective-permute-start(f32[5,160,128]{2,1,0:T(8,128)S(1)} %pack_2.1.refs_1_.own), channel_id=1, source_target_pairs={{0,8},{8,0},{16,24},{24,16},{32,40},{40,32},{48,56},{56,48},{64,72... | collective-permute-start | bytes 1228808 | tf_op jit(solution)/shard_map/swap_2/ppermute | solution.py:457
  40.1 0.9 pick.1.tables
  41.1 6.0 %forward_0.1 = (f32[2,8,160,256]{3,2,1,0:T(8,128)S(1)}, f32[2,160,256]{2,1,0:T(8,128)S(1)}, f32[2,160,256]{2,1,0:T(8,128)S(1)}, f32[8,128]{1,0:T(8,128)S(1)}) custom-call(s32[1]{0:T(128)} %bitcast.refs_0_.core, f32[10,160,128]{2,1,0:T(8,128)} %pack_0.1.refs_1_.own, f32[10,160,128]{2,1,0:T(8,128)} %collective-permute-done.4.refs_2_.swap, ...), custom_call_target="tpu_custom_call" | custom-call | flops 1 | bytes 1 | tf_op jit(solution)/shard_map/forward_0/pallas_call | solution.py:115
  47.1 6.0 %forward_1.1 = (f32[2,8,160,256]{3,2,1,0:T(8,128)S(1)}, f32[2,160,256]{2,1,0:T(8,128)S(1)}, f32[2,160,256]{2,1,0:T(8,128)S(1)}, f32[8,128]{1,0:T(8,128)S(1)}) custom-call(s32[1]{0:T(128)} %bitcast.refs_0_.core, f32[10,160,128]{2,1,0:T(8,128)} %pack_1.1.refs_1_.own, f32[10,160,128]{2,1,0:T(8,128)} %collective-permute-done.2.refs_2_.swap, ...), custom_call_target="tpu_custom_call" | custom-call | flops 1 | bytes 1 | tf_op jit(solution)/shard_map/forward_1/pallas_call | solution.py:115
  53.2 0.9 collective-permute-done.1.refs_3_.vis
  54.1 2.3 %forward_2.1 = (f32[2,4,160,256]{3,2,1,0:T(8,128)S(1)}, f32[8,14,8,128]{3,2,1,0:T(8,128)S(1)}) custom-call(s32[1]{0:T(128)} %bitcast.refs_0_.core, f32[5,160,128]{2,1,0:T(8,128)S(1)} %pack_2.1.refs_1_.own, f32[5,160,128]{2,1,0:T(8,128)S(1)} %collective-permute-done.refs_2_.swap, f32[5,160,128]{2,1,0:T(8,128)S(1)} %collective-permute-done.1.refs_3_.vis, ...), custom_call_target="tpu_custom_call" | custom-call | flops 1 | bytes 1 | tf_op jit(solution)/shard_map/forward_2/pallas_call | solution.py:115
  56.4 14.7 %all_to_all.18 = f32[8,112,128]{2,1,0:T(8,128)S(1)} all-to-all(f32[8,112,128]{2,1,0:T(8,128)S(1)} %bitcast.8), channel_id=1, replica_groups=mesh['band'=32,'slab'=8] {'slab'}, dimensions={0} | all-to-all | bytes 917504 | tf_op jit(solution)/shard_map/all_to_all | solution.py:452
  71.2 0.2 solve.1
  71.4 12.8 %all_to_all.19 = f32[8,104,128]{2,1,0:T(8,128)S(1)} all-to-all(f32[8,104,128]{2,1,0:T(8,128)S(1)} %bitcast.9), channel_id=1, replica_groups=mesh['band'=32,'slab'=8] {'slab'}, dimensions={0} | all-to-all | bytes 851968 | tf_op jit(solution)/shard_map/all_to_all | solution.py:452
  84.2 1.5 %products_2.1 = (f32[5,160,128]{2,1,0:T(8,128)S(1)}, f32[5,160,128]{2,1,0:T(8,128)S(1)}, f32[5,160,128]{2,1,0:T(8,128)S(1)}, f32[2,160,256]{2,1,0:T(8,128)S(1)}, f32[2,160,256]{2,1,0:T(8,128)S(1)}) custom-call(s32[1]{0:T(128)} %bitcast.refs_0_.core, f32[5,160,128]{2,1,0:T(8,128)S(1)} %pack_2.1.refs_1_.own, ...), custom_call_target="tpu_custom_call" | custom-call | flops 1 | bytes 1 | tf_op jit(solution)/shard_map/products_2/pallas_call | solution.py:115
  85.7 0.3 collective-permute-start.6
  86.1 4.7 %products_1.1 = (f32[10,160,128]{2,1,0:T(8,128)S(1)}, f32[10,160,128]{2,1,0:T(8,128)S(1)}, f32[10,160,128]{2,1,0:T(8,128)S(1)}, f32[2,160,256]{2,1,0:T(8,128)S(1)}, f32[2,160,256]{2,1,0:T(8,128)S(1)}) custom-call(s32[1]{0:T(128)} %bitcast.refs_0_.core, f32[10,160,128]{2,1,0:T(8,128)} %pack_1.1.refs_1_.own, ...), custom_call_target="tpu_custom_call" | custom-call | flops 1 | bytes 1 | tf_op jit(solution)/shard_map/products_1/pallas_call | solution.py:115
  90.7 0.1 collective-permute-start.9
  90.8 1.3 collective-permute-start.10
  92.1 10.3 %collective-permute-done.6.returned = f32[5,160,128]{2,1,0:T(8,128)S(1)} collective-permute-done((f32[5,160,128]{2,1,0:T(8,128)S(1)}, f32[5,160,128]{2,1,0:T(8,128)S(1)}, u32[]{:S(2)}, u32[]{:S(2)}) %collective-permute-start.6) | collective-permute-done | bytes 409632 | tf_op jit(solution)/shard_map/return_2/ppermute | solution.py:457
  102.5 4.8 %products_0.1 = (f32[10,160,128]{2,1,0:T(8,128)S(1)}, f32[10,160,128]{2,1,0:T(8,128)S(1)}, f32[10,160,128]{2,1,0:T(8,128)S(1)}, f32[2,160,256]{2,1,0:T(8,128)}, f32[2,160,256]{2,1,0:T(8,128)}) custom-call(s32[1]{0:T(128)} %bitcast.refs_0_.core, f32[10,160,128]{2,1,0:T(8,128)} %pack_0.1.refs_1_.own, f32[10,160,128]{2,1,0:T(8,128)} %collective-permute-done.4.refs_2_.swap, ...), custom_call_target="tpu_custom_call" | custom-call | flops 1 | bytes 1 | tf_op jit(solution)/shard_map/products_0/pallas_call | solution.py:115
  107.2 0.5 collective-permute-start.11
  107.8 2.4 %collective-permute-done.11.crossed = f32[5,160,128]{2,1,0:T(8,128)S(1)} collective-permute-done((f32[5,160,128]{2,1,0:T(8,128)S(1)}, f32[5,160,128]{2,1,0:T(8,128)S(1)}, u32[]{:S(2)}, u32[]{:S(2)}) %collective-permute-start.11) | collective-permute-done | bytes 409632 | tf_op jit(solution)/shard_map/cross_2/ppermute | solution.py:457
  110.2 1.0 finish_2.1.refs_0_
  111.1 4.9 %collective-permute-done.10.returned = f32[10,160,128]{2,1,0:T(8,128)S(1)} collective-permute-done((f32[10,160,128]{2,1,0:T(8,128)S(1)}, f32[10,160,128]{2,1,0:T(8,128)S(1)}, u32[]{:S(2)}, u32[]{:S(2)}) %collective-permute-start.10) | collective-permute-done | bytes 819232 | tf_op jit(solution)/shard_map/return_1/ppermute | solution.py:457
  116.1 1.2 finish_1.1.refs_0_
  117.3 20.6 %collective-permute-done.8.returned = f32[10,160,128]{2,1,0:T(8,128)S(1)} collective-permute-done((f32[10,160,128]{2,1,0:T(8,128)S(1)}, f32[10,160,128]{2,1,0:T(8,128)S(1)}, u32[]{:S(2)}, u32[]{:S(2)}) %collective-permute-start.8) | collective-permute-done | bytes 819232 | tf_op jit(solution)/shard_map/return_0/ppermute | solution.py:457
  137.9 1.2 finish_0.1
  (28 shorter events, 0.1 us)
Async XLA Ops:
  2.2 20.4 %collective-permute-start.5 = (f32[10,160,128]{2,1,0:T(8,128)}, f32[10,160,128]{2,1,0:T(8,128)}, u32[]{:S(2)}, u32[]{:S(2)}) collective-permute-start(f32[10,160,128]{2,1,0:T(8,128)} %pack_0.1.refs_1_.own), channel_id=1, source_target_pairs={{0,240},{8,24},{16,0},{24,40},{32,16},{40,56},{48,32},{56,72},{64,... | collective-permute-start | bytes 2457608 | tf_op jit(solution)/shard_map/visit_0/ppermute | solution.py:457
  10.1 30.9 %collective-permute-start.4 = (f32[10,160,128]{2,1,0:T(8,128)}, f32[10,160,128]{2,1,0:T(8,128)}, u32[]{:S(2)}, u32[]{:S(2)}) collective-permute-start(f32[10,160,128]{2,1,0:T(8,128)} %pack_0.1.refs_1_.own), channel_id=1, source_target_pairs={{0,8},{8,0},{16,24},{24,16},{32,40},{40,32},{48,56},{56,48},{64,72... | collective-permute-start | bytes 2457608 | tf_op jit(solution)/shard_map/swap_0/ppermute | solution.py:457
  12.3 28.7 %copy-start = (f32[5,160,256]{2,1,0:T(8,128)S(1)}, f32[5,160,256]{2,1,0:T(8,128)}, u32[]{:S(2)}) copy-start(f32[5,160,256]{2,1,0:T(8,128)} %constant.39.clone.refs_7_) | copy-start | bytes 2457604
  12.4 28.7 %copy-start.1 = (f32[160,256]{1,0:T(8,128)S(1)}, f32[160,256]{1,0:T(8,128)}, u32[]{:S(2)}) copy-start(f32[160,256]{1,0:T(8,128)} %constant.37.clone.refs_6_.ratio) | copy-start | bytes 491524
  12.4 28.7 %copy-start.2 = (bf16[160,480]{1,0:T(8,128)(2,1)S(1)}, bf16[160,480]{1,0:T(8,128)(2,1)}, u32[]{:S(2)}) copy-start(bf16[160,480]{1,0:T(8,128)(2,1)} %constant.36.clone.refs_5_.hartley) | copy-start | bytes 460804
  12.4 28.7 %copy-start.4 = (bf16[768,256]{1,0:T(8,128)(2,1)S(1)}, bf16[768,256]{1,0:T(8,128)(2,1)}, u32[]{:S(2)}) copy-start(bf16[768,256]{1,0:T(8,128)(2,1)} %constant.34.clone.refs_4_) | copy-start | bytes 1179652
  12.4 34.7 %collective-permute-start.3 = (f32[10,160,128]{2,1,0:T(8,128)}, f32[10,160,128]{2,1,0:T(8,128)}, u32[]{:S(2)}, u32[]{:S(2)}) collective-permute-start(f32[10,160,128]{2,1,0:T(8,128)} %pack_1.1.refs_1_.own), channel_id=1, source_target_pairs={{0,240},{8,24},{16,0},{24,40},{32,16},{40,56},{48,32},{56,72},{64,... | collective-permute-start | bytes 2457608 | tf_op jit(solution)/shard_map/visit_1/ppermute | solution.py:457
  13.9 33.2 %collective-permute-start.2 = (f32[10,160,128]{2,1,0:T(8,128)}, f32[10,160,128]{2,1,0:T(8,128)}, u32[]{:S(2)}, u32[]{:S(2)}) collective-permute-start(f32[10,160,128]{2,1,0:T(8,128)} %pack_1.1.refs_1_.own), channel_id=1, source_target_pairs={{0,8},{8,0},{16,24},{24,16},{32,40},{40,32},{48,56},{56,48},{64,72... | collective-permute-start | bytes 2457608 | tf_op jit(solution)/shard_map/swap_1/ppermute | solution.py:457
  15.2 38.9 %collective-permute-start.1 = (f32[5,160,128]{2,1,0:T(8,128)S(1)}, f32[5,160,128]{2,1,0:T(8,128)S(1)}, u32[]{:S(2)}, u32[]{:S(2)}) collective-permute-start(f32[5,160,128]{2,1,0:T(8,128)S(1)} %pack_2.1.refs_1_.own), channel_id=1, source_target_pairs={{0,240},{8,24},{16,0},{24,40},{32,16},{40,56},{48,32},{56,72},{64,... | collective-permute-start | bytes 1228808 | tf_op jit(solution)/shard_map/visit_2/ppermute | solution.py:457
  22.6 31.5 %collective-permute-start = (f32[5,160,128]{2,1,0:T(8,128)S(1)}, f32[5,160,128]{2,1,0:T(8,128)S(1)}, u32[]{:S(2)}, u32[]{:S(2)}) collective-permute-start(f32[5,160,128]{2,1,0:T(8,128)S(1)} %pack_2.1.refs_1_.own), channel_id=1, source_target_pairs={{0,8},{8,0},{16,24},{24,16},{32,40},{40,32},{48,56},{56,48},{64,72... | collective-permute-start | bytes 1228808 | tf_op jit(solution)/shard_map/swap_2/ppermute | solution.py:457
  53.2 18.0 %copy-start.9 = (f32[8,24,128]{2,1,0:T(8,128)S(1)}, f32[8,24,128]{2,1,0:T(8,128)}, u32[]{:S(2)}) copy-start(f32[8,24,128]{2,1,0:T(8,128)} %constant.43.clone.zero) | copy-start | bytes 294916
  54.1 30.0 %copy-start.3 = (bf16[768,256]{1,0:T(8,128)(2,1)S(1)}, bf16[768,256]{1,0:T(8,128)(2,1)}, u32[]{:S(2)}) copy-start(bf16[768,256]{1,0:T(8,128)(2,1)} %constant.35.clone.table) | copy-start | bytes 1179652
  54.1 30.0 %copy-start.5 = (f32[160,256]{1,0:T(8,128)S(1)}, f32[160,256]{1,0:T(8,128)}, u32[]{:S(2)}) copy-start(f32[160,256]{1,0:T(8,128)} %constant.38.clone.scale) | copy-start | bytes 491524
  54.1 30.0 %copy-start.8 = (f32[4,160,256]{2,1,0:T(8,128)S(1)}, f32[4,160,256]{2,1,0:T(8,128)}, u32[]{:S(2)}) copy-start(f32[4,160,256]{2,1,0:T(8,128)} %constant.46.edge) | copy-start | bytes 1966084
  84.2 1.9 %copy-start.7 = (f32[8,160,256]{2,1,0:T(8,128)S(1)}, f32[8,160,256]{2,1,0:T(8,128)}, u32[]{:S(2)}) copy-start(f32[8,160,256]{2,1,0:T(8,128)} %constant.47.edge) | copy-start | bytes 3932164
  85.7 16.7 %collective-permute-start.6 = (f32[5,160,128]{2,1,0:T(8,128)S(1)}, f32[5,160,128]{2,1,0:T(8,128)S(1)}, u32[]{:S(2)}, u32[]{:S(2)}) collective-permute-start(f32[5,160,128]{2,1,0:T(8,128)S(1)} %get-tuple-element.54), channel_id=1, source_target_pairs={{240,0},{24,8},{0,16},{40,24},{16,32},{56,40},{32,48},{72,56},{48,... | collective-permute-start | bytes 1228808 | tf_op jit(solution)/shard_map/return_2/ppermute | solution.py:457
  86.0 16.4 %copy-start.6 = (f32[8,160,256]{2,1,0:T(8,128)S(1)}, f32[8,160,256]{2,1,0:T(8,128)}, u32[]{:S(2)}) copy-start(f32[8,160,256]{2,1,0:T(8,128)} %constant.45.edge) | copy-start | bytes 3932164
  90.7 20.4 %collective-permute-start.9 = (f32[10,160,128]{2,1,0:T(8,128)S(1)}, f32[10,160,128]{2,1,0:T(8,128)S(1)}, u32[]{:S(2)}, u32[]{:S(2)}) collective-permute-start(f32[10,160,128]{2,1,0:T(8,128)S(1)} %get-tuple-element.68), channel_id=1, source_target_pairs={{0,8},{8,0},{16,24},{24,16},{32,40},{40,32},{48,56},{56,48},{64,72... | collective-permute-start | bytes 2457608 | tf_op jit(solution)/shard_map/cross_1/ppermute | solution.py:457
  90.8 25.3 %collective-permute-start.10 = (f32[10,160,128]{2,1,0:T(8,128)S(1)}, f32[10,160,128]{2,1,0:T(8,128)S(1)}, u32[]{:S(2)}, u32[]{:S(2)}) collective-permute-start(f32[10,160,128]{2,1,0:T(8,128)S(1)} %get-tuple-element.69), channel_id=1, source_target_pairs={{240,0},{24,8},{0,16},{40,24},{16,32},{56,40},{32,48},{72,56},{48,... | collective-permute-start | bytes 2457608 | tf_op jit(solution)/shard_map/return_1/ppermute | solution.py:457
  107.2 10.0 %collective-permute-start.7 = (f32[10,160,128]{2,1,0:T(8,128)S(1)}, f32[10,160,128]{2,1,0:T(8,128)S(1)}, u32[]{:S(2)}, u32[]{:S(2)}) collective-permute-start(f32[10,160,128]{2,1,0:T(8,128)S(1)} %get-tuple-element.63), channel_id=1, source_target_pairs={{0,8},{8,0},{16,24},{24,16},{32,40},{40,32},{48,56},{56,48},{64,72... | collective-permute-start | bytes 2457608 | tf_op jit(solution)/shard_map/cross_0/ppermute | solution.py:457
  107.2 30.6 %collective-permute-start.8 = (f32[10,160,128]{2,1,0:T(8,128)S(1)}, f32[10,160,128]{2,1,0:T(8,128)S(1)}, u32[]{:S(2)}, u32[]{:S(2)}) collective-permute-start(f32[10,160,128]{2,1,0:T(8,128)S(1)} %get-tuple-element.64), channel_id=1, source_target_pairs={{240,0},{24,8},{0,16},{40,24},{16,32},{56,40},{32,48},{72,56},{48,... | collective-permute-start | bytes 2457608 | tf_op jit(solution)/shard_map/return_0/ppermute | solution.py:457
  107.2 2.9 %collective-permute-start.11 = (f32[5,160,128]{2,1,0:T(8,128)S(1)}, f32[5,160,128]{2,1,0:T(8,128)S(1)}, u32[]{:S(2)}, u32[]{:S(2)}) collective-permute-start(f32[5,160,128]{2,1,0:T(8,128)S(1)} %get-tuple-element.71), channel_id=1, source_target_pairs={{0,8},{8,0},{16,24},{24,16},{32,40},{40,32},{48,56},{56,48},{64,72... | collective-permute-start | bytes 1228808 | tf_op jit(solution)/shard_map/cross_2/ppermute | solution.py:457

commit v4 on v3

--- a/solution.py
+++ b/solution.py
@@ -137,6 +137,10 @@
     return pltpu.VMEM
 
 
+def resting(g):
+    return pltpu.HBM if g == 0 else pltpu.VMEM
+
+
 def f32_shape(*shape):
     return jax.ShapeDtypeStruct(shape, F32)
 
@@ -146,12 +150,12 @@
 
 
 def own_shape(g):
-    return group_shape(g) if g == 2 else pltpu.HBM((GROUPS[g] * (PLANES + 1), NG, 128), F32)
+    return pltpu.HBM((GROUPS[g] * (PLANES + 1), NG, 128), F32) if g == 1 else group_shape(g)
 
 
 def packed(orbitals, g):
     count = GROUPS[g]
-    close = g == len(GROUPS) - 1
+    close = g != 1
 
     def kernel(orbitals, out, block, *refs):
         ready, (arrived, gone) = (out, refs) if close else (refs[0], refs[1:])
@@ -186,6 +190,22 @@
         [HBM],
         VMEM if close else HBM,
         scratch_shapes=scratch + [pltpu.SemaphoreType.DMA((count,))] * 2,
+    )
+
+
+def fetched(array):
+    def kernel(array, out, arrived):
+        copy = pltpu.make_async_copy(array, out, arrived)
+        copy.start()
+        copy.wait()
+
+    return call(
+        kernel,
+        "fetch",
+        [pltpu.with_memory_space_constraint(array, pltpu.HBM)],
+        pltpu.VMEM(array.shape, F32),
+        [HBM],
+        scratch_shapes=[pltpu.SemaphoreType.DMA],
     )
 
 
@@ -270,12 +290,12 @@
         for to in range(SLABS):
             out[to, SEND_TILES] = means
 
-    outs = [space(g)((2, GROUPS[g] * PLANES, NG, WIDE), F32)]
+    outs = [resting(g)((2, GROUPS[g] * PLANES, NG, WIDE), F32)]
     if last:
         outs += [f32_shape(SLABS, SEND_TILES + 1, 8, 128)]
     else:
         outs += [space(g + 1)((2, NG, WIDE), F32)] * 2 + [f32_shape(8, 128)]
-    operands = [core, *at(g, [own]), *at(g, [swap, vis])]
+    operands = [core, *(at(g, [own]) if g == 1 else kept_close([own])), *at(g, [swap, vis])]
     operands += kept_close([t["forward"], t["hartley"], t["ratio"], t["powers"]])
     if not first:
         operands += [*kept_close(state[:2]), state[2]]
@@ -357,9 +377,6 @@
         rights, lefts = edges[:2], edges[2:]
         second = core[0] == 1
         h, r, c, x_table, owner = hartley[...], ratio[...], scale[...], table[...], strip()
-        row = lax.broadcasted_iota(jnp.int32, (NG, WIDE), 0)
-        lane = lax.broadcasted_iota(jnp.int32, (NG, WIDE), 1)
-        corner = (row == 0) & (lane == 0)
         count = GROUPS[g] * PLANES
         sums = [[], []]
         for pair in range(2):
@@ -385,11 +402,10 @@
                     run = r * lefts[pair]
                     value = c * (sums[pair][z] + run) + edge[z] * rights[pair]
                     lefts[pair] = run + fields[pair, z]
-                    middle = mean[pair, PLANES * FIRST[g] + z : PLANES * FIRST[g] + z + 1, :1]
-                    value = jnp.where(corner, jnp.broadcast_to(middle, (NG, WIDE)), value)
                     along_y.append(table_times(h, value))
                 both = times_table(jnp.concatenate(along_y, axis=0), x_table)
-                parts = [both[:NG], both[NG:]]
+                middles = [mean[pair, PLANES * FIRST[g] + z : PLANES * FIRST[g] + z + 1, :1] for pair in range(2)]
+                parts = [both[:NG] + middles[0], both[NG:] + middles[1]]
                 for pair in range(2):
                     rest = parts[pair][:, 128:]
                     rests[pair] = rest if rests[pair] is None else jnp.where(owner == j, rest, rests[pair])
@@ -401,7 +417,7 @@
 
     count = GROUPS[g] * PLANES
     edge = t["edge"][PLANES * FIRST[g] : PLANES * FIRST[g] + count]
-    operands = [core, *at(g, [own]), *at(g, [swap, vis]), *kept_close([field]), mean]
+    operands = [core, *(at(g, [own]) if g == 1 else kept_close([own])), *at(g, [swap, vis]), *([pltpu.with_memory_space_constraint(field, pltpu.HBM)] if g == 0 else kept_close([field])), mean]
     operands += kept_close([edge, t["ratio"], t["scale"], t["inverse"], t["hartley"]])
     if whole:
         operands += kept_close([before])
@@ -473,6 +489,8 @@
 
     fields, befores, state = [], [], None
     for g in groups:
+        if g == 1:
+            swap[2], *state = lax.optimization_barrier((fetched(swap[2]), *state))
         befores.append(state and state[0])
         field, state = transformed(g, core, own[g], swap[g], vis[g], state, t)
         fields.append(field)

time: 139 us -> 139 us (level)
  starting transfers between devices: 34.3 us -> 17.2 us
  waiting for transfers between devices: 41.5 us -> 55.7 us
  Pallas kernels: 35.5 us -> 37.5 us
    ppermute x12, starting transfers between devices: 34.3 us -> 17.2 us  [moved(): return lax.ppermute(array, 'band', pairs)]
    ppermute x12, waiting for transfers between devices: 41.5 us -> 55.7 us  [moved(): return lax.ppermute(array, 'band', pairs)]
    pallas_call x14 -> x15, Pallas kernels: 35.5 us -> 37.5 us  [call(): pl.pallas_call(kernel, name=name, out_shape=outs, in_specs=in_specs, out_...]
  transfers between devices with their start and end apart: 12 -> 12, of which waited for: 6 -> 7; matrix products, arithmetic and copies ran while one was open for 0% -> 0% of each run, Pallas kernels for 20% -> 22%
where the time goes in v4:
time: 139 us; the launch traced here: 138 us
  waiting for transfers between devices  55.7 us (40%)
  Pallas kernels  37.5 us (27%)
  blocking collectives  27.5 us (20%)
  starting transfers between devices  17.2 us (12%)
    ppermute x12, waiting for transfers between devices, moved(): return lax.ppermute(array, 'band', pairs)  55.7 us
    pallas_call x15, Pallas kernels, call(): pl.pallas_call(kernel, name=name, out_shape=outs, in_specs=in_specs, out_...  37.5 us
    all_to_all x2, blocking collectives, exchanged(): return lax.all_to_all(flat, 'slab', 0, 0, tiled=True).reshape(array.shape)  27.5 us
    ppermute x12, starting transfers between devices, moved(): return lax.ppermute(array, 'band', pairs)  17.2 us
  transfers between devices with their start and end apart: 12, of which 7 were waited for; matrix products, arithmetic and copies ran while one was open for 0% of the time, Pallas kernels for 22%

profile of v4, /device:TPU:32, one launch (start us, length us, event | category | flops | bytes accessed | tf_op | source)
XLA Modules:
  0.0 138.1 jit_solution(15958961383611807934)
XLA Ops:
  0.0 1.5 %pack_0.1.refs_1_.own = f32[10,160,128]{2,1,0:T(8,128)S(1)} custom-call(f32[1,20,160,160]{3,2,1,0:T(8,128)} %orbitals.5), custom_call_target="tpu_custom_call" | custom-call | flops 1 | bytes 1 | tf_op jit(solution)/shard_map/pack_0/pallas_call | solution.py:115
  1.5 7.9 %collective-permute-start.2 = (f32[10,160,128]{2,1,0:T(8,128)S(1)}, f32[10,160,128]{2,1,0:T(8,128)}, u32[]{:S(2)}, u32[]{:S(2)}) collective-permute-start(f32[10,160,128]{2,1,0:T(8,128)S(1)} %pack_0.1.refs_1_.own), channel_id=1, source_target_pairs={{0,240},{8,24},{16,0},{24,40},{32,16},{40,56},{48,32},{56,72},{64,... | collective-permute-start | bytes 2457608 | tf_op jit(solution)/shard_map/visit_0/ppermute | solution.py:473
  9.4 2.2 %pack_1.1.refs_1_.own = f32[10,160,128]{2,1,0:T(8,128)} custom-call(f32[1,20,160,160]{3,2,1,0:T(8,128)} %orbitals.5), custom_call_target="tpu_custom_call" | custom-call | flops 1 | bytes 1 | tf_op jit(solution)/shard_map/pack_1/pallas_call | solution.py:115
  11.7 1.5 %collective-permute-start.5 = (f32[10,160,128]{2,1,0:T(8,128)}, f32[10,160,128]{2,1,0:T(8,128)}, u32[]{:S(2)}, u32[]{:S(2)}) collective-permute-start(f32[10,160,128]{2,1,0:T(8,128)} %pack_1.1.refs_1_.own), channel_id=1, source_target_pairs={{0,240},{8,24},{16,0},{24,40},{32,16},{40,56},{48,32},{56,72},{64,... | collective-permute-start | bytes 2457608 | tf_op jit(solution)/shard_map/visit_1/ppermute | solution.py:473
  13.2 1.3 pack_2.1.refs_1_.own
  14.5 0.6 collective-permute-start
  15.1 1.5 %collective-permute-done.array = f32[5,160,128]{2,1,0:T(8,128)} collective-permute-done((f32[5,160,128]{2,1,0:T(8,128)S(1)}, f32[5,160,128]{2,1,0:T(8,128)}, u32[]{:S(2)}, u32[]{:S(2)}) %collective-permute-start) | collective-permute-done | bytes 409632 | tf_op jit(solution)/shard_map/swap_2/ppermute | solution.py:473
  16.6 4.9 %collective-permute-start.3 = (f32[5,160,128]{2,1,0:T(8,128)S(1)}, f32[5,160,128]{2,1,0:T(8,128)S(1)}, u32[]{:S(2)}, u32[]{:S(2)}) collective-permute-start(f32[5,160,128]{2,1,0:T(8,128)S(1)} %pack_2.1.refs_1_.own), channel_id=1, source_target_pairs={{0,240},{8,24},{16,0},{24,40},{32,16},{40,56},{48,32},{56,72},{64,... | collective-permute-start | bytes 1228808 | tf_op jit(solution)/shard_map/visit_2/ppermute | solution.py:473
  21.4 0.9 pick.1.tables
  22.3 1.0 fetch.1.refs_2_.swap
  23.4 7.2 %forward_0.1 = (f32[2,8,160,256]{3,2,1,0:T(8,128)}, f32[2,160,256]{2,1,0:T(8,128)S(1)}, f32[2,160,256]{2,1,0:T(8,128)S(1)}, f32[8,128]{1,0:T(8,128)S(1)}) custom-call(s32[1]{0:T(128)} %bitcast.refs_0_.core, f32[10,160,128]{2,1,0:T(8,128)S(1)} %pack_0.1.refs_1_.own, f32[10,160,128]{2,1,0:T(8,128)} %collective-permute-done.1.refs_2_.swap, ...), custom_call_target="tpu_custom_call" | custom-call | flops 1 | bytes 1 | tf_op jit(solution)/shard_map/forward_0/pallas_call | solution.py:115
  30.6 1.8 %collective-permute-done.5.refs_3_.vis = f32[10,160,128]{2,1,0:T(8,128)} collective-permute-done((f32[10,160,128]{2,1,0:T(8,128)}, f32[10,160,128]{2,1,0:T(8,128)}, u32[]{:S(2)}, u32[]{:S(2)}) %collective-permute-start.5) | collective-permute-done | bytes 819232 | tf_op jit(solution)/shard_map/visit_1/ppermute | solution.py:473
  32.4 6.0 %forward_1.1 = (f32[2,8,160,256]{3,2,1,0:T(8,128)S(1)}, f32[2,160,256]{2,1,0:T(8,128)S(1)}, f32[2,160,256]{2,1,0:T(8,128)S(1)}, f32[8,128]{1,0:T(8,128)S(1)}) custom-call(s32[1]{0:T(128)} %bitcast.refs_0_.core, f32[10,160,128]{2,1,0:T(8,128)} %pack_1.1.refs_1_.own, f32[10,160,128]{2,1,0:T(8,128)} %collective-permute-done.4.refs_2_.swap, ...), custom_call_target="tpu_custom_call" | custom-call | flops 1 | bytes 1 | tf_op jit(solution)/shard_map/forward_1/pallas_call | solution.py:115
  38.5 14.7 %collective-permute-done.3.refs_3_.vis = f32[5,160,128]{2,1,0:T(8,128)S(1)} collective-permute-done((f32[5,160,128]{2,1,0:T(8,128)S(1)}, f32[5,160,128]{2,1,0:T(8,128)S(1)}, u32[]{:S(2)}, u32[]{:S(2)}) %collective-permute-start.3) | collective-permute-done | bytes 409632 | tf_op jit(solution)/shard_map/visit_2/ppermute | solution.py:473
  53.2 2.3 %forward_2.1 = (f32[2,4,160,256]{3,2,1,0:T(8,128)S(1)}, f32[8,14,8,128]{3,2,1,0:T(8,128)S(1)}) custom-call(s32[1]{0:T(128)} %bitcast.refs_0_.core, f32[5,160,128]{2,1,0:T(8,128)S(1)} %pack_2.1.refs_1_.own, f32[5,160,128]{2,1,0:T(8,128)S(1)} %fetch.1.refs_2_.swap, f32[5,160,128]{2,1,0:T(8,128)S(1)} %collective-permute-done.3.refs_3_.vis, ...), custom_call_target="tpu_custom_call" | custom-call | flops 1 | bytes 1 | tf_op jit(solution)/shard_map/forward_2/pallas_call | solution.py:115
  55.5 14.7 %all_to_all.18 = f32[8,112,128]{2,1,0:T(8,128)S(1)} all-to-all(f32[8,112,128]{2,1,0:T(8,128)S(1)} %bitcast.8), channel_id=1, replica_groups=mesh['band'=32,'slab'=8] {'slab'}, dimensions={0} | all-to-all | bytes 917504 | tf_op jit(solution)/shard_map/all_to_all | solution.py:468
  70.2 0.2 solve.1
  70.4 12.8 %all_to_all.19 = f32[8,104,128]{2,1,0:T(8,128)S(1)} all-to-all(f32[8,104,128]{2,1,0:T(8,128)S(1)} %bitcast.9), channel_id=1, replica_groups=mesh['band'=32,'slab'=8] {'slab'}, dimensions={0} | all-to-all | bytes 851968 | tf_op jit(solution)/shard_map/all_to_all | solution.py:468
  83.2 1.5 %products_2.1 = (f32[5,160,128]{2,1,0:T(8,128)S(1)}, f32[5,160,128]{2,1,0:T(8,128)S(1)}, f32[5,160,128]{2,1,0:T(8,128)S(1)}, f32[2,160,256]{2,1,0:T(8,128)S(1)}, f32[2,160,256]{2,1,0:T(8,128)S(1)}) custom-call(s32[1]{0:T(128)} %bitcast.refs_0_.core, f32[5,160,128]{2,1,0:T(8,128)S(1)} %pack_2.1.refs_1_.own, f32[5,160,128]{2,1,0:T(8,128)S(1)} %fetch.1.refs_2_.swap, ...), custom_call_target="tpu_custom_call" | custom-call | flops 1 | bytes 1 | tf_op jit(solution)/shard_map/products_2/pallas_call | solution.py:115
  84.8 0.3 collective-permute-start.6
  85.1 4.6 %products_1.1 = (f32[10,160,128]{2,1,0:T(8,128)S(1)}, f32[10,160,128]{2,1,0:T(8,128)S(1)}, f32[10,160,128]{2,1,0:T(8,128)S(1)}, f32[2,160,256]{2,1,0:T(8,128)S(1)}, f32[2,160,256]{2,1,0:T(8,128)S(1)}) custom-call(s32[1]{0:T(128)} %bitcast.refs_0_.core, f32[10,160,128]{2,1,0:T(8,128)} %pack_1.1.refs_1_.own, ...), custom_call_target="tpu_custom_call" | custom-call | flops 1 | bytes 1 | tf_op jit(solution)/shard_map/products_1/pallas_call | solution.py:115
  89.7 0.1 collective-permute-start.9
  89.8 1.3 collective-permute-start.10
  91.2 10.3 %collective-permute-done.6.returned = f32[5,160,128]{2,1,0:T(8,128)S(1)} collective-permute-done((f32[5,160,128]{2,1,0:T(8,128)S(1)}, f32[5,160,128]{2,1,0:T(8,128)S(1)}, u32[]{:S(2)}, u32[]{:S(2)}) %collective-permute-start.6) | collective-permute-done | bytes 409632 | tf_op jit(solution)/shard_map/return_2/ppermute | solution.py:473
  101.5 5.4 %products_0.1 = (f32[10,160,128]{2,1,0:T(8,128)S(1)}, f32[10,160,128]{2,1,0:T(8,128)S(1)}, f32[10,160,128]{2,1,0:T(8,128)S(1)}, f32[2,160,256]{2,1,0:T(8,128)}, f32[2,160,256]{2,1,0:T(8,128)}) custom-call(s32[1]{0:T(128)} %bitcast.refs_0_.core, f32[10,160,128]{2,1,0:T(8,128)S(1)} %pack_0.1.refs_1_.own, f32[10,160,128]{2,1,0:T(8,128)} %collective-permute-done.1.refs_2_.swap, ...), custom_call_target="tpu_custom_call" | custom-call | flops 1 | bytes 1 | tf_op jit(solution)/shard_map/products_0/pallas_call | solution.py:115
  106.9 0.5 collective-permute-start.11
  107.4 2.4 %collective-permute-done.11.crossed = f32[5,160,128]{2,1,0:T(8,128)S(1)} collective-permute-done((f32[5,160,128]{2,1,0:T(8,128)S(1)}, f32[5,160,128]{2,1,0:T(8,128)S(1)}, u32[]{:S(2)}, u32[]{:S(2)}) %collective-permute-start.11) | collective-permute-done | bytes 409632 | tf_op jit(solution)/shard_map/cross_2/ppermute | solution.py:473
  109.8 1.0 finish_2.1.refs_0_
  110.8 4.4 %collective-permute-done.10.returned = f32[10,160,128]{2,1,0:T(8,128)S(1)} collective-permute-done((f32[10,160,128]{2,1,0:T(8,128)S(1)}, f32[10,160,128]{2,1,0:T(8,128)S(1)}, u32[]{:S(2)}, u32[]{:S(2)}) %collective-permute-start.10) | collective-permute-done | bytes 819232 | tf_op jit(solution)/shard_map/return_1/ppermute | solution.py:473
  115.2 1.2 finish_1.1.refs_0_
  116.4 20.5 %collective-permute-done.8.returned = f32[10,160,128]{2,1,0:T(8,128)S(1)} collective-permute-done((f32[10,160,128]{2,1,0:T(8,128)S(1)}, f32[10,160,128]{2,1,0:T(8,128)S(1)}, u32[]{:S(2)}, u32[]{:S(2)}) %collective-permute-start.8) | collective-permute-done | bytes 819232 | tf_op jit(solution)/shard_map/return_0/ppermute | solution.py:473
  136.9 1.2 finish_0.1
  (29 shorter events, 0.1 us)
Async XLA Ops:
  1.5 21.9 %collective-permute-start.2 = (f32[10,160,128]{2,1,0:T(8,128)S(1)}, f32[10,160,128]{2,1,0:T(8,128)}, u32[]{:S(2)}, u32[]{:S(2)}) collective-permute-start(f32[10,160,128]{2,1,0:T(8,128)S(1)} %pack_0.1.refs_1_.own), channel_id=1, source_target_pairs={{0,240},{8,24},{16,0},{24,40},{32,16},{40,56},{48,32},{56,72},{64,... | collective-permute-start | bytes 2457608 | tf_op jit(solution)/shard_map/visit_0/ppermute | solution.py:473
  9.4 13.9 %collective-permute-start.1 = (f32[10,160,128]{2,1,0:T(8,128)S(1)}, f32[10,160,128]{2,1,0:T(8,128)}, u32[]{:S(2)}, u32[]{:S(2)}) collective-permute-start(f32[10,160,128]{2,1,0:T(8,128)S(1)} %pack_0.1.refs_1_.own), channel_id=1, source_target_pairs={{0,8},{8,0},{16,24},{24,16},{32,40},{40,32},{48,56},{56,48},{64,72... | collective-permute-start | bytes 2457608 | tf_op jit(solution)/shard_map/swap_0/ppermute | solution.py:473
  11.6 11.7 %copy-start = (f32[5,160,256]{2,1,0:T(8,128)S(1)}, f32[5,160,256]{2,1,0:T(8,128)}, u32[]{:S(2)}) copy-start(f32[5,160,256]{2,1,0:T(8,128)} %constant.39.clone.refs_7_) | copy-start | bytes 2457604
  11.6 11.7 %copy-start.1 = (f32[160,256]{1,0:T(8,128)S(1)}, f32[160,256]{1,0:T(8,128)}, u32[]{:S(2)}) copy-start(f32[160,256]{1,0:T(8,128)} %constant.37.clone.refs_6_.ratio) | copy-start | bytes 491524
  11.6 11.7 %copy-start.2 = (bf16[160,480]{1,0:T(8,128)(2,1)S(1)}, bf16[160,480]{1,0:T(8,128)(2,1)}, u32[]{:S(2)}) copy-start(bf16[160,480]{1,0:T(8,128)(2,1)} %constant.36.clone.refs_5_.hartley) | copy-start | bytes 460804
  11.7 11.7 %copy-start.4 = (bf16[768,256]{1,0:T(8,128)(2,1)S(1)}, bf16[768,256]{1,0:T(8,128)(2,1)}, u32[]{:S(2)}) copy-start(bf16[768,256]{1,0:T(8,128)(2,1)} %constant.34.clone.refs_4_) | copy-start | bytes 1179652
  11.7 20.8 %collective-permute-start.5 = (f32[10,160,128]{2,1,0:T(8,128)}, f32[10,160,128]{2,1,0:T(8,128)}, u32[]{:S(2)}, u32[]{:S(2)}) collective-permute-start(f32[10,160,128]{2,1,0:T(8,128)} %pack_1.1.refs_1_.own), channel_id=1, source_target_pairs={{0,240},{8,24},{16,0},{24,40},{32,16},{40,56},{48,32},{56,72},{64,... | collective-permute-start | bytes 2457608 | tf_op jit(solution)/shard_map/visit_1/ppermute | solution.py:473
  13.2 19.3 %collective-permute-start.4 = (f32[10,160,128]{2,1,0:T(8,128)}, f32[10,160,128]{2,1,0:T(8,128)}, u32[]{:S(2)}, u32[]{:S(2)}) collective-permute-start(f32[10,160,128]{2,1,0:T(8,128)} %pack_1.1.refs_1_.own), channel_id=1, source_target_pairs={{0,8},{8,0},{16,24},{24,16},{32,40},{40,32},{48,56},{56,48},{64,72... | collective-permute-start | bytes 2457608 | tf_op jit(solution)/shard_map/swap_1/ppermute | solution.py:473
  14.5 2.1 %collective-permute-start = (f32[5,160,128]{2,1,0:T(8,128)S(1)}, f32[5,160,128]{2,1,0:T(8,128)}, u32[]{:S(2)}, u32[]{:S(2)}) collective-permute-start(f32[5,160,128]{2,1,0:T(8,128)S(1)} %pack_2.1.refs_1_.own), channel_id=1, source_target_pairs={{0,8},{8,0},{16,24},{24,16},{32,40},{40,32},{48,56},{56,48},{64,72... | collective-permute-start | bytes 1228808 | tf_op jit(solution)/shard_map/swap_2/ppermute | solution.py:473
  16.6 36.6 %collective-permute-start.3 = (f32[5,160,128]{2,1,0:T(8,128)S(1)}, f32[5,160,128]{2,1,0:T(8,128)S(1)}, u32[]{:S(2)}, u32[]{:S(2)}) collective-permute-start(f32[5,160,128]{2,1,0:T(8,128)S(1)} %pack_2.1.refs_1_.own), channel_id=1, source_target_pairs={{0,240},{8,24},{16,0},{24,40},{32,16},{40,56},{48,32},{56,72},{64,... | collective-permute-start | bytes 1228808 | tf_op jit(solution)/shard_map/visit_2/ppermute | solution.py:473
  38.5 31.7 %copy-start.9 = (f32[8,24,128]{2,1,0:T(8,128)S(1)}, f32[8,24,128]{2,1,0:T(8,128)}, u32[]{:S(2)}) copy-start(f32[8,24,128]{2,1,0:T(8,128)} %constant.43.clone.zero) | copy-start | bytes 294916
  53.2 30.0 %copy-start.3 = (bf16[768,256]{1,0:T(8,128)(2,1)S(1)}, bf16[768,256]{1,0:T(8,128)(2,1)}, u32[]{:S(2)}) copy-start(bf16[768,256]{1,0:T(8,128)(2,1)} %constant.35.clone.table) | copy-start | bytes 1179652
  53.2 30.0 %copy-start.5 = (f32[160,256]{1,0:T(8,128)S(1)}, f32[160,256]{1,0:T(8,128)}, u32[]{:S(2)}) copy-start(f32[160,256]{1,0:T(8,128)} %constant.38.clone.scale) | copy-start | bytes 491524
  53.2 30.0 %copy-start.8 = (f32[4,160,256]{2,1,0:T(8,128)S(1)}, f32[4,160,256]{2,1,0:T(8,128)}, u32[]{:S(2)}) copy-start(f32[4,160,256]{2,1,0:T(8,128)} %constant.46.edge) | copy-start | bytes 1966084
  83.2 1.9 %copy-start.7 = (f32[8,160,256]{2,1,0:T(8,128)S(1)}, f32[8,160,256]{2,1,0:T(8,128)}, u32[]{:S(2)}) copy-start(f32[8,160,256]{2,1,0:T(8,128)} %constant.47.edge) | copy-start | bytes 3932164
  84.8 16.7 %collective-permute-start.6 = (f32[5,160,128]{2,1,0:T(8,128)S(1)}, f32[5,160,128]{2,1,0:T(8,128)S(1)}, u32[]{:S(2)}, u32[]{:S(2)}) collective-permute-start(f32[5,160,128]{2,1,0:T(8,128)S(1)} %get-tuple-element.62), channel_id=1, source_target_pairs={{240,0},{24,8},{0,16},{40,24},{16,32},{56,40},{32,48},{72,56},{48,... | collective-permute-start | bytes 1228808 | tf_op jit(solution)/shard_map/return_2/ppermute | solution.py:473
  85.1 16.4 %copy-start.6 = (f32[8,160,256]{2,1,0:T(8,128)S(1)}, f32[8,160,256]{2,1,0:T(8,128)}, u32[]{:S(2)}) copy-start(f32[8,160,256]{2,1,0:T(8,128)} %constant.45.edge) | copy-start | bytes 3932164
  89.7 21.0 %collective-permute-start.9 = (f32[10,160,128]{2,1,0:T(8,128)S(1)}, f32[10,160,128]{2,1,0:T(8,128)S(1)}, u32[]{:S(2)}, u32[]{:S(2)}) collective-permute-start(f32[10,160,128]{2,1,0:T(8,128)S(1)} %get-tuple-element.76), channel_id=1, source_target_pairs={{0,8},{8,0},{16,24},{24,16},{32,40},{40,32},{48,56},{56,48},{64,72... | collective-permute-start | bytes 2457608 | tf_op jit(solution)/shard_map/cross_1/ppermute | solution.py:473
  89.8 25.3 %collective-permute-start.10 = (f32[10,160,128]{2,1,0:T(8,128)S(1)}, f32[10,160,128]{2,1,0:T(8,128)S(1)}, u32[]{:S(2)}, u32[]{:S(2)}) collective-permute-start(f32[10,160,128]{2,1,0:T(8,128)S(1)} %get-tuple-element.77), channel_id=1, source_target_pairs={{240,0},{24,8},{0,16},{40,24},{16,32},{56,40},{32,48},{72,56},{48,... | collective-permute-start | bytes 2457608 | tf_op jit(solution)/shard_map/return_1/ppermute | solution.py:473
  106.9 9.5 %collective-permute-start.7 = (f32[10,160,128]{2,1,0:T(8,128)S(1)}, f32[10,160,128]{2,1,0:T(8,128)S(1)}, u32[]{:S(2)}, u32[]{:S(2)}) collective-permute-start(f32[10,160,128]{2,1,0:T(8,128)S(1)} %get-tuple-element.71), channel_id=1, source_target_pairs={{0,8},{8,0},{16,24},{24,16},{32,40},{40,32},{48,56},{56,48},{64,72... | collective-permute-start | bytes 2457608 | tf_op jit(solution)/shard_map/cross_0/ppermute | solution.py:473
  106.9 30.0 %collective-permute-start.8 = (f32[10,160,128]{2,1,0:T(8,128)S(1)}, f32[10,160,128]{2,1,0:T(8,128)S(1)}, u32[]{:S(2)}, u32[]{:S(2)}) collective-permute-start(f32[10,160,128]{2,1,0:T(8,128)S(1)} %get-tuple-element.72), channel_id=1, source_target_pairs={{240,0},{24,8},{0,16},{40,24},{16,32},{56,40},{32,48},{72,56},{48,... | collective-permute-start | bytes 2457608 | tf_op jit(solution)/shard_map/return_0/ppermute | solution.py:473
  106.9 2.9 %collective-permute-start.11 = (f32[5,160,128]{2,1,0:T(8,128)S(1)}, f32[5,160,128]{2,1,0:T(8,128)S(1)}, u32[]{:S(2)}, u32[]{:S(2)}) collective-permute-start(f32[5,160,128]{2,1,0:T(8,128)S(1)} %get-tuple-element.79), channel_id=1, source_target_pairs={{0,8},{8,0},{16,24},{24,16},{32,40},{40,32},{48,56},{56,48},{64,72... | collective-permute-start | bytes 1228808 | tf_op jit(solution)/shard_map/cross_2/ppermute | solution.py:473

commit v5 on v4

--- a/solution.py
+++ b/solution.py
@@ -138,7 +138,7 @@
 
 
 def resting(g):
-    return pltpu.HBM if g == 0 else pltpu.VMEM
+    return pltpu.VMEM
 
 
 def f32_shape(*shape):
@@ -417,7 +417,7 @@
 
     count = GROUPS[g] * PLANES
     edge = t["edge"][PLANES * FIRST[g] : PLANES * FIRST[g] + count]
-    operands = [core, *(at(g, [own]) if g == 1 else kept_close([own])), *at(g, [swap, vis]), *([pltpu.with_memory_space_constraint(field, pltpu.HBM)] if g == 0 else kept_close([field])), mean]
+    operands = [core, *(at(g, [own]) if g == 1 else kept_close([own])), *at(g, [swap, vis]), *kept_close([field]), mean]
     operands += kept_close([edge, t["ratio"], t["scale"], t["inverse"], t["hartley"]])
     if whole:
         operands += kept_close([before])
@@ -434,18 +434,28 @@
 
 
 def finished(g, kept, crossed, returned, result):
+    count = GROUPS[g]
+
     def kernel(kept, crossed, returned, *refs):
-        out = refs[-1]
-        total = kept[...] + crossed[...] + returned[...]
-        out[0, :, :, :128] = total[:PLANES]
-        rest = total[PLANES]
-        for j in range(PLANES):
-            moved = rest if j == 0 else pltpu.roll(rest, 128 - 32 * j, 1)
-            out[0, j, :, 128:] = moved[:, :32]
-
-    block = pl.BlockSpec((PLANES + 1, NG, 128), lambda i: (i, 0, 0))
+        out, block, gone = refs[-3:]
+        copies = []
+        for c in range(count):
+            base = c * (PLANES + 1)
+            rest = kept[base + PLANES] + crossed[base + PLANES] + returned[base + PLANES]
+            for j in range(PLANES):
+                z = c * PLANES + j
+                block[z, :, :128] = kept[base + j] + crossed[base + j] + returned[base + j]
+                moved = rest if j == 0 else pltpu.roll(rest, 128 - 32 * j, 1)
+                block[z, :, 128:] = moved[:, :32]
+            here = pl.ds(c * PLANES, PLANES)
+            there = pl.ds((FIRST[g] + c) * PLANES, PLANES)
+            copies.append(pltpu.make_async_copy(block.at[here], out.at[0, there], gone.at[c]))
+            copies[c].start()
+        for copy in copies:
+            copy.wait()
+
     operands = [kept, crossed, returned]
-    specs = [block] * 3
+    specs = [VMEM] * 3
     aliases = {}
     if result is not None:
         operands.append(result)
@@ -457,9 +467,9 @@
         operands,
         pltpu.HBM((1, DEPTH, NG, NG), F32),
         specs,
-        pl.BlockSpec((1, PLANES, NG, NG), lambda i: (0, FIRST[g] + i, 0, 0)),
-        grid=(GROUPS[g],),
+        HBM,
         input_output_aliases=aliases,
+        scratch_shapes=[pltpu.VMEM((count * PLANES, NG, NG), F32), pltpu.SemaphoreType.DMA((count,))],
     )
 
 

time: 139 us -> 139 us (level)
  Pallas kernels: 37.5 us -> 35.2 us
  waiting for transfers between devices: 55.7 us -> 58 us
    pallas_call x15, Pallas kernels: 37.5 us -> 35.2 us  [call(): pl.pallas_call(kernel, name=name, out_shape=outs, in_specs=in_specs, out_...]
    ppermute x12, waiting for transfers between devices: 55.7 us -> 58 us  [moved(): return lax.ppermute(array, 'band', pairs)]
  transfers between devices with their start and end apart: 12 -> 12, of which waited for: 7 -> 7; matrix products, arithmetic and copies ran while one was open for 0% -> 0% of each run, Pallas kernels for 22% -> 21%
where the time goes in v5:
time: 139 us; the launch traced here: 138 us
  waiting for transfers between devices  58 us (42%)
  Pallas kernels  35.2 us (25%)
  blocking collectives  27.5 us (20%)
  starting transfers between devices  17.2 us (12%)
    ppermute x12, waiting for transfers between devices, moved(): return lax.ppermute(array, 'band', pairs)  58 us
    pallas_call x15, Pallas kernels, call(): pl.pallas_call(kernel, name=name, out_shape=outs, in_specs=in_specs, out_...  35.2 us
    all_to_all x2, blocking collectives, exchanged(): return lax.all_to_all(flat, 'slab', 0, 0, tiled=True).reshape(array.shape)  27.5 us
    ppermute x12, starting transfers between devices, moved(): return lax.ppermute(array, 'band', pairs)  17.2 us
  transfers between devices with their start and end apart: 12, of which 7 were waited for; matrix products, arithmetic and copies ran while one was open for 0% of the time, Pallas kernels for 21%

profile of v5, /device:TPU:32, one launch (start us, length us, event | category | flops | bytes accessed | tf_op | source)
XLA Modules:
  0.0 138.3 jit_solution(4988605616421370959)
XLA Ops:
  0.0 1.5 %pack_0.1.refs_1_.own = f32[10,160,128]{2,1,0:T(8,128)S(1)} custom-call(f32[1,20,160,160]{3,2,1,0:T(8,128)} %orbitals.5), custom_call_target="tpu_custom_call" | custom-call | flops 1 | bytes 1 | tf_op jit(solution)/shard_map/pack_0/pallas_call | solution.py:115
  1.5 7.9 %collective-permute-start.2 = (f32[10,160,128]{2,1,0:T(8,128)S(1)}, f32[10,160,128]{2,1,0:T(8,128)}, u32[]{:S(2)}, u32[]{:S(2)}) collective-permute-start(f32[10,160,128]{2,1,0:T(8,128)S(1)} %pack_0.1.refs_1_.own), channel_id=1, source_target_pairs={{0,240},{8,24},{16,0},{24,40},{32,16},{40,56},{48,32},{56,72},{64,... | collective-permute-start | bytes 2457608 | tf_op jit(solution)/shard_map/visit_0/ppermute | solution.py:483
  9.4 2.2 %pack_1.1.refs_1_.own = f32[10,160,128]{2,1,0:T(8,128)} custom-call(f32[1,20,160,160]{3,2,1,0:T(8,128)} %orbitals.5), custom_call_target="tpu_custom_call" | custom-call | flops 1 | bytes 1 | tf_op jit(solution)/shard_map/pack_1/pallas_call | solution.py:115
  11.7 1.5 %collective-permute-start.5 = (f32[10,160,128]{2,1,0:T(8,128)}, f32[10,160,128]{2,1,0:T(8,128)}, u32[]{:S(2)}, u32[]{:S(2)}) collective-permute-start(f32[10,160,128]{2,1,0:T(8,128)} %pack_1.1.refs_1_.own), channel_id=1, source_target_pairs={{0,240},{8,24},{16,0},{24,40},{32,16},{40,56},{48,32},{56,72},{64,... | collective-permute-start | bytes 2457608 | tf_op jit(solution)/shard_map/visit_1/ppermute | solution.py:483
  13.2 1.3 pack_2.1.refs_1_.own
  14.5 0.6 collective-permute-start
  15.1 1.5 %collective-permute-done.array = f32[5,160,128]{2,1,0:T(8,128)} collective-permute-done((f32[5,160,128]{2,1,0:T(8,128)S(1)}, f32[5,160,128]{2,1,0:T(8,128)}, u32[]{:S(2)}, u32[]{:S(2)}) %collective-permute-start) | collective-permute-done | bytes 409632 | tf_op jit(solution)/shard_map/swap_2/ppermute | solution.py:483
  16.6 4.9 %collective-permute-start.3 = (f32[5,160,128]{2,1,0:T(8,128)S(1)}, f32[5,160,128]{2,1,0:T(8,128)S(1)}, u32[]{:S(2)}, u32[]{:S(2)}) collective-permute-start(f32[5,160,128]{2,1,0:T(8,128)S(1)} %pack_2.1.refs_1_.own), channel_id=1, source_target_pairs={{0,240},{8,24},{16,0},{24,40},{32,16},{40,56},{48,32},{56,72},{64,... | collective-permute-start | bytes 1228808 | tf_op jit(solution)/shard_map/visit_2/ppermute | solution.py:483
  21.4 0.9 pick.1.tables
  22.3 1.0 fetch.1.refs_2_.swap
  23.4 5.8 %forward_0.1 = (f32[2,8,160,256]{3,2,1,0:T(8,128)S(1)}, f32[2,160,256]{2,1,0:T(8,128)S(1)}, f32[2,160,256]{2,1,0:T(8,128)S(1)}, f32[8,128]{1,0:T(8,128)S(1)}) custom-call(s32[1]{0:T(128)} %bitcast.refs_0_.core, f32[10,160,128]{2,1,0:T(8,128)S(1)} %pack_0.1.refs_1_.own, f32[10,160,128]{2,1,0:T(8,128)} %collective-permute-done.1.refs_2_.swap, ...), custom_call_target="tpu_custom_call" | custom-call | flops 1 | bytes 1 | tf_op jit(solution)/shard_map/forward_0/pallas_call | solution.py:115
  29.2 3.3 %collective-permute-done.5.refs_3_.vis = f32[10,160,128]{2,1,0:T(8,128)} collective-permute-done((f32[10,160,128]{2,1,0:T(8,128)}, f32[10,160,128]{2,1,0:T(8,128)}, u32[]{:S(2)}, u32[]{:S(2)}) %collective-permute-start.5) | collective-permute-done | bytes 819232 | tf_op jit(solution)/shard_map/visit_1/ppermute | solution.py:483
  32.4 6.0 %forward_1.1 = (f32[2,8,160,256]{3,2,1,0:T(8,128)S(1)}, f32[2,160,256]{2,1,0:T(8,128)S(1)}, f32[2,160,256]{2,1,0:T(8,128)S(1)}, f32[8,128]{1,0:T(8,128)S(1)}) custom-call(s32[1]{0:T(128)} %bitcast.refs_0_.core, f32[10,160,128]{2,1,0:T(8,128)} %pack_1.1.refs_1_.own, f32[10,160,128]{2,1,0:T(8,128)} %collective-permute-done.4.refs_2_.swap, ...), custom_call_target="tpu_custom_call" | custom-call | flops 1 | bytes 1 | tf_op jit(solution)/shard_map/forward_1/pallas_call | solution.py:115
  38.5 14.7 %collective-permute-done.3.refs_3_.vis = f32[5,160,128]{2,1,0:T(8,128)S(1)} collective-permute-done((f32[5,160,128]{2,1,0:T(8,128)S(1)}, f32[5,160,128]{2,1,0:T(8,128)S(1)}, u32[]{:S(2)}, u32[]{:S(2)}) %collective-permute-start.3) | collective-permute-done | bytes 409632 | tf_op jit(solution)/shard_map/visit_2/ppermute | solution.py:483
  53.2 2.3 %forward_2.1 = (f32[2,4,160,256]{3,2,1,0:T(8,128)S(1)}, f32[8,14,8,128]{3,2,1,0:T(8,128)S(1)}) custom-call(s32[1]{0:T(128)} %bitcast.refs_0_.core, f32[5,160,128]{2,1,0:T(8,128)S(1)} %pack_2.1.refs_1_.own, f32[5,160,128]{2,1,0:T(8,128)S(1)} %fetch.1.refs_2_.swap, f32[5,160,128]{2,1,0:T(8,128)S(1)} %collective-permute-done.3.refs_3_.vis, ...), custom_call_target="tpu_custom_call" | custom-call | flops 1 | bytes 1 | tf_op jit(solution)/shard_map/forward_2/pallas_call | solution.py:115
  55.5 14.7 %all_to_all.18 = f32[8,112,128]{2,1,0:T(8,128)S(1)} all-to-all(f32[8,112,128]{2,1,0:T(8,128)S(1)} %bitcast.8), channel_id=1, replica_groups=mesh['band'=32,'slab'=8] {'slab'}, dimensions={0} | all-to-all | bytes 917504 | tf_op jit(solution)/shard_map/all_to_all | solution.py:478
  70.2 0.2 solve.1
  70.4 12.8 %all_to_all.19 = f32[8,104,128]{2,1,0:T(8,128)S(1)} all-to-all(f32[8,104,128]{2,1,0:T(8,128)S(1)} %bitcast.9), channel_id=1, replica_groups=mesh['band'=32,'slab'=8] {'slab'}, dimensions={0} | all-to-all | bytes 851968 | tf_op jit(solution)/shard_map/all_to_all | solution.py:478
  83.2 1.5 %products_2.1 = (f32[5,160,128]{2,1,0:T(8,128)S(1)}, f32[5,160,128]{2,1,0:T(8,128)S(1)}, f32[5,160,128]{2,1,0:T(8,128)S(1)}, f32[2,160,256]{2,1,0:T(8,128)S(1)}, f32[2,160,256]{2,1,0:T(8,128)S(1)}) custom-call(s32[1]{0:T(128)} %bitcast.refs_0_.core, f32[5,160,128]{2,1,0:T(8,128)S(1)} %pack_2.1.refs_1_.own, f32[5,160,128]{2,1,0:T(8,128)S(1)} %fetch.1.refs_2_.swap, ...), custom_call_target="tpu_custom_call" | custom-call | flops 1 | bytes 1 | tf_op jit(solution)/shard_map/products_2/pallas_call | solution.py:115
  84.8 0.3 collective-permute-start.6
  85.1 4.6 %products_1.1 = (f32[10,160,128]{2,1,0:T(8,128)S(1)}, f32[10,160,128]{2,1,0:T(8,128)S(1)}, f32[10,160,128]{2,1,0:T(8,128)S(1)}, f32[2,160,256]{2,1,0:T(8,128)S(1)}, f32[2,160,256]{2,1,0:T(8,128)S(1)}) custom-call(s32[1]{0:T(128)} %bitcast.refs_0_.core, f32[10,160,128]{2,1,0:T(8,128)} %pack_1.1.refs_1_.own, ...), custom_call_target="tpu_custom_call" | custom-call | flops 1 | bytes 1 | tf_op jit(solution)/shard_map/products_1/pallas_call | solution.py:115
  89.7 0.1 collective-permute-start.9
  89.8 1.3 collective-permute-start.10
  91.2 10.3 %collective-permute-done.6.returned = f32[5,160,128]{2,1,0:T(8,128)S(1)} collective-permute-done((f32[5,160,128]{2,1,0:T(8,128)S(1)}, f32[5,160,128]{2,1,0:T(8,128)S(1)}, u32[]{:S(2)}, u32[]{:S(2)}) %collective-permute-start.6) | collective-permute-done | bytes 409632 | tf_op jit(solution)/shard_map/return_2/ppermute | solution.py:483
  101.5 4.5 %products_0.1 = (f32[10,160,128]{2,1,0:T(8,128)S(1)}, f32[10,160,128]{2,1,0:T(8,128)S(1)}, f32[10,160,128]{2,1,0:T(8,128)S(1)}, f32[2,160,256]{2,1,0:T(8,128)}, f32[2,160,256]{2,1,0:T(8,128)}) custom-call(s32[1]{0:T(128)} %bitcast.refs_0_.core, f32[10,160,128]{2,1,0:T(8,128)S(1)} %pack_0.1.refs_1_.own, f32[10,160,128]{2,1,0:T(8,128)} %collective-permute-done.1.refs_2_.swap, ...), custom_call_target="tpu_custom_call" | custom-call | flops 1 | bytes 1 | tf_op jit(solution)/shard_map/products_0/pallas_call | solution.py:115
  106.0 0.5 collective-permute-start.11
  106.5 2.4 %collective-permute-done.11.crossed = f32[5,160,128]{2,1,0:T(8,128)S(1)} collective-permute-done((f32[5,160,128]{2,1,0:T(8,128)S(1)}, f32[5,160,128]{2,1,0:T(8,128)S(1)}, u32[]{:S(2)}, u32[]{:S(2)}) %collective-permute-start.11) | collective-permute-done | bytes 409632 | tf_op jit(solution)/shard_map/cross_2/ppermute | solution.py:483
  108.9 1.0 finish_2.1.refs_0_
  109.9 5.3 %collective-permute-done.10.returned = f32[10,160,128]{2,1,0:T(8,128)S(1)} collective-permute-done((f32[10,160,128]{2,1,0:T(8,128)S(1)}, f32[10,160,128]{2,1,0:T(8,128)S(1)}, u32[]{:S(2)}, u32[]{:S(2)}) %collective-permute-start.10) | collective-permute-done | bytes 819232 | tf_op jit(solution)/shard_map/return_1/ppermute | solution.py:483
  115.2 1.2 finish_1.1.refs_0_
  116.4 20.5 %collective-permute-done.8.returned = f32[10,160,128]{2,1,0:T(8,128)S(1)} collective-permute-done((f32[10,160,128]{2,1,0:T(8,128)S(1)}, f32[10,160,128]{2,1,0:T(8,128)S(1)}, u32[]{:S(2)}, u32[]{:S(2)}) %collective-permute-start.8) | collective-permute-done | bytes 819232 | tf_op jit(solution)/shard_map/return_0/ppermute | solution.py:483
  136.9 1.2 finish_0.1
  (29 shorter events, 0.1 us)
Async XLA Ops:
  1.5 21.9 %collective-permute-start.2 = (f32[10,160,128]{2,1,0:T(8,128)S(1)}, f32[10,160,128]{2,1,0:T(8,128)}, u32[]{:S(2)}, u32[]{:S(2)}) collective-permute-start(f32[10,160,128]{2,1,0:T(8,128)S(1)} %pack_0.1.refs_1_.own), channel_id=1, source_target_pairs={{0,240},{8,24},{16,0},{24,40},{32,16},{40,56},{48,32},{56,72},{64,... | collective-permute-start | bytes 2457608 | tf_op jit(solution)/shard_map/visit_0/ppermute | solution.py:483
  9.4 13.9 %collective-permute-start.1 = (f32[10,160,128]{2,1,0:T(8,128)S(1)}, f32[10,160,128]{2,1,0:T(8,128)}, u32[]{:S(2)}, u32[]{:S(2)}) collective-permute-start(f32[10,160,128]{2,1,0:T(8,128)S(1)} %pack_0.1.refs_1_.own), channel_id=1, source_target_pairs={{0,8},{8,0},{16,24},{24,16},{32,40},{40,32},{48,56},{56,48},{64,72... | collective-permute-start | bytes 2457608 | tf_op jit(solution)/shard_map/swap_0/ppermute | solution.py:483
  11.6 11.7 %copy-start = (f32[5,160,256]{2,1,0:T(8,128)S(1)}, f32[5,160,256]{2,1,0:T(8,128)}, u32[]{:S(2)}) copy-start(f32[5,160,256]{2,1,0:T(8,128)} %constant.39.clone.refs_7_) | copy-start | bytes 2457604
  11.6 11.7 %copy-start.1 = (f32[160,256]{1,0:T(8,128)S(1)}, f32[160,256]{1,0:T(8,128)}, u32[]{:S(2)}) copy-start(f32[160,256]{1,0:T(8,128)} %constant.37.clone.refs_6_.ratio) | copy-start | bytes 491524
  11.6 11.7 %copy-start.2 = (bf16[160,480]{1,0:T(8,128)(2,1)S(1)}, bf16[160,480]{1,0:T(8,128)(2,1)}, u32[]{:S(2)}) copy-start(bf16[160,480]{1,0:T(8,128)(2,1)} %constant.36.clone.refs_5_.hartley) | copy-start | bytes 460804
  11.7 11.7 %copy-start.4 = (bf16[768,256]{1,0:T(8,128)(2,1)S(1)}, bf16[768,256]{1,0:T(8,128)(2,1)}, u32[]{:S(2)}) copy-start(bf16[768,256]{1,0:T(8,128)(2,1)} %constant.34.clone.refs_4_) | copy-start | bytes 1179652
  11.7 20.8 %collective-permute-start.5 = (f32[10,160,128]{2,1,0:T(8,128)}, f32[10,160,128]{2,1,0:T(8,128)}, u32[]{:S(2)}, u32[]{:S(2)}) collective-permute-start(f32[10,160,128]{2,1,0:T(8,128)} %pack_1.1.refs_1_.own), channel_id=1, source_target_pairs={{0,240},{8,24},{16,0},{24,40},{32,16},{40,56},{48,32},{56,72},{64,... | collective-permute-start | bytes 2457608 | tf_op jit(solution)/shard_map/visit_1/ppermute | solution.py:483
  13.2 19.3 %collective-permute-start.4 = (f32[10,160,128]{2,1,0:T(8,128)}, f32[10,160,128]{2,1,0:T(8,128)}, u32[]{:S(2)}, u32[]{:S(2)}) collective-permute-start(f32[10,160,128]{2,1,0:T(8,128)} %pack_1.1.refs_1_.own), channel_id=1, source_target_pairs={{0,8},{8,0},{16,24},{24,16},{32,40},{40,32},{48,56},{56,48},{64,72... | collective-permute-start | bytes 2457608 | tf_op jit(solution)/shard_map/swap_1/ppermute | solution.py:483
  14.5 2.1 %collective-permute-start = (f32[5,160,128]{2,1,0:T(8,128)S(1)}, f32[5,160,128]{2,1,0:T(8,128)}, u32[]{:S(2)}, u32[]{:S(2)}) collective-permute-start(f32[5,160,128]{2,1,0:T(8,128)S(1)} %pack_2.1.refs_1_.own), channel_id=1, source_target_pairs={{0,8},{8,0},{16,24},{24,16},{32,40},{40,32},{48,56},{56,48},{64,72... | collective-permute-start | bytes 1228808 | tf_op jit(solution)/shard_map/swap_2/ppermute | solution.py:483
  16.6 36.6 %collective-permute-start.3 = (f32[5,160,128]{2,1,0:T(8,128)S(1)}, f32[5,160,128]{2,1,0:T(8,128)S(1)}, u32[]{:S(2)}, u32[]{:S(2)}) collective-permute-start(f32[5,160,128]{2,1,0:T(8,128)S(1)} %pack_2.1.refs_1_.own), channel_id=1, source_target_pairs={{0,240},{8,24},{16,0},{24,40},{32,16},{40,56},{48,32},{56,72},{64,... | collective-permute-start | bytes 1228808 | tf_op jit(solution)/shard_map/visit_2/ppermute | solution.py:483
  38.5 31.7 %copy-start.9 = (f32[8,24,128]{2,1,0:T(8,128)S(1)}, f32[8,24,128]{2,1,0:T(8,128)}, u32[]{:S(2)}) copy-start(f32[8,24,128]{2,1,0:T(8,128)} %constant.43.clone.zero) | copy-start | bytes 294916
  53.2 30.0 %copy-start.3 = (bf16[768,256]{1,0:T(8,128)(2,1)S(1)}, bf16[768,256]{1,0:T(8,128)(2,1)}, u32[]{:S(2)}) copy-start(bf16[768,256]{1,0:T(8,128)(2,1)} %constant.35.clone.table) | copy-start | bytes 1179652
  53.2 30.0 %copy-start.5 = (f32[160,256]{1,0:T(8,128)S(1)}, f32[160,256]{1,0:T(8,128)}, u32[]{:S(2)}) copy-start(f32[160,256]{1,0:T(8,128)} %constant.38.clone.scale) | copy-start | bytes 491524
  53.2 30.0 %copy-start.8 = (f32[4,160,256]{2,1,0:T(8,128)S(1)}, f32[4,160,256]{2,1,0:T(8,128)}, u32[]{:S(2)}) copy-start(f32[4,160,256]{2,1,0:T(8,128)} %constant.46.edge) | copy-start | bytes 1966084
  83.2 1.9 %copy-start.7 = (f32[8,160,256]{2,1,0:T(8,128)S(1)}, f32[8,160,256]{2,1,0:T(8,128)}, u32[]{:S(2)}) copy-start(f32[8,160,256]{2,1,0:T(8,128)} %constant.47.edge) | copy-start | bytes 3932164
  84.8 16.7 %collective-permute-start.6 = (f32[5,160,128]{2,1,0:T(8,128)S(1)}, f32[5,160,128]{2,1,0:T(8,128)S(1)}, u32[]{:S(2)}, u32[]{:S(2)}) collective-permute-start(f32[5,160,128]{2,1,0:T(8,128)S(1)} %get-tuple-element.62), channel_id=1, source_target_pairs={{240,0},{24,8},{0,16},{40,24},{16,32},{56,40},{32,48},{72,56},{48,... | collective-permute-start | bytes 1228808 | tf_op jit(solution)/shard_map/return_2/ppermute | solution.py:483
  85.1 16.4 %copy-start.6 = (f32[8,160,256]{2,1,0:T(8,128)S(1)}, f32[8,160,256]{2,1,0:T(8,128)}, u32[]{:S(2)}) copy-start(f32[8,160,256]{2,1,0:T(8,128)} %constant.45.edge) | copy-start | bytes 3932164
  89.7 20.1 %collective-permute-start.9 = (f32[10,160,128]{2,1,0:T(8,128)S(1)}, f32[10,160,128]{2,1,0:T(8,128)S(1)}, u32[]{:S(2)}, u32[]{:S(2)}) collective-permute-start(f32[10,160,128]{2,1,0:T(8,128)S(1)} %get-tuple-element.76), channel_id=1, source_target_pairs={{0,8},{8,0},{16,24},{24,16},{32,40},{40,32},{48,56},{56,48},{64,72... | collective-permute-start | bytes 2457608 | tf_op jit(solution)/shard_map/cross_1/ppermute | solution.py:483
  89.8 25.3 %collective-permute-start.10 = (f32[10,160,128]{2,1,0:T(8,128)S(1)}, f32[10,160,128]{2,1,0:T(8,128)S(1)}, u32[]{:S(2)}, u32[]{:S(2)}) collective-permute-start(f32[10,160,128]{2,1,0:T(8,128)S(1)} %get-tuple-element.77), channel_id=1, source_target_pairs={{240,0},{24,8},{0,16},{40,24},{16,32},{56,40},{32,48},{72,56},{48,... | collective-permute-start | bytes 2457608 | tf_op jit(solution)/shard_map/return_1/ppermute | solution.py:483
  106.0 10.4 %collective-permute-start.7 = (f32[10,160,128]{2,1,0:T(8,128)S(1)}, f32[10,160,128]{2,1,0:T(8,128)S(1)}, u32[]{:S(2)}, u32[]{:S(2)}) collective-permute-start(f32[10,160,128]{2,1,0:T(8,128)S(1)} %get-tuple-element.71), channel_id=1, source_target_pairs={{0,8},{8,0},{16,24},{24,16},{32,40},{40,32},{48,56},{56,48},{64,72... | collective-permute-start | bytes 2457608 | tf_op jit(solution)/shard_map/cross_0/ppermute | solution.py:483
  106.0 30.9 %collective-permute-start.8 = (f32[10,160,128]{2,1,0:T(8,128)S(1)}, f32[10,160,128]{2,1,0:T(8,128)S(1)}, u32[]{:S(2)}, u32[]{:S(2)}) collective-permute-start(f32[10,160,128]{2,1,0:T(8,128)S(1)} %get-tuple-element.72), channel_id=1, source_target_pairs={{240,0},{24,8},{0,16},{40,24},{16,32},{56,40},{32,48},{72,56},{48,... | collective-permute-start | bytes 2457608 | tf_op jit(solution)/shard_map/return_0/ppermute | solution.py:483
  106.0 2.9 %collective-permute-start.11 = (f32[5,160,128]{2,1,0:T(8,128)S(1)}, f32[5,160,128]{2,1,0:T(8,128)S(1)}, u32[]{:S(2)}, u32[]{:S(2)}) collective-permute-start(f32[5,160,128]{2,1,0:T(8,128)S(1)} %get-tuple-element.79), channel_id=1, source_target_pairs={{0,8},{8,0},{16,24},{24,16},{32,40},{40,32},{48,56},{56,48},{64,72... | collective-permute-start | bytes 1228808 | tf_op jit(solution)/shard_map/cross_2/ppermute | solution.py:483

commit v6 on v5

--- a/solution.py
+++ b/solution.py
@@ -160,16 +160,15 @@
     def kernel(orbitals, out, block, *refs):
         ready, (arrived, gone) = (out, refs) if close else (refs[0], refs[1:])
         comes, goes = [], []
+        for z in range(count * PLANES):
+            there = orbitals.at[0, FIRST[g] * PLANES + z]
+            comes.append(pltpu.make_async_copy(there, block.at[z], arrived.at[z]))
+            comes[z].start()
         for c in range(count):
-            there = pl.ds((FIRST[g] + c) * PLANES, PLANES)
-            here = pl.ds(c * PLANES, PLANES)
-            comes.append(pltpu.make_async_copy(orbitals.at[0, there], block.at[here], arrived.at[c]))
-            comes[c].start()
-        for c in range(count):
-            comes[c].wait()
             base = c * (PLANES + 1)
             planes = range(c * PLANES, (c + 1) * PLANES)
             for j, z in enumerate(planes):
+                comes[z].wait()
                 ready[base + j] = block[z, :, :128]
             ready[base + PLANES] = jnp.concatenate([block[z, :, 128:] for z in planes], axis=1)
             if not close:
@@ -189,7 +188,7 @@
         own_shape(g),
         [HBM],
         VMEM if close else HBM,
-        scratch_shapes=scratch + [pltpu.SemaphoreType.DMA((count,))] * 2,
+        scratch_shapes=scratch + [pltpu.SemaphoreType.DMA((n,)) for n in (count * PLANES, count)],
     )
 
 

time: 139 us -> 139 us (level)
  no operation moved by 1% of the time
where the time goes in v6:
time: 139 us; the launch traced here: 138 us
  waiting for transfers between devices  57.8 us (42%)
  Pallas kernels  35.5 us (26%)
  blocking collectives  27.5 us (20%)
  starting transfers between devices  17.2 us (12%)
    ppermute x12, waiting for transfers between devices, moved(): return lax.ppermute(array, 'band', pairs)  57.8 us
    pallas_call x15, Pallas kernels, call(): pl.pallas_call(kernel, name=name, out_shape=outs, in_specs=in_specs, out_...  35.5 us
    all_to_all x2, blocking collectives, exchanged(): return lax.all_to_all(flat, 'slab', 0, 0, tiled=True).reshape(array.shape)  27.5 us
    ppermute x12, starting transfers between devices, moved(): return lax.ppermute(array, 'band', pairs)  17.2 us
  transfers between devices with their start and end apart: 12, of which 7 were waited for; matrix products, arithmetic and copies ran while one was open for 0% of the time, Pallas kernels for 21%

profile of v6, /device:TPU:32, one launch (start us, length us, event | category | flops | bytes accessed | tf_op | source)
XLA Modules:
  0.0 138.5 jit_solution(8896676760355032661)
XLA Ops:
  0.0 1.6 %pack_0.1.refs_1_.own = f32[10,160,128]{2,1,0:T(8,128)S(1)} custom-call(f32[1,20,160,160]{3,2,1,0:T(8,128)} %orbitals.5), custom_call_target="tpu_custom_call" | custom-call | flops 1 | bytes 1 | tf_op jit(solution)/shard_map/pack_0/pallas_call | solution.py:115
  1.6 7.9 %collective-permute-start.2 = (f32[10,160,128]{2,1,0:T(8,128)S(1)}, f32[10,160,128]{2,1,0:T(8,128)}, u32[]{:S(2)}, u32[]{:S(2)}) collective-permute-start(f32[10,160,128]{2,1,0:T(8,128)S(1)} %pack_0.1.refs_1_.own), channel_id=1, source_target_pairs={{0,240},{8,24},{16,0},{24,40},{32,16},{40,56},{48,32},{56,72},{64,... | collective-permute-start | bytes 2457608 | tf_op jit(solution)/shard_map/visit_0/ppermute | solution.py:482
  9.5 2.4 %pack_1.1.refs_1_.own = f32[10,160,128]{2,1,0:T(8,128)} custom-call(f32[1,20,160,160]{3,2,1,0:T(8,128)} %orbitals.5), custom_call_target="tpu_custom_call" | custom-call | flops 1 | bytes 1 | tf_op jit(solution)/shard_map/pack_1/pallas_call | solution.py:115
  12.0 1.5 %collective-permute-start.5 = (f32[10,160,128]{2,1,0:T(8,128)}, f32[10,160,128]{2,1,0:T(8,128)}, u32[]{:S(2)}, u32[]{:S(2)}) collective-permute-start(f32[10,160,128]{2,1,0:T(8,128)} %pack_1.1.refs_1_.own), channel_id=1, source_target_pairs={{0,240},{8,24},{16,0},{24,40},{32,16},{40,56},{48,32},{56,72},{64,... | collective-permute-start | bytes 2457608 | tf_op jit(solution)/shard_map/visit_1/ppermute | solution.py:482
  13.5 1.3 pack_2.1.refs_1_.own
  14.8 0.6 collective-permute-start
  15.4 1.5 %collective-permute-done.array = f32[5,160,128]{2,1,0:T(8,128)} collective-permute-done((f32[5,160,128]{2,1,0:T(8,128)S(1)}, f32[5,160,128]{2,1,0:T(8,128)}, u32[]{:S(2)}, u32[]{:S(2)}) %collective-permute-start) | collective-permute-done | bytes 409632 | tf_op jit(solution)/shard_map/swap_2/ppermute | solution.py:482
  16.9 4.9 %collective-permute-start.3 = (f32[5,160,128]{2,1,0:T(8,128)S(1)}, f32[5,160,128]{2,1,0:T(8,128)S(1)}, u32[]{:S(2)}, u32[]{:S(2)}) collective-permute-start(f32[5,160,128]{2,1,0:T(8,128)S(1)} %pack_2.1.refs_1_.own), channel_id=1, source_target_pairs={{0,240},{8,24},{16,0},{24,40},{32,16},{40,56},{48,32},{56,72},{64,... | collective-permute-start | bytes 1228808 | tf_op jit(solution)/shard_map/visit_2/ppermute | solution.py:482
  21.8 0.9 pick.1.tables
  22.7 1.0 fetch.1.refs_2_.swap
  23.8 5.8 %forward_0.1 = (f32[2,8,160,256]{3,2,1,0:T(8,128)S(1)}, f32[2,160,256]{2,1,0:T(8,128)S(1)}, f32[2,160,256]{2,1,0:T(8,128)S(1)}, f32[8,128]{1,0:T(8,128)S(1)}) custom-call(s32[1]{0:T(128)} %bitcast.refs_0_.core, f32[10,160,128]{2,1,0:T(8,128)S(1)} %pack_0.1.refs_1_.own, f32[10,160,128]{2,1,0:T(8,128)} %collective-permute-done.1.refs_2_.swap, ...), custom_call_target="tpu_custom_call" | custom-call | flops 1 | bytes 1 | tf_op jit(solution)/shard_map/forward_0/pallas_call | solution.py:115
  29.5 3.0 %collective-permute-done.5.refs_3_.vis = f32[10,160,128]{2,1,0:T(8,128)} collective-permute-done((f32[10,160,128]{2,1,0:T(8,128)}, f32[10,160,128]{2,1,0:T(8,128)}, u32[]{:S(2)}, u32[]{:S(2)}) %collective-permute-start.5) | collective-permute-done | bytes 819232 | tf_op jit(solution)/shard_map/visit_1/ppermute | solution.py:482
  32.6 6.0 %forward_1.1 = (f32[2,8,160,256]{3,2,1,0:T(8,128)S(1)}, f32[2,160,256]{2,1,0:T(8,128)S(1)}, f32[2,160,256]{2,1,0:T(8,128)S(1)}, f32[8,128]{1,0:T(8,128)S(1)}) custom-call(s32[1]{0:T(128)} %bitcast.refs_0_.core, f32[10,160,128]{2,1,0:T(8,128)} %pack_1.1.refs_1_.own, f32[10,160,128]{2,1,0:T(8,128)} %collective-permute-done.4.refs_2_.swap, ...), custom_call_target="tpu_custom_call" | custom-call | flops 1 | bytes 1 | tf_op jit(solution)/shard_map/forward_1/pallas_call | solution.py:115
  38.6 14.7 %collective-permute-done.3.refs_3_.vis = f32[5,160,128]{2,1,0:T(8,128)S(1)} collective-permute-done((f32[5,160,128]{2,1,0:T(8,128)S(1)}, f32[5,160,128]{2,1,0:T(8,128)S(1)}, u32[]{:S(2)}, u32[]{:S(2)}) %collective-permute-start.3) | collective-permute-done | bytes 409632 | tf_op jit(solution)/shard_map/visit_2/ppermute | solution.py:482
  53.3 2.3 %forward_2.1 = (f32[2,4,160,256]{3,2,1,0:T(8,128)S(1)}, f32[8,14,8,128]{3,2,1,0:T(8,128)S(1)}) custom-call(s32[1]{0:T(128)} %bitcast.refs_0_.core, f32[5,160,128]{2,1,0:T(8,128)S(1)} %pack_2.1.refs_1_.own, f32[5,160,128]{2,1,0:T(8,128)S(1)} %fetch.1.refs_2_.swap, f32[5,160,128]{2,1,0:T(8,128)S(1)} %collective-permute-done.3.refs_3_.vis, ...), custom_call_target="tpu_custom_call" | custom-call | flops 1 | bytes 1 | tf_op jit(solution)/shard_map/forward_2/pallas_call | solution.py:115
  55.6 14.7 %all_to_all.18 = f32[8,112,128]{2,1,0:T(8,128)S(1)} all-to-all(f32[8,112,128]{2,1,0:T(8,128)S(1)} %bitcast.8), channel_id=1, replica_groups=mesh['band'=32,'slab'=8] {'slab'}, dimensions={0} | all-to-all | bytes 917504 | tf_op jit(solution)/shard_map/all_to_all | solution.py:477
  70.4 0.2 solve.1
  70.6 12.8 %all_to_all.19 = f32[8,104,128]{2,1,0:T(8,128)S(1)} all-to-all(f32[8,104,128]{2,1,0:T(8,128)S(1)} %bitcast.9), channel_id=1, replica_groups=mesh['band'=32,'slab'=8] {'slab'}, dimensions={0} | all-to-all | bytes 851968 | tf_op jit(solution)/shard_map/all_to_all | solution.py:477
  83.4 1.5 %products_2.1 = (f32[5,160,128]{2,1,0:T(8,128)S(1)}, f32[5,160,128]{2,1,0:T(8,128)S(1)}, f32[5,160,128]{2,1,0:T(8,128)S(1)}, f32[2,160,256]{2,1,0:T(8,128)S(1)}, f32[2,160,256]{2,1,0:T(8,128)S(1)}) custom-call(s32[1]{0:T(128)} %bitcast.refs_0_.core, f32[5,160,128]{2,1,0:T(8,128)S(1)} %pack_2.1.refs_1_.own, f32[5,160,128]{2,1,0:T(8,128)S(1)} %fetch.1.refs_2_.swap, ...), custom_call_target="tpu_custom_call" | custom-call | flops 1 | bytes 1 | tf_op jit(solution)/shard_map/products_2/pallas_call | solution.py:115
  84.9 0.3 collective-permute-start.6
  85.2 4.6 %products_1.1 = (f32[10,160,128]{2,1,0:T(8,128)S(1)}, f32[10,160,128]{2,1,0:T(8,128)S(1)}, f32[10,160,128]{2,1,0:T(8,128)S(1)}, f32[2,160,256]{2,1,0:T(8,128)S(1)}, f32[2,160,256]{2,1,0:T(8,128)S(1)}) custom-call(s32[1]{0:T(128)} %bitcast.refs_0_.core, f32[10,160,128]{2,1,0:T(8,128)} %pack_1.1.refs_1_.own, ...), custom_call_target="tpu_custom_call" | custom-call | flops 1 | bytes 1 | tf_op jit(solution)/shard_map/products_1/pallas_call | solution.py:115
  89.9 0.1 collective-permute-start.9
  90.0 1.3 collective-permute-start.10
  91.3 10.3 %collective-permute-done.6.returned = f32[5,160,128]{2,1,0:T(8,128)S(1)} collective-permute-done((f32[5,160,128]{2,1,0:T(8,128)S(1)}, f32[5,160,128]{2,1,0:T(8,128)S(1)}, u32[]{:S(2)}, u32[]{:S(2)}) %collective-permute-start.6) | collective-permute-done | bytes 409632 | tf_op jit(solution)/shard_map/return_2/ppermute | solution.py:482
  101.6 4.5 %products_0.1 = (f32[10,160,128]{2,1,0:T(8,128)S(1)}, f32[10,160,128]{2,1,0:T(8,128)S(1)}, f32[10,160,128]{2,1,0:T(8,128)S(1)}, f32[2,160,256]{2,1,0:T(8,128)}, f32[2,160,256]{2,1,0:T(8,128)}) custom-call(s32[1]{0:T(128)} %bitcast.refs_0_.core, f32[10,160,128]{2,1,0:T(8,128)S(1)} %pack_0.1.refs_1_.own, f32[10,160,128]{2,1,0:T(8,128)} %collective-permute-done.1.refs_2_.swap, ...), custom_call_target="tpu_custom_call" | custom-call | flops 1 | bytes 1 | tf_op jit(solution)/shard_map/products_0/pallas_call | solution.py:115
  106.1 0.5 collective-permute-start.11
  106.6 2.4 %collective-permute-done.11.crossed = f32[5,160,128]{2,1,0:T(8,128)S(1)} collective-permute-done((f32[5,160,128]{2,1,0:T(8,128)S(1)}, f32[5,160,128]{2,1,0:T(8,128)S(1)}, u32[]{:S(2)}, u32[]{:S(2)}) %collective-permute-start.11) | collective-permute-done | bytes 409632 | tf_op jit(solution)/shard_map/cross_2/ppermute | solution.py:482
  109.0 1.0 finish_2.1.refs_0_
  110.0 5.3 %collective-permute-done.10.returned = f32[10,160,128]{2,1,0:T(8,128)S(1)} collective-permute-done((f32[10,160,128]{2,1,0:T(8,128)S(1)}, f32[10,160,128]{2,1,0:T(8,128)S(1)}, u32[]{:S(2)}, u32[]{:S(2)}) %collective-permute-start.10) | collective-permute-done | bytes 819232 | tf_op jit(solution)/shard_map/return_1/ppermute | solution.py:482
  115.3 1.2 finish_1.1.refs_0_
  116.5 20.6 %collective-permute-done.8.returned = f32[10,160,128]{2,1,0:T(8,128)S(1)} collective-permute-done((f32[10,160,128]{2,1,0:T(8,128)S(1)}, f32[10,160,128]{2,1,0:T(8,128)S(1)}, u32[]{:S(2)}, u32[]{:S(2)}) %collective-permute-start.8) | collective-permute-done | bytes 819232 | tf_op jit(solution)/shard_map/return_0/ppermute | solution.py:482
  137.1 1.2 finish_0.1
  (29 shorter events, 0.1 us)
Async XLA Ops:
  1.6 22.1 %collective-permute-start.2 = (f32[10,160,128]{2,1,0:T(8,128)S(1)}, f32[10,160,128]{2,1,0:T(8,128)}, u32[]{:S(2)}, u32[]{:S(2)}) collective-permute-start(f32[10,160,128]{2,1,0:T(8,128)S(1)} %pack_0.1.refs_1_.own), channel_id=1, source_target_pairs={{0,240},{8,24},{16,0},{24,40},{32,16},{40,56},{48,32},{56,72},{64,... | collective-permute-start | bytes 2457608 | tf_op jit(solution)/shard_map/visit_0/ppermute | solution.py:482
  9.5 14.2 %collective-permute-start.1 = (f32[10,160,128]{2,1,0:T(8,128)S(1)}, f32[10,160,128]{2,1,0:T(8,128)}, u32[]{:S(2)}, u32[]{:S(2)}) collective-permute-start(f32[10,160,128]{2,1,0:T(8,128)S(1)} %pack_0.1.refs_1_.own), channel_id=1, source_target_pairs={{0,8},{8,0},{16,24},{24,16},{32,40},{40,32},{48,56},{56,48},{64,72... | collective-permute-start | bytes 2457608 | tf_op jit(solution)/shard_map/swap_0/ppermute | solution.py:482
  11.9 11.8 %copy-start = (f32[5,160,256]{2,1,0:T(8,128)S(1)}, f32[5,160,256]{2,1,0:T(8,128)}, u32[]{:S(2)}) copy-start(f32[5,160,256]{2,1,0:T(8,128)} %constant.39.clone.refs_7_) | copy-start | bytes 2457604
  11.9 11.8 %copy-start.1 = (f32[160,256]{1,0:T(8,128)S(1)}, f32[160,256]{1,0:T(8,128)}, u32[]{:S(2)}) copy-start(f32[160,256]{1,0:T(8,128)} %constant.37.clone.refs_6_.ratio) | copy-start | bytes 491524
  11.9 11.8 %copy-start.2 = (bf16[160,480]{1,0:T(8,128)(2,1)S(1)}, bf16[160,480]{1,0:T(8,128)(2,1)}, u32[]{:S(2)}) copy-start(bf16[160,480]{1,0:T(8,128)(2,1)} %constant.36.clone.refs_5_.hartley) | copy-start | bytes 460804
  11.9 11.8 %copy-start.4 = (bf16[768,256]{1,0:T(8,128)(2,1)S(1)}, bf16[768,256]{1,0:T(8,128)(2,1)}, u32[]{:S(2)}) copy-start(bf16[768,256]{1,0:T(8,128)(2,1)} %constant.34.clone.refs_4_) | copy-start | bytes 1179652
  12.0 20.6 %collective-permute-start.5 = (f32[10,160,128]{2,1,0:T(8,128)}, f32[10,160,128]{2,1,0:T(8,128)}, u32[]{:S(2)}, u32[]{:S(2)}) collective-permute-start(f32[10,160,128]{2,1,0:T(8,128)} %pack_1.1.refs_1_.own), channel_id=1, source_target_pairs={{0,240},{8,24},{16,0},{24,40},{32,16},{40,56},{48,32},{56,72},{64,... | collective-permute-start | bytes 2457608 | tf_op jit(solution)/shard_map/visit_1/ppermute | solution.py:482
  13.5 19.1 %collective-permute-start.4 = (f32[10,160,128]{2,1,0:T(8,128)}, f32[10,160,128]{2,1,0:T(8,128)}, u32[]{:S(2)}, u32[]{:S(2)}) collective-permute-start(f32[10,160,128]{2,1,0:T(8,128)} %pack_1.1.refs_1_.own), channel_id=1, source_target_pairs={{0,8},{8,0},{16,24},{24,16},{32,40},{40,32},{48,56},{56,48},{64,72... | collective-permute-start | bytes 2457608 | tf_op jit(solution)/shard_map/swap_1/ppermute | solution.py:482
  14.8 2.1 %collective-permute-start = (f32[5,160,128]{2,1,0:T(8,128)S(1)}, f32[5,160,128]{2,1,0:T(8,128)}, u32[]{:S(2)}, u32[]{:S(2)}) collective-permute-start(f32[5,160,128]{2,1,0:T(8,128)S(1)} %pack_2.1.refs_1_.own), channel_id=1, source_target_pairs={{0,8},{8,0},{16,24},{24,16},{32,40},{40,32},{48,56},{56,48},{64,72... | collective-permute-start | bytes 1228808 | tf_op jit(solution)/shard_map/swap_2/ppermute | solution.py:482
  16.9 36.4 %collective-permute-start.3 = (f32[5,160,128]{2,1,0:T(8,128)S(1)}, f32[5,160,128]{2,1,0:T(8,128)S(1)}, u32[]{:S(2)}, u32[]{:S(2)}) collective-permute-start(f32[5,160,128]{2,1,0:T(8,128)S(1)} %pack_2.1.refs_1_.own), channel_id=1, source_target_pairs={{0,240},{8,24},{16,0},{24,40},{32,16},{40,56},{48,32},{56,72},{64,... | collective-permute-start | bytes 1228808 | tf_op jit(solution)/shard_map/visit_2/ppermute | solution.py:482
  38.6 31.7 %copy-start.9 = (f32[8,24,128]{2,1,0:T(8,128)S(1)}, f32[8,24,128]{2,1,0:T(8,128)}, u32[]{:S(2)}) copy-start(f32[8,24,128]{2,1,0:T(8,128)} %constant.43.clone.zero) | copy-start | bytes 294916
  53.3 30.0 %copy-start.3 = (bf16[768,256]{1,0:T(8,128)(2,1)S(1)}, bf16[768,256]{1,0:T(8,128)(2,1)}, u32[]{:S(2)}) copy-start(bf16[768,256]{1,0:T(8,128)(2,1)} %constant.35.clone.table) | copy-start | bytes 1179652
  53.3 30.0 %copy-start.5 = (f32[160,256]{1,0:T(8,128)S(1)}, f32[160,256]{1,0:T(8,128)}, u32[]{:S(2)}) copy-start(f32[160,256]{1,0:T(8,128)} %constant.38.clone.scale) | copy-start | bytes 491524
  53.3 30.0 %copy-start.8 = (f32[4,160,256]{2,1,0:T(8,128)S(1)}, f32[4,160,256]{2,1,0:T(8,128)}, u32[]{:S(2)}) copy-start(f32[4,160,256]{2,1,0:T(8,128)} %constant.46.edge) | copy-start | bytes 1966084
  83.3 1.9 %copy-start.7 = (f32[8,160,256]{2,1,0:T(8,128)S(1)}, f32[8,160,256]{2,1,0:T(8,128)}, u32[]{:S(2)}) copy-start(f32[8,160,256]{2,1,0:T(8,128)} %constant.47.edge) | copy-start | bytes 3932164
  84.9 16.7 %collective-permute-start.6 = (f32[5,160,128]{2,1,0:T(8,128)S(1)}, f32[5,160,128]{2,1,0:T(8,128)S(1)}, u32[]{:S(2)}, u32[]{:S(2)}) collective-permute-start(f32[5,160,128]{2,1,0:T(8,128)S(1)} %get-tuple-element.62), channel_id=1, source_target_pairs={{240,0},{24,8},{0,16},{40,24},{16,32},{56,40},{32,48},{72,56},{48,... | collective-permute-start | bytes 1228808 | tf_op jit(solution)/shard_map/return_2/ppermute | solution.py:482
  85.2 16.4 %copy-start.6 = (f32[8,160,256]{2,1,0:T(8,128)S(1)}, f32[8,160,256]{2,1,0:T(8,128)}, u32[]{:S(2)}) copy-start(f32[8,160,256]{2,1,0:T(8,128)} %constant.45.edge) | copy-start | bytes 3932164
  89.9 20.1 %collective-permute-start.9 = (f32[10,160,128]{2,1,0:T(8,128)S(1)}, f32[10,160,128]{2,1,0:T(8,128)S(1)}, u32[]{:S(2)}, u32[]{:S(2)}) collective-permute-start(f32[10,160,128]{2,1,0:T(8,128)S(1)} %get-tuple-element.76), channel_id=1, source_target_pairs={{0,8},{8,0},{16,24},{24,16},{32,40},{40,32},{48,56},{56,48},{64,72... | collective-permute-start | bytes 2457608 | tf_op jit(solution)/shard_map/cross_1/ppermute | solution.py:482
  90.0 25.3 %collective-permute-start.10 = (f32[10,160,128]{2,1,0:T(8,128)S(1)}, f32[10,160,128]{2,1,0:T(8,128)S(1)}, u32[]{:S(2)}, u32[]{:S(2)}) collective-permute-start(f32[10,160,128]{2,1,0:T(8,128)S(1)} %get-tuple-element.77), channel_id=1, source_target_pairs={{240,0},{24,8},{0,16},{40,24},{16,32},{56,40},{32,48},{72,56},{48,... | collective-permute-start | bytes 2457608 | tf_op jit(solution)/shard_map/return_1/ppermute | solution.py:482
  106.1 10.4 %collective-permute-start.7 = (f32[10,160,128]{2,1,0:T(8,128)S(1)}, f32[10,160,128]{2,1,0:T(8,128)S(1)}, u32[]{:S(2)}, u32[]{:S(2)}) collective-permute-start(f32[10,160,128]{2,1,0:T(8,128)S(1)} %get-tuple-element.71), channel_id=1, source_target_pairs={{0,8},{8,0},{16,24},{24,16},{32,40},{40,32},{48,56},{56,48},{64,72... | collective-permute-start | bytes 2457608 | tf_op jit(solution)/shard_map/cross_0/ppermute | solution.py:482
  106.1 31.0 %collective-permute-start.8 = (f32[10,160,128]{2,1,0:T(8,128)S(1)}, f32[10,160,128]{2,1,0:T(8,128)S(1)}, u32[]{:S(2)}, u32[]{:S(2)}) collective-permute-start(f32[10,160,128]{2,1,0:T(8,128)S(1)} %get-tuple-element.72), channel_id=1, source_target_pairs={{240,0},{24,8},{0,16},{40,24},{16,32},{56,40},{32,48},{72,56},{48,... | collective-permute-start | bytes 2457608 | tf_op jit(solution)/shard_map/return_0/ppermute | solution.py:482
  106.1 2.9 %collective-permute-start.11 = (f32[5,160,128]{2,1,0:T(8,128)S(1)}, f32[5,160,128]{2,1,0:T(8,128)S(1)}, u32[]{:S(2)}, u32[]{:S(2)}) collective-permute-start(f32[5,160,128]{2,1,0:T(8,128)S(1)} %get-tuple-element.79), channel_id=1, source_target_pairs={{0,8},{8,0},{16,24},{24,16},{32,40},{40,32},{48,56},{56,48},{64,72... | collective-permute-start | bytes 1228808 | tf_op jit(solution)/shard_map/cross_2/ppermute | solution.py:482
